TPU v7x, 32 devices: a whole 2x2x4 slice. The times are simulated.
32 devices in a mesh: rep: 8 (over z, x), shard: 4 (over y, core).
Axes of the slice: x: 2, y: 2, z: 4, core: 2. Of those that a mesh axis runs over, the one named last changes fastest.
Arguments:
- patches: bfloat16 [192, 196, 768], P(('rep', 'shard')), may hold values from -6 to 6
- labels: int32 [192], P(('rep', 'shard')), may hold values from 0 to 999
- counts: int32 [32], P(('rep', 'shard')), may hold values from 1 to 6, as said below
- patch_w: float32 [768, 384], P('shard'), may hold values from -0.21875 to 0.21875
- layer_in: float32 [3, 384, 3072], P(None, 'shard')
- layer_down: float32 [3, 1536, 384], P(None, 'shard'), may hold values from -0.15625 to 0.15625
- layer_vecs: float32 [3, 4608], replicated
- glob_vecs: float32 [4, 384], replicated
- pos_embed: float32 [197, 384], replicated, may hold values from -3 to 3
- head: float32 [385, 1000], replicated, may hold values from -0.625 to 0.625
- m_patch: float32 [768, 384], P('shard'), may hold values from -3.0517578e-05 to 3.0517578e-05
- v_patch: float32 [768, 384], P('shard'), may hold values from 2e-13 to 3.3e-12
- m_in: float32 [3, 384, 3072], P(None, 'shard'), may hold values from -3.0517578e-05 to 3.0517578e-05
- v_in: float32 [3, 384, 3072], P(None, 'shard'), may hold values from 2e-13 to 3.3e-12
- m_down: float32 [3, 1536, 384], P(None, 'shard'), may hold values from -3.0517578e-05 to 3.0517578e-05
- v_down: float32 [3, 1536, 384], P(None, 'shard'), may hold values from 2e-13 to 3.3e-12
- m_vecs: float32 [3, 4608], replicated, may hold values from -0.00015258789 to 0.00015258789
- v_vecs: float32 [3, 4608], replicated, may hold values from 5e-12 to 8e-11
- m_glob: float32 [4, 384], replicated, may hold values from -0.00015258789 to 0.00015258789
- v_glob: float32 [4, 384], replicated, may hold values from 5e-12 to 8e-11
- m_pos: float32 [197, 384], replicated, may hold values from -1.5258789e-05 to 1.5258789e-05
- v_pos: float32 [197, 384], replicated, may hold values from 4e-14 to 6.5e-13
- m_head: float32 [385, 1000], replicated, may hold values from -6.1035156e-05 to 6.1035156e-05
- v_head: float32 [385, 1000], replicated, may hold values from 8e-13 to 1.3e-11
Outputs:
- loss: float32 [], replicated
- grad_norm: float32 [], replicated
- new_patch_w: float32 [768, 384], P('shard')
- new_m_patch: float32 [768, 384], P('shard')
- new_v_patch: float32 [768, 384], P('shard')
- new_layer_in: float32 [3, 384, 3072], P(None, 'shard')
- new_m_in: float32 [3, 384, 3072], P(None, 'shard')
- new_v_in: float32 [3, 384, 3072], P(None, 'shard')
- new_layer_down: float32 [3, 1536, 384], P(None, 'shard')
- new_m_down: float32 [3, 1536, 384], P(None, 'shard')
- new_v_down: float32 [3, 1536, 384], P(None, 'shard')
- new_layer_vecs: float32 [3, 4608], replicated
- new_m_vecs: float32 [3, 4608], replicated
- new_v_vecs: float32 [3, 4608], replicated
- new_glob_vecs: float32 [4, 384], replicated
- new_m_glob: float32 [4, 384], replicated
- new_v_glob: float32 [4, 384], replicated
- new_pos_embed: float32 [197, 384], replicated
- new_m_pos: float32 [197, 384], replicated
- new_v_pos: float32 [197, 384], replicated
- new_head: float32 [385, 1000], replicated
- new_m_head: float32 [385, 1000], replicated
- new_v_head: float32 [385, 1000], replicated
Inputs may be any that keep to these rules, and one draw needn't show every extreme that they name: `counts`: the last device of the flattened rep, shard order always holds 6 live images; devices of the lower half of that order hold at most 2, those of the upper half at least 3.
All inputs are finite; a program needn't handle non-finite values.
Results may differ from a plain program's by a relative error of at most 0.019.
Values may be sent and summed in bfloat16 or wider, within the bound.
A program may use at most 160 MiB of HBM per device.

v0:
```python
import jax
import jax.numpy as jnp
from jax import lax
from jax.sharding import PartitionSpec as P

D = 384
HEADS = 6
HEAD_DIM = 64
FF = 1536
PATCH_DIM = 768
PATCHES = 196
NCLS = 1000
LAYERS = 3
MICRO = 2
SEQ = 197


NORM_EPS = 1e-06
SMOOTHING = 0.1
CLIP_NORM = 0.05
LEARNING_RATE = 0.05
VECTOR_RATE = 0.5
BETA_FIRST = 0.9
BETA_SECOND = 0.999
ADAM_EPS = 1e-08
WEIGHT_DECAY = 0.05
ADAM_STEP = 10
GELU_SCALE = 0.7978845608028654
GELU_CUBIC = 0.044715


def mixed(left, right):
    return jnp.dot(left, right, preferred_element_type=jnp.float32)


def lead_contract(left, right):
    return lax.dot_general(
        left, right, (((0,), (0,)), ((), ())), preferred_element_type=jnp.float32
    )


def tail_contract(left, right):
    return lax.dot_general(
        left, right, (((1,), (1,)), ((), ())), preferred_element_type=jnp.float32
    )


def norm_forward(values, gain, shift):
    centre = values - jnp.mean(values, axis=-1, keepdims=True)
    inverse = lax.rsqrt(jnp.mean(centre * centre, axis=-1, keepdims=True) + NORM_EPS)
    normed = centre * inverse
    return (normed * gain + shift, normed, inverse)


def norm_backward(upstream, normed, inverse, gain):
    scaled = upstream * gain
    inner = (
        scaled
        - jnp.mean(scaled, axis=-1, keepdims=True)
        - normed * jnp.mean(scaled * normed, axis=-1, keepdims=True)
    )
    return (inverse * inner, jnp.sum(upstream * normed, axis=0), jnp.sum(upstream, axis=0))


def split_vectors(vectors):
    return (
        vectors[0:D],
        vectors[D : 2 * D],
        vectors[2 * D : 3 * D],
        vectors[3 * D : 4 * D],
        vectors[4 * D : 5 * D],
        vectors[5 * D : 6 * D],
        vectors[6 * D : 7 * D],
        vectors[7 * D : 7 * D + FF],
        vectors[7 * D + FF :],
    )


def split_heads(joined, images):
    shaped = joined.reshape(images, -1, 3, HEADS, HEAD_DIM)
    return (shaped[:, :, 0], shaped[:, :, 1], shaped[:, :, 2])


def score_block(query, keys):
    return jnp.einsum(
        "bqhd,bkhd->bhqk", query, keys, preferred_element_type=jnp.float32
    ) * HEAD_DIM ** (-0.5)


def layer_forward(stream, w_in, w_down, vectors, images):
    (
        gain_one,
        shift_one,
        bias_query,
        bias_value,
        bias_out,
        gain_two,
        shift_two,
        bias_up,
        bias_down,
    ) = split_vectors(vectors)
    normed_one, stat_one, inverse_one = norm_forward(stream, gain_one, shift_one)
    normed_one = normed_one.astype(jnp.bfloat16)
    bias_qkv = jnp.concatenate([bias_query, jnp.zeros_like(bias_query), bias_value])
    joined = (mixed(normed_one, w_in[:, : 3 * D]) + bias_qkv).astype(jnp.bfloat16)
    query, keys, values = split_heads(joined, images)
    scores = score_block(query, keys)
    log_total = jax.nn.logsumexp(scores, axis=-1, keepdims=True)
    probs = jnp.exp(scores - log_total).astype(jnp.bfloat16)
    heads_out = jnp.einsum("bhqk,bkhd->bqhd", probs, values, preferred_element_type=jnp.float32)
    heads_out = heads_out.reshape(-1, D).astype(jnp.bfloat16)
    middle = stream + mixed(heads_out, w_in[:, 3 * D : 4 * D]) + bias_out
    normed_two, stat_two, inverse_two = norm_forward(middle, gain_two, shift_two)
    normed_two = normed_two.astype(jnp.bfloat16)
    hidden = mixed(normed_two, w_in[:, 4 * D :]) + bias_up
    active = jax.nn.gelu(hidden, approximate=True).astype(jnp.bfloat16)
    result = middle + mixed(active, w_down) + bias_down
    stored = (
        stat_one,
        inverse_one,
        normed_one,
        joined,
        log_total,
        heads_out,
        stat_two,
        inverse_two,
        normed_two,
        hidden,
        active,
    )
    return (result, stored)


def layer_backward(upstream, w_in, w_down, vectors, stored, images):
    (
        gain_one,
        shift_one,
        bias_query,
        bias_value,
        bias_out,
        gain_two,
        shift_two,
        bias_up,
        bias_down,
    ) = split_vectors(vectors)
    (
        stat_one,
        inverse_one,
        normed_one,
        joined,
        log_total,
        heads_out,
        stat_two,
        inverse_two,
        normed_two,
        hidden,
        active,
    ) = stored
    upstream_low = upstream.astype(jnp.bfloat16)
    grad_down = lead_contract(active, upstream_low)
    grad_bias_down = jnp.sum(upstream, axis=0)
    d_active = tail_contract(upstream_low, w_down)
    tangent = jnp.tanh(GELU_SCALE * (hidden + GELU_CUBIC * hidden * hidden * hidden))
    slope = 0.5 * (1.0 + tangent) + 0.5 * hidden * (1.0 - tangent * tangent) * GELU_SCALE * (
        1.0 + 3.0 * GELU_CUBIC * hidden * hidden
    )
    d_hidden = (d_active * slope).astype(jnp.bfloat16)
    grad_bias_up = jnp.sum(d_hidden.astype(jnp.float32), axis=0)
    grad_up = lead_contract(normed_two, d_hidden)
    d_normed_two = tail_contract(d_hidden, w_in[:, 4 * D :])
    d_middle, grad_gain_two, grad_shift_two = norm_backward(
        d_normed_two, stat_two, inverse_two, gain_two
    )
    d_middle = d_middle + upstream
    middle_low = d_middle.astype(jnp.bfloat16)
    grad_out = lead_contract(heads_out, middle_low)
    grad_bias_out = jnp.sum(d_middle, axis=0)
    d_heads = tail_contract(middle_low, w_in[:, 3 * D : 4 * D]).astype(jnp.bfloat16)
    d_heads = d_heads.reshape(images, -1, HEADS, HEAD_DIM)
    query, keys, values = split_heads(joined, images)
    probs = jnp.exp(score_block(query, keys) - log_total)
    probs_low = probs.astype(jnp.bfloat16)
    d_probs = jnp.einsum("bqhd,bkhd->bhqk", d_heads, values, preferred_element_type=jnp.float32)
    d_values = jnp.einsum("bhqk,bqhd->bkhd", probs_low, d_heads, preferred_element_type=jnp.float32)
    d_scores = (probs * (d_probs - jnp.sum(d_probs * probs, axis=-1, keepdims=True))).astype(
        jnp.bfloat16
    )
    d_query = jnp.einsum(
        "bhqk,bkhd->bqhd", d_scores, keys, preferred_element_type=jnp.float32
    ) * HEAD_DIM ** (-0.5)
    d_keys = jnp.einsum(
        "bhqk,bqhd->bkhd", d_scores, query, preferred_element_type=jnp.float32
    ) * HEAD_DIM ** (-0.5)
    d_joined = (
        jnp.stack([d_query, d_keys, d_values], axis=2).reshape(-1, 3 * D).astype(jnp.bfloat16)
    )
    grad_qkv = lead_contract(normed_one, d_joined)
    bias_sums = jnp.sum(d_joined.astype(jnp.float32), axis=0)
    d_normed_one = tail_contract(d_joined, w_in[:, : 3 * D])
    d_stream, grad_gain_one, grad_shift_one = norm_backward(
        d_normed_one, stat_one, inverse_one, gain_one
    )
    d_stream = d_stream + d_middle
    grad_in = jnp.concatenate([grad_qkv, grad_out, grad_up], axis=1)
    grad_vectors = jnp.concatenate(
        [
            grad_gain_one,
            grad_shift_one,
            bias_sums[:D],
            bias_sums[2 * D :],
            grad_bias_out,
            grad_gain_two,
            grad_shift_two,
            grad_bias_up,
            grad_bias_down,
        ]
    )
    return (d_stream, grad_in, grad_down, grad_vectors)


def micro_forward(
    pixels, classes, alive_mask, ahead, layer_vecs, glob_vecs, pos_embed, head, inv_count
):
    patch_full, in_full, down_full = ahead
    images = pixels.shape[0]
    pixel_rows = pixels.reshape(-1, PATCH_DIM)
    embedded = mixed(pixel_rows, patch_full[0]).reshape(images, PATCHES, D) + glob_vecs[0]
    leading = jnp.broadcast_to(glob_vecs[1], (images, 1, D))
    stream = (jnp.concatenate([leading, embedded], axis=1) + pos_embed).reshape(-1, D)
    stores = []
    for layer_index in range(LAYERS):
        stream, stored = layer_forward(
            stream, in_full[layer_index], down_full[layer_index], layer_vecs[layer_index], images
        )
        stores.append(stored)
    first = stream.reshape(images, -1, D)[:, 0]
    final, final_stat, final_inverse = norm_forward(first, glob_vecs[2], glob_vecs[3])
    final = final.astype(jnp.bfloat16)
    head_low = head[:D].astype(jnp.bfloat16)
    logits = mixed(final, head_low) + head[D]
    log_probs = jax.nn.log_softmax(logits, axis=-1)
    onehot = (classes[:, None] == jnp.arange(NCLS)[None, :]).astype(jnp.float32)
    target = (1.0 - SMOOTHING) * onehot + SMOOTHING / NCLS
    loss_part = jnp.sum(-jnp.sum(target * log_probs, axis=1) * alive_mask)
    d_logits = ((jnp.exp(log_probs) - target) * (alive_mask * inv_count)[:, None]).astype(
        jnp.bfloat16
    )
    grad_head = jnp.concatenate(
        [lead_contract(final, d_logits), jnp.sum(d_logits.astype(jnp.float32), axis=0)[None]],
        axis=0,
    )
    d_final = tail_contract(d_logits, head_low)
    d_first, grad_gain, grad_shift = norm_backward(d_final, final_stat, final_inverse, glob_vecs[2])
    upstream = jnp.zeros((images, SEQ, D), jnp.float32).at[:, 0].set(d_first).reshape(-1, D)
    return (loss_part, (pixel_rows, stores, upstream, grad_head, grad_gain, grad_shift))


def micro_backward(kept, behind, layer_vecs, images):
    pixel_rows, stores, upstream, grad_head, grad_gain, grad_shift = kept
    in_full, down_full = behind
    grads_in = [None] * LAYERS
    grads_down = [None] * LAYERS
    grads_vec = [None] * LAYERS
    for layer_index in reversed(range(LAYERS)):
        upstream, grads_in[layer_index], grads_down[layer_index], grads_vec[layer_index] = (
            layer_backward(
                upstream,
                in_full[layer_index],
                down_full[layer_index],
                layer_vecs[layer_index],
                stores[layer_index],
                images,
            )
        )
    upstream = upstream.reshape(images, SEQ, D)
    grad_pos = jnp.sum(upstream, axis=0)
    d_embedded = upstream[:, 1:].reshape(-1, D)
    grad_glob = jnp.stack(
        [jnp.sum(d_embedded, axis=0), jnp.sum(upstream[:, 0], axis=0), grad_gain, grad_shift]
    )
    grad_patch = lead_contract(pixel_rows, d_embedded.astype(jnp.bfloat16))
    matrices = (grad_patch[None], jnp.stack(grads_in), jnp.stack(grads_down))
    vectors = (jnp.stack(grads_vec), grad_glob, grad_pos, grad_head)
    return (matrices, vectors)


def add_trees(first, second):
    if first is None:
        return second
    return jax.tree.map(lambda left, right: left + right, first, second)


def adam_update(weight, first, second, grad, factor, rate):
    grad = grad * factor
    first = BETA_FIRST * first + (1.0 - BETA_FIRST) * grad
    second = BETA_SECOND * second + (1.0 - BETA_SECOND) * grad * grad
    first_hat = first / (1.0 - BETA_FIRST**ADAM_STEP)
    second_hat = second / (1.0 - BETA_SECOND**ADAM_STEP)
    weight = weight - rate * (first_hat / (jnp.sqrt(second_hat) + ADAM_EPS) + WEIGHT_DECAY * weight)
    return (weight, first, second)


def shards(
    patches,
    labels,
    counts,
    patch_w,
    layer_in,
    layer_down,
    layer_vecs,
    glob_vecs,
    pos_embed,
    head,
    m_patch,
    v_patch,
    m_in,
    v_in,
    m_down,
    v_down,
    m_vecs,
    v_vecs,
    m_glob,
    v_glob,
    m_pos,
    v_pos,
    m_head,
    v_head,
):
    slot_count = patches.shape[0]
    share = slot_count // MICRO
    image_sum = lax.psum(counts, ("rep", "shard"))
    inv_count = 1.0 / image_sum[0].astype(jnp.float32)
    alive_mask = (jnp.arange(slot_count) < counts[0]).astype(jnp.float32)
    own_patch = patch_w.astype(jnp.bfloat16)[None]
    own_in = layer_in.astype(jnp.bfloat16)
    own_down = layer_down.astype(jnp.bfloat16)
    loss_sum = jnp.zeros((), jnp.float32)
    matrix_acc = None
    vector_acc = None
    for block_index in range(MICRO):
        start = block_index * share
        ahead = (
            lax.all_gather(own_patch, "shard", axis=1, tiled=True),
            lax.all_gather(own_in, "shard", axis=1, tiled=True),
            lax.all_gather(own_down, "shard", axis=1, tiled=True),
        )
        loss_part, kept = micro_forward(
            patches[start : start + share],
            labels[start : start + share],
            alive_mask[start : start + share],
            ahead,
            layer_vecs,
            glob_vecs,
            pos_embed,
            head,
            inv_count,
        )
        behind = (
            lax.all_gather(own_in, "shard", axis=1, tiled=True),
            lax.all_gather(own_down, "shard", axis=1, tiled=True),
        )
        matrices, vectors = micro_backward(kept, behind, layer_vecs, share)
        loss_sum = loss_sum + loss_part
        vector_acc = add_trees(vector_acc, vectors)
        matrix_acc = add_trees(matrix_acc, matrices)
    full_patch, full_in, full_down = matrix_acc
    matrix_acc = (
        lax.psum_scatter(
            full_patch.astype(jnp.bfloat16), "shard", scatter_dimension=1, tiled=True
        ).astype(jnp.float32),
        lax.psum_scatter(
            full_in.astype(jnp.bfloat16), "shard", scatter_dimension=1, tiled=True
        ).astype(jnp.float32),
        lax.psum_scatter(
            full_down.astype(jnp.bfloat16), "shard", scatter_dimension=1, tiled=True
        ).astype(jnp.float32),
    )
    owned_patch, owned_in, owned_down = matrix_acc
    grad_patch, grad_in, grad_down = (
        lax.psum(owned_patch.astype(jnp.bfloat16), "rep").astype(jnp.float32),
        lax.psum(owned_in.astype(jnp.bfloat16), "rep").astype(jnp.float32),
        lax.psum(owned_down.astype(jnp.bfloat16), "rep").astype(jnp.float32),
    )
    grad_patch = grad_patch[0]
    sum_vecs, sum_glob, sum_pos, sum_head = vector_acc
    grad_vecs, grad_glob, grad_pos, grad_head, loss_total = lax.psum(
        (sum_vecs, sum_glob, sum_pos, sum_head, loss_sum), ("rep", "shard")
    )
    own_squares = (
        jnp.sum(grad_patch * grad_patch)
        + jnp.sum(grad_in * grad_in)
        + jnp.sum(grad_down * grad_down)
    )
    matrix_squares = lax.psum(own_squares, "shard")
    small_squares = (
        jnp.sum(grad_vecs * grad_vecs)
        + jnp.sum(grad_glob * grad_glob)
        + jnp.sum(grad_pos * grad_pos)
        + jnp.sum(grad_head * grad_head)
    )
    grad_norm = jnp.sqrt(matrix_squares + small_squares)
    factor = jnp.minimum(1.0, CLIP_NORM / grad_norm)
    loss = loss_total * inv_count
    new_patch = adam_update(patch_w, m_patch, v_patch, grad_patch, factor, LEARNING_RATE)
    new_in = adam_update(layer_in, m_in, v_in, grad_in, factor, LEARNING_RATE)
    new_down = adam_update(layer_down, m_down, v_down, grad_down, factor, LEARNING_RATE)
    new_vecs = adam_update(layer_vecs, m_vecs, v_vecs, grad_vecs, factor, VECTOR_RATE)
    new_glob = adam_update(glob_vecs, m_glob, v_glob, grad_glob, factor, VECTOR_RATE)
    new_pos = adam_update(pos_embed, m_pos, v_pos, grad_pos, factor, VECTOR_RATE)
    new_head = adam_update(head, m_head, v_head, grad_head, factor, LEARNING_RATE)
    return (
        loss,
        grad_norm,
        new_patch[0],
        new_patch[1],
        new_patch[2],
        new_in[0],
        new_in[1],
        new_in[2],
        new_down[0],
        new_down[1],
        new_down[2],
        new_vecs[0],
        new_vecs[1],
        new_vecs[2],
        new_glob[0],
        new_glob[1],
        new_glob[2],
        new_pos[0],
        new_pos[1],
        new_pos[2],
        new_head[0],
        new_head[1],
        new_head[2],
    )


def solution(mesh):
    return jax.shard_map(
        shards,
        mesh=mesh,
        in_specs=(
            P(("rep", "shard"), None, None),
            P(("rep", "shard")),
            P(("rep", "shard")),
            P("shard", None),
            P(None, "shard", None),
            P(None, "shard", None),
            P(),
            P(),
            P(),
            P(),
            P("shard", None),
            P("shard", None),
            P(None, "shard", None),
            P(None, "shard", None),
            P(None, "shard", None),
            P(None, "shard", None),
            P(),
            P(),
            P(),
            P(),
            P(),
            P(),
            P(),
            P(),
        ),
        out_specs=(
            P(),
            P(),
            P("shard", None),
            P("shard", None),
            P("shard", None),
            P(None, "shard", None),
            P(None, "shard", None),
            P(None, "shard", None),
            P(None, "shard", None),
            P(None, "shard", None),
            P(None, "shard", None),
            P(),
            P(),
            P(),
            P(),
            P(),
            P(),
            P(),
            P(),
            P(),
            P(),
            P(),
            P(),
        ),
        check_vma=False,
    )
```

profile of v0, /device:TPU:0, one launch (start us, length us, event | category | flops | bytes accessed | tf_op | source)
XLA Modules:
  0.0 1035.3 jit_solution(5038077234871512504)
XLA Ops:
  13.4 9.0 all-gather
  29.9 40.9 %psum.71 = s32[1]{0:T(128)} all-reduce(s32[1]{0:T(128)} %param.31), channel_id=1, replica_groups=mesh['rep'=8,'shard'=4] {'rep','shard'}, use_global_device_ids=true, to_apply=%region_47.0 | all-reduce | flops 1 | bytes 8 | tf_op jit(solution)/shard_map/psum | solution.py:331
  79.7 5.9 slice_bitcast_fusion
  89.1 5.3 reshape.959
  94.5 4.1 fusion.373
  109.4 5.3 reshape.962
  114.8 4.1 fusion.376
  140.3 4.1 fusion.391
  148.1 5.3 reshape.963
  153.4 4.1 fusion.375
  176.4 3.7 fusion.393
  183.8 5.3 reshape.964
  189.1 4.1 fusion.374
  232.3 3.7 fusion.385
  239.7 5.7 reshape.960
  245.4 4.1 fusion.372
  266.9 3.7 fusion.387
  274.2 5.4 reshape.961
  279.6 4.1 fusion.371
  326.3 5.4 convolution_bitcast_fusion
  358.1 4.0 convolution_bitcast_fusion.13
  372.7 4.0 convolution_bitcast_fusion.9
  385.8 5.5 convert_element_type.509
  391.3 3.9 fusion.328
  399.3 5.6 convert_element_type.533
  405.0 3.9 multiply_reduce_fusion.16
  440.6 3.8 convolution_bitcast_fusion.12
  453.6 3.8 convolution_bitcast_fusion.8
  465.8 5.5 convert_element_type.516
  476.4 5.6 convert_element_type.540
  482.1 3.7 multiply_reduce_fusion.18
  510.2 4.0 convolution_bitcast_fusion.11
  524.4 3.8 convolution_bitcast_fusion.7
  536.8 4.8 convert_element_type.523
  546.5 5.5 convert_element_type.547
  552.0 3.9 multiply_reduce_fusion.20
  560.4 4.4 multiply_reduce_fusion.26
  574.8 4.6 copy.560
  583.1 3.8 convolution_bitcast_fusion.5
  619.8 3.9 fusion
  639.5 8.3 reduce-scatter.8.cloned.1.call-done
  647.8 66.2 %reduce-scatter.6.cloned.1.call-done = bf16[3,96,3072]{2,1,0:T(8,128)(2,1)} async-done(((bf16[3,384,3072]{2,1,0:T(8,128)(2,1)}), bf16[3,96,3072]{2,1,0:T(8,128)(2,1)}) %reduce-scatter.6.cloned.1.call-update) | async-done | bytes 1769488 | tf_op jit(solution)/shard_map/reduce_scatter | solution.py:371
  717.7 40.4 %all-reduce.2 = (f32[]{:T(128)}, f32[3,4608]{1,0:T(4,128)S(1)}, f32[4,384]{1,0:T(4,128)S(1)}) all-reduce(f32[]{:T(128)S(6)} %add.1055, f32[3,4608]{1,0:T(4,128)S(1)} %maximum_add_fusion.3, f32[4,384]{1,0:T(4,128)S(1)} %maximum_add_fusion.4), channel_id=1, replica_groups=mesh['rep'=8,'shard'=4] {'rep','shard'}, use_global_device_ids=true, to_apply=%region_46.0 | all-reduce | flops 15361 | bytes 122888 | tf_op jit(solution)/shard_map/psum | solution.py:386
  761.3 91.9 %all-reduce.8.cloned.1.call-done = (f32[197,384]{1,0:T(8,128)}, f32[385,1000]{1,0:T(8,128)}) async-done(((f32[197,384]{1,0:T(8,128)}, f32[385,1000]{1,0:T(8,128)}), (f32[197,384]{1,0:T(8,128)}, f32[385,1000]{1,0:T(8,128)})) %all-reduce.8.cloned.1.call-update) | async-done | bytes 1842608 | tf_op jit(solution)/shard_map/psum | solution.py:386
  858.0 120.9 %all-reduce.10.cloned.1.call-done = (bf16[1,192,384]{1,2,0:T(8,128)(2,1)}, bf16[3,96,3072]{2,1,0:T(8,128)(2,1)}, bf16[3,384,384]{2,1,0:T(8,128)(2,1)}) async-done(((bf16[1,192,384]{1,2,0:T(8,128)(2,1)}, bf16[3,96,3072]{2,1,0:T(8,128)(2,1)}, bf16[3,384,384]{2,1,0:T(8,128)(2,1)}), (bf16[1,192,384]{1,2,0:T(8,128)(2,1)}, bf16[3,96,3072]{2,1,0:T(8,128)(2,1)}, ...) | async-done | bytes 2801680 | tf_op jit(solution)/shard_map/psum | solution.py:380
  988.5 7.6 psum.75
  1009.9 4.7 multiply_subtract_fusion.2
  1020.5 5.5 multiply_subtract_fusion
  (1174 shorter events, 438.3 us)
Async XLA Ops:
  7.2 72.5 %all-gather.4.cloned.1.call-start = ((), (), s32[]{:S(2)}) async-start(), calls=%async_computation.3 | async-start | bytes 8847360 | tf_op jit(solution)/shard_map/all_gather | solution.py:344
  10.9 129.4 %all-gather.6.cloned.1.call-start = ((), (), s32[]{:S(2)}) async-start(), calls=%async_computation.4 | async-start | bytes 4423680 | tf_op jit(solution)/shard_map/all_gather | solution.py:345
  11.9 12.4 %copy-start.59 = (bf16[6,196,768]{2,1,0:T(8,128)(2,1)S(1)}, bf16[6,196,768]{2,1,0:T(8,128)(2,1)}, u32[]{:S(2)}) copy-start(bf16[6,196,768]{2,1,0:T(8,128)(2,1)} %param.29) | copy-start | bytes 5419012
  11.9 13.7 %copy-start.334 = (s32[6]{0:T(128)S(1)}, s32[6]{0:T(128)}, u32[]{:S(2)}) copy-start(s32[6]{0:T(128)} %param.30) | copy-start | bytes 76
  12.0 625.6 %reduce-scatter.10.cloned.1.call-start = ((), (), s32[]{:S(2)}) async-start(), calls=%async_computation.7 | async-start | bytes 737280
  12.0 14.3 %copy-start.148 = (f32[197,384]{1,0:T(8,128)S(1)}, f32[197,384]{1,0:T(8,128)}, u32[]{:S(2)}) copy-start(f32[197,384]{1,0:T(8,128)} %param.37) | copy-start | bytes 907780
  12.6 14.8 %copy-start.285 = (f32[384]{0:T(512)}, f32[384]{0:T(512)S(1)}, u32[]{:S(2)}) copy-start(f32[384]{0:T(512)S(1)} %get-tuple-element.236) | copy-start | bytes 4612
  12.6 93.5 %copy-start.195 = (f32[384]{0:T(512)}, f32[384]{0:T(512)S(1)}, u32[]{:S(2)}) copy-start(f32[384]{0:T(512)S(1)} %get-tuple-element.237) | copy-start | bytes 4612
  13.4 298.3 %copy-start.177 = (f32[384]{0:T(512)}, f32[384]{0:T(512)S(1)}, u32[]{:S(2)}) copy-start(f32[384]{0:T(512)S(1)} %get-tuple-element.249) | copy-start | bytes 4612
  13.4 303.2 %copy-start.167 = (f32[384]{0:T(512)}, f32[384]{0:T(512)S(1)}, u32[]{:S(2)}) copy-start(f32[384]{0:T(512)S(1)} %get-tuple-element.247) | copy-start | bytes 4612
  27.1 47.3 %copy-start.12 = (f32[385,1000]{1,0:T(8,128)S(1)}, f32[385,1000]{1,0:T(8,128)}, u32[]{:S(2)}) copy-start(f32[385,1000]{1,0:T(8,128)} %param.38) | copy-start | bytes 4620004
  70.8 14.8 %copy-start.179 = (f32[591]{0:T(1024)}, f32[591]{0:T(1024)S(1)}, u32[]{:S(2)}) copy-start(f32[591]{0:T(1024)S(1)} %div.287) | copy-start | bytes 7096
  71.6 34.6 %copy-start.212 = (f32[591]{0:T(1024)}, f32[591]{0:T(1024)S(1)}, u32[]{:S(2)}) copy-start(f32[591]{0:T(1024)S(1)} %rsqrt.129) | copy-start | bytes 7096
  71.7 14.0 %copy-start.181 = (f32[591]{0:T(1024)}, f32[591]{0:T(1024)S(1)}, u32[]{:S(2)}) copy-start(f32[591]{0:T(1024)S(1)} %rsqrt.121) | copy-start | bytes 7096
  144.4 28.5 %copy-start.30 = (f32[591,384]{1,0:T(8,128)}, f32[591,384]{1,0:T(8,128)S(1)}, u32[]{:S(2)}) copy-start(f32[591,384]{1,0:T(8,128)S(1)} %get-tuple-element.418) | copy-start | bytes 2723332
  180.2 28.3 %copy-start.33 = (f32[591,384]{1,0:T(8,128)}, f32[591,384]{1,0:T(8,128)S(1)}, u32[]{:S(2)}) copy-start(f32[591,384]{1,0:T(8,128)S(1)} %get-tuple-element.424) | copy-start | bytes 2723332
  220.4 95.3 %copy-start.162 = (f32[3,1,384]{2,1,0:T(1,128)}, f32[3,1,384]{2,1,0:T(1,128)S(1)}, u32[]{:S(2)}) copy-start(f32[3,1,384]{2,1,0:T(1,128)S(1)} %get-tuple-element.345) | copy-start | bytes 13828
  300.8 45.9 %copy-start.189 = (f32[591]{0:T(1024)}, f32[591]{0:T(1024)S(1)}, u32[]{:S(2)}) copy-start(f32[591]{0:T(1024)S(1)} %broadcast_multiply_fusion.29) | copy-start | bytes 7096
  504.3 15.0 %copy-start.51 = (f32[591,384]{1,0:T(8,128)}, f32[591,384]{1,0:T(8,128)S(1)}, u32[]{:S(2)}) copy-start(f32[591,384]{1,0:T(8,128)S(1)} %get-tuple-element.288) | copy-start | bytes 2723332
  581.8 66.1 %reduce-scatter.8.cloned.1.call-start = ((), (), s32[]{:S(2)}) async-start(), calls=%async_computation.6 | async-start | bytes 4423680 | tf_op jit(solution)/shard_map/reduce_scatter | solution.py:374
  590.9 123.1 %reduce-scatter.6.cloned.1.call-start = ((), (), s32[]{:S(2)}) async-start(), calls=%async_computation.5 | async-start | bytes 8847360 | tf_op jit(solution)/shard_map/reduce_scatter | solution.py:371
  624.0 10.1 copy-start.166
  624.0 10.1 copy-start.168
  624.0 10.0 copy-start.174
  624.1 10.5 %copy-start.163 = (f32[3,1,384]{2,1,0:T(1,128)S(1)}, f32[3,1,384]{2,1,0:T(1,128)}, u32[]{:S(2)}) copy-start(f32[3,1,384]{2,1,0:T(1,128)} %copy-done.162) | copy-start | bytes 13828
  624.1 10.5 %copy-start.172 = (bf16[3,1000]{1,0:T(4,128)(2,1)S(1)}, bf16[3,1000]{1,0:T(4,128)(2,1)}, u32[]{:S(2)}) copy-start(bf16[3,1000]{1,0:T(4,128)(2,1)} %copy-done.171) | copy-start | bytes 18004
  624.1 10.5 %copy-start.234 = (f32[3]{0:T(128)S(1)}, f32[3]{0:T(128)}, u32[]{:S(2)}) copy-start(f32[3]{0:T(128)} %copy-done.232) | copy-start | bytes 40
  624.1 10.5 %copy-start.239 = (f32[3]{0:T(128)S(1)}, f32[3]{0:T(128)}, u32[]{:S(2)}) copy-start(f32[3]{0:T(128)} %copy-done.237) | copy-start | bytes 40
  624.1 229.2 %all-reduce.8.cloned.1.call-start = ((), (), s32[]{:S(2)}) async-start(), calls=%async_computation.8 | async-start | bytes 3825664 | tf_op jit(solution)/shard_map/psum | solution.py:386
  636.7 77.4 %copy-start.288 = (f32[384]{0:T(512)S(1)}, f32[384]{0:T(512)}, u32[]{:S(2)}) copy-start(f32[384]{0:T(512)} %get-tuple-element.177) | copy-start | bytes 4612
  636.7 77.4 %copy-start.287 = (f32[384]{0:T(512)S(1)}, f32[384]{0:T(512)}, u32[]{:S(2)}) copy-start(f32[384]{0:T(512)} %get-tuple-element.206) | copy-start | bytes 4612
  636.7 77.4 %copy-start.259 = (f32[384]{0:T(512)S(1)}, f32[384]{0:T(512)}, u32[]{:S(2)}) copy-start(f32[384]{0:T(512)} %get-tuple-element.303) | copy-start | bytes 4612
  636.7 77.5 %copy-start.327 = (f32[384]{0:T(512)S(1)}, f32[384]{0:T(512)}, u32[]{:S(2)}) copy-start(f32[384]{0:T(512)} %get-tuple-element.370) | copy-start | bytes 4612
  636.7 77.5 %copy-start.326 = (f32[384]{0:T(512)S(1)}, f32[384]{0:T(512)}, u32[]{:S(2)}) copy-start(f32[384]{0:T(512)} %get-tuple-element.367) | copy-start | bytes 4612
  636.7 77.5 %copy-start.276 = (f32[1536]{0:T(1024)S(1)}, f32[1536]{0:T(1024)}, u32[]{:S(2)}) copy-start(f32[1536]{0:T(1024)} %get-tuple-element.460) | copy-start | bytes 18436
  636.7 77.5 %copy-start.256 = (f32[384]{0:T(512)S(1)}, f32[384]{0:T(512)}, u32[]{:S(2)}) copy-start(f32[384]{0:T(512)} %get-tuple-element.301) | copy-start | bytes 4612
  636.7 77.9 %copy-start.273 = (f32[6]{0:T(128)S(1)}, f32[6]{0:T(128)}, u32[]{:S(2)}) copy-start(f32[6]{0:T(128)} %compare_convert_fusion) | copy-start | bytes 76
  636.8 77.9 %copy-start.299 = (f32[3]{0:T(128)S(1)}, f32[3]{0:T(128)}, u32[]{:S(2)}) copy-start(f32[3]{0:T(128)} %get-tuple-element.348) | copy-start | bytes 40
  636.8 77.9 %copy-start.300 = (f32[3]{0:T(128)S(1)}, f32[3]{0:T(128)}, u32[]{:S(2)}) copy-start(f32[3]{0:T(128)} %get-tuple-element.468) | copy-start | bytes 40
  636.8 80.0 %copy-start.161 = (f32[192,384]{1,0:T(8,128)S(1)}, f32[192,384]{1,0:T(8,128)}, u32[]{:S(2)}) copy-start(f32[192,384]{1,0:T(8,128)} %param.40) | copy-start | bytes 884740
  636.8 342.2 %all-reduce.10.cloned.1.call-start = ((), (), s32[]{:S(2)}) async-start(), calls=%async_computation.9 | async-start | bytes 5701632 | tf_op jit(solution)/shard_map/psum | solution.py:380
  758.1 238.7 %copy-start.159 = (f32[3,4608]{1,0:T(4,128)}, f32[3,4608]{1,0:T(4,128)S(1)}, u32[]{:S(2)}) copy-start(f32[3,4608]{1,0:T(4,128)S(1)} %get-tuple-element.253) | copy-start | bytes 165892
  979.0 26.2 %copy-start.198 = (f32[4,384]{1,0:T(4,128)S(1)}, f32[4,384]{1,0:T(4,128)}, u32[]{:S(2)}) copy-start(f32[4,384]{1,0:T(4,128)} %param.36) | copy-start | bytes 18436
  979.0 26.2 %copy-start.289 = (f32[4,384]{1,0:T(4,128)S(1)}, f32[4,384]{1,0:T(4,128)}, u32[]{:S(2)}) copy-start(f32[4,384]{1,0:T(4,128)} %param.47) | copy-start | bytes 18436
  979.0 26.2 %copy-start.290 = (f32[4,384]{1,0:T(4,128)S(1)}, f32[4,384]{1,0:T(4,128)}, u32[]{:S(2)}) copy-start(f32[4,384]{1,0:T(4,128)} %param.48) | copy-start | bytes 18436
  981.2 26.3 %copy-start.147 = (f32[197,384]{1,0:T(8,128)S(1)}, f32[197,384]{1,0:T(8,128)}, u32[]{:S(2)}) copy-start(f32[197,384]{1,0:T(8,128)} %get-tuple-element.255) | copy-start | bytes 907780
  996.9 12.9 %copy-start.13 = (f32[385,1000]{1,0:T(8,128)S(1)}, f32[385,1000]{1,0:T(8,128)}, u32[]{:S(2)}) copy-start(f32[385,1000]{1,0:T(8,128)} %param.38) | copy-start | bytes 4620004
  996.9 12.9 %copy-start.58 = (f32[385,1000]{1,0:T(8,128)S(1)}, f32[385,1000]{1,0:T(8,128)}, u32[]{:S(2)}) copy-start(f32[385,1000]{1,0:T(8,128)} %get-tuple-element.256) | copy-start | bytes 4620004
  (320 other events, 1322.2 us)
Sparse Core Ops, SparseCore 0:
  11.0 54.3 all-gather.3
  67.5 30.7 all-gather.5
  581.9 22.4 reduce-scatter.9
  607.4 40.4 reduce-scatter.7
  650.4 63.6 reduce-scatter.5
  719.9 133.3 all-reduce.7
  857.8 121.1 all-reduce.9
where the time goes:
time: 1040 us
  waiting for transfers between devices  288 us (28%)
  local copies, waits for them, and re-layouts  281 us (27%)
  matrix products  248 us (24%)
  blocking collectives  97.9 us (9%)
  other arithmetic  90.3 us (9%)
  between operations  30 us (3%)
    psum x1, waiting for transfers between devices, shards(): lax.psum(owned_patch.astype(jnp.bfloat16), 'rep').astype(jnp.float32)  121 us
    psum x1, waiting for transfers between devices, shards(): lax.psum((sum_vecs, sum_glob, sum_pos, sum_head, loss_sum), ('rep', 'shar...  91.9 us
    unnamed x799, local copies, waits for them, and re-layouts  91 us
    reduce_scatter x1, waiting for transfers between devices, shards(): lax.psum_scatter(full_in.astype(jnp.bfloat16), 'shard', scatter_dimension...  66.2 us
    dot_general x28, matrix products, mixed(): return jnp.dot(left, right, preferred_element_type=jnp.float32)  64.7 us
    dot_general x26, matrix products, tail_contract(): lax.dot_general(left, right, (((1,), (1,)), ((), ())), preferred_element_...  63.1 us
    dot_general x28, matrix products, lead_contract(): lax.dot_general(left, right, (((0,), (0,)), ((), ())), preferred_element_...  57.6 us
    convert_element_type x12, local copies, waits for them, and re-layouts, layer_backward(): jnp.stack([d_query, d_keys, d_values], axis=2).reshape(-1, 3 * D)  50.3 us
  transfers between devices with their start and end apart: 7, of which 4 were waited for; matrix products, arithmetic and copies ran while one was open for 12% of the time, Pallas kernels for 0%

commit v1 on v0

v1 whole, which is shorter than its diff:
```python
import functools

import jax
import jax.numpy as jnp
from jax import lax
from jax.experimental import pallas as pl
from jax.experimental.pallas import tpu as pltpu
from jax.sharding import PartitionSpec as P

D = 384
HEADS = 6
HEAD_DIM = 64
FF = 1536
PATCH_DIM = 768
PATCHES = 196
NCLS = 1000
LAYERS = 3
SEQ = 197

BLK = 208
CLS = 200
TAIL = 192
KEPT = 4
ROWS = KEPT * BLK
HALF = 2 * BLK
CROWS = KEPT * 16
CPAD = 1024
WIDE = 8 * D + FF

NORM_EPS = 1e-06
SMOOTHING = 0.1
CLIP_NORM = 0.05
LEARNING_RATE = 0.05
VECTOR_RATE = 0.5
BETA_FIRST = 0.9
BETA_SECOND = 0.999
ADAM_EPS = 1e-08
WEIGHT_DECAY = 0.05
ADAM_STEP = 10
GELU_SCALE = 0.7978845608028654
GELU_CUBIC = 0.044715

F32 = jnp.float32
BF = jnp.bfloat16


def mm(left, right):
    return jnp.dot(left, right, preferred_element_type=F32)


def mm_nt(left, right):
    return lax.dot_general(left, right, (((1,), (1,)), ((), ())), preferred_element_type=F32)


def mm_tn(left, right):
    return lax.dot_general(left, right, (((0,), (0,)), ((), ())), preferred_element_type=F32)


def fold(values):
    return jnp.sum(values.reshape(-1, 8, values.shape[-1]), axis=0)


def down_sum(values):
    return jnp.sum(values, axis=0, keepdims=True)


def norm(values):
    centre = values - jnp.mean(values, axis=-1, keepdims=True)
    inverse = lax.rsqrt(jnp.mean(centre * centre, axis=-1, keepdims=True) + NORM_EPS)
    return centre * inverse, inverse


def norm_back(upstream, normed, inverse, gain):
    scaled = upstream * gain
    first = jnp.mean(scaled, axis=-1, keepdims=True)
    second = jnp.mean(scaled * normed, axis=-1, keepdims=True)
    return inverse * (scaled - first - normed * second)


def gelu_parts(hidden):
    square = hidden * hidden
    tangent = jnp.tanh(hidden * (GELU_SCALE + (GELU_SCALE * GELU_CUBIC) * square))
    share = 0.5 + 0.5 * tangent
    active = hidden * share
    inner = (2.0 * GELU_SCALE) + (6.0 * GELU_SCALE * GELU_CUBIC) * square
    slope = share + active * (1.0 - share) * inner
    return active, slope


def lane_mask(width, low, high):
    lane = lax.broadcasted_iota(jnp.int32, (1, width), 1)
    return jnp.where((lane >= low) & (lane < high), 1.0, 0.0).astype(BF)


STEP = 32


def pieces(total):
    return [(at, min(STEP, total - at)) for at in range(0, total, STEP)]


def compute(
    pix, wp, win, wdn, vecs, glob, addend, head, hbias, lab,
    gin, gdn, gkv, gpatch, gvec, gfin, gpos, left, right,
    X, N1, H1, I1, QKV, ATT, N2, H2, I2, ACT, SLOPE,
    DXB, DH, DMB, DA, DQKV, KV, SUMS,
):
    even = lane_mask(128, 0, 64)
    odd = lane_mask(128, 64, 128)
    low_lane = lax.broadcasted_iota(jnp.int32, (1, 128), 1) < 64
    key_lane = lax.broadcasted_iota(jnp.int32, (1, BLK), 1)
    key_row = jnp.where((key_lane < PATCHES) | (key_lane == CLS), 0.0, -1e30)
    key_sub = lax.broadcasted_iota(jnp.int32, (BLK, 1), 0)
    key_column = jnp.where((key_sub < PATCHES) | (key_sub == CLS), 0.0, -1e30)

    def vector(layer, at, size):
        return vecs[layer, :, at : at + size]

    def embed(half, carry):
        rows = pl.ds(pl.multiple_of(half * HALF, HALF), HALF)
        made = mm(pix[rows, :], wp[...])
        for image in range(2):
            for at, size in pieces(BLK):
                start = pl.multiple_of(half * HALF + image * BLK + at, 16)
                X[pl.ds(start, size), :] = (
                    made[image * BLK + at : image * BLK + at + size] + addend[at : at + size, :]
                )
        return carry

    lax.fori_loop(0, 2, embed, 0)

    def first_norm(layer, half, columns):
        base = half * HALF
        gain, shift = vector(layer, 0, D), vector(layer, D, D)
        for at, size in pieces(HALF):
            rows = pl.ds(pl.multiple_of(base + at, 16), size)
            normed, inverse = norm(X[rows, :])
            N1[layer, rows, :] = normed.astype(BF)
            I1[layer, rows, :] = jnp.broadcast_to(inverse, (size, 128))
            H1[layer, rows, :] = (normed * gain + shift).astype(BF)
        rows = pl.ds(pl.multiple_of(base, HALF), HALF)
        h1 = H1[layer, rows, :]
        for tile in columns:
            made = mm(h1, win[layer, :, tile * D : (tile + 1) * D])
            if tile == 0:
                made = made + vector(layer, 2 * D, D)
            if tile == 2:
                made = made + vector(layer, 3 * D, D)
            if len(columns) == 3:
                QKV[layer, rows, tile * D : (tile + 1) * D] = made.astype(BF)
            else:
                KV[rows, (tile - 1) * D : tile * D] = made.astype(BF)

    def attend(layer, image):
        rows = pl.ds(pl.multiple_of(image * BLK, BLK), BLK)
        for pair in range(3):
            at = pair * 128
            query = QKV[layer, rows, at : at + 128] * BF(0.125)
            keys = QKV[layer, rows, D + at : D + at + 128]
            values = QKV[layer, rows, 2 * D + at : 2 * D + at + 128]
            both = jnp.concatenate([query * even, query * odd], axis=0)
            scores = mm_nt(both, keys) + key_row
            top = jnp.max(scores, axis=-1, keepdims=True)
            raw = jnp.exp(scores - top)
            probs = (raw * (1.0 / jnp.sum(raw, axis=-1, keepdims=True))).astype(BF)
            made = mm(probs[:BLK], values * even) + mm(probs[BLK:], values * odd)
            ATT[layer, rows, at : at + 128] = made.astype(BF)

    def mlp(layer, half):
        base = half * HALF
        whole = pl.ds(pl.multiple_of(base, HALF), HALF)
        made = mm(ATT[layer, whole, :], win[layer, :, 3 * D : 4 * D])
        bias_out = vector(layer, 4 * D, D)
        gain, shift = vector(layer, 5 * D, D), vector(layer, 6 * D, D)
        for at, size in pieces(HALF):
            rows = pl.ds(pl.multiple_of(base + at, 16), size)
            middle = X[rows, :] + made[at : at + size] + bias_out
            X[rows, :] = middle
            normed, inverse = norm(middle)
            N2[layer, rows, :] = normed.astype(BF)
            I2[layer, rows, :] = jnp.broadcast_to(inverse, (size, 128))
            H2[layer, rows, :] = (normed * gain + shift).astype(BF)
        h2 = H2[layer, whole, :]
        for tile in range(4):
            columns = slice(tile * D, (tile + 1) * D)
            made = mm(h2, win[layer, :, (4 + tile) * D : (5 + tile) * D])
            bias = vector(layer, 7 * D + tile * D, D)
            for at, size in pieces(HALF):
                rows = pl.ds(pl.multiple_of(base + at, 16), size)
                active, slope = gelu_parts(made[at : at + size] + bias)
                ACT[layer, rows, columns] = active.astype(BF)
                SLOPE[layer, rows, columns] = slope.astype(BF)
        made = mm(ACT[layer, whole, :], wdn[layer])
        bias = vector(layer, 7 * D + FF, D)
        for at, size in pieces(HALF):
            rows = pl.ds(pl.multiple_of(base + at, 16), size)
            X[rows, :] = X[rows, :] + made[at : at + size] + bias

    def forward(layer, carry):
        def one(half, c):
            first_norm(layer, half, (0, 1, 2))
            return c

        lax.fori_loop(0, 2, one, 0)

        def two(image, c):
            attend(layer, image)
            return c

        lax.fori_loop(0, KEPT, two, 0)

        def three(half, c):
            mlp(layer, half)
            return c

        lax.fori_loop(0, 2, three, 0)
        return carry

    lax.fori_loop(0, LAYERS - 1, forward, 0)

    last = LAYERS - 1

    def last_norm(half, c):
        first_norm(last, half, (1, 2))
        return c

    lax.fori_loop(0, 2, last_norm, 0)

    def tails(ref, layer=None):
        found = []
        for image in range(KEPT):
            rows = slice(image * BLK + TAIL, (image + 1) * BLK)
            found.append(ref[rows, :] if layer is None else ref[layer, rows, :])
        return jnp.concatenate(found, axis=0)

    h1 = tails(H1, last)
    stream = tails(X)
    query = ((mm(h1, win[last, :, 0:D]) + vector(last, 2 * D, D)).astype(BF)) * BF(0.125)
    head_masks = [lane_mask(D, head * 64, (head + 1) * 64) for head in range(HEADS)]

    def spread(values):
        return jnp.concatenate([values * mask for mask in head_masks], axis=0)

    def gather_heads(values):
        total = None
        for index in range(HEADS):
            part = values[index * 16 : (index + 1) * 16] * head_masks[index].astype(F32)
            total = part if total is None else total + part
        return total

    spread_queries, probabilities, outs = [], [], []
    for image in range(KEPT):
        rows = slice(image * BLK, (image + 1) * BLK)
        queries = spread(query[image * 16 : (image + 1) * 16])
        scores = mm_nt(queries, KV[rows, 0:D]) + key_row
        raw = jnp.exp(scores - jnp.max(scores, axis=-1, keepdims=True))
        probs = raw * (1.0 / jnp.sum(raw, axis=-1, keepdims=True))
        spread_queries.append(queries)
        probabilities.append(probs)
        outs.append(gather_heads(mm(probs.astype(BF), KV[rows, D : 2 * D])))
    attended = jnp.concatenate(outs, axis=0).astype(BF)
    middle = stream + mm(attended, win[last, :, 3 * D : 4 * D]) + vector(last, 4 * D, D)
    n2, i2 = norm(middle)
    h2 = (n2 * vector(last, 5 * D, D) + vector(last, 6 * D, D)).astype(BF)
    active, slope = gelu_parts(mm(h2, win[last, :, 4 * D :]) + vector(last, 7 * D, FF))
    active = active.astype(BF)
    top = middle + mm(active, wdn[last]) + vector(last, 7 * D + FF, D)
    gain_final = glob[2:3, :]
    nf, inf = norm(top)
    final = (nf * gain_final + glob[3:4, :]).astype(BF)
    class_lane = lax.broadcasted_iota(jnp.int32, (1, CPAD), 1)
    logits = mm(final, head[...]) + hbias[...]
    logits = jnp.where(class_lane < NCLS, logits, -1e30)
    peak = jnp.max(logits, axis=-1, keepdims=True)
    shifted = logits - peak
    raw = jnp.exp(shifted)
    total = jnp.sum(raw, axis=-1, keepdims=True)
    log_total = jnp.log(total)
    labels = lab[...]
    alive = jnp.where(labels >= 0, 1.0, 0.0)
    target = jnp.where(class_lane == labels, 1.0 - SMOOTHING, 0.0) + jnp.where(
        class_lane < NCLS, SMOOTHING / NCLS, 0.0
    )
    log_probs = jnp.where(class_lane < NCLS, shifted - log_total, 0.0)
    losses = -jnp.sum(target * log_probs, axis=-1, keepdims=True) * alive
    d_logits = ((raw * (1.0 / total) - target) * alive).astype(BF)
    d_final = mm_nt(d_logits, head[...])
    gfin[:, 0:D] = down_sum(d_final * nf)
    gfin[:, D : 2 * D] = down_sum(d_final)
    gfin[:, 2 * D : 2 * D + 128] = jnp.broadcast_to(down_sum(losses), (1, 128))
    d_top = norm_back(d_final, nf, inf, gain_final)
    low_top = d_top.astype(BF)
    gvec[last, :, 7 * D + FF :] = down_sum(d_top)
    d_up = (mm_nt(low_top, wdn[last]) * slope).astype(BF)
    gvec[last, :, 7 * D : 7 * D + FF] = down_sum(d_up.astype(F32))
    d_h2 = mm_nt(d_up, win[last, :, 4 * D :])
    gvec[last, :, 5 * D : 6 * D] = down_sum(d_h2 * n2)
    gvec[last, :, 6 * D : 7 * D] = down_sum(d_h2)
    d_middle = d_top + norm_back(d_h2, n2, i2, vector(last, 5 * D, D))
    low_middle = d_middle.astype(BF)
    gvec[last, :, 4 * D : 5 * D] = down_sum(d_middle)
    d_heads = mm_nt(low_middle, win[last, :, 3 * D : 4 * D]).astype(BF)
    d_queries = []
    for image in range(KEPT):
        rows = slice(image * BLK, (image + 1) * BLK)
        ups = spread(d_heads[image * 16 : (image + 1) * 16])
        probs = probabilities[image]
        d_probs = mm_nt(ups, KV[rows, D : 2 * D])
        inner = jnp.sum(d_probs * probs, axis=-1, keepdims=True)
        d_scores = (probs * (d_probs - inner)).astype(BF)
        d_queries.append(gather_heads(mm(d_scores, KV[rows, 0:D])) * 0.125)
        DQKV[rows, D : 2 * D] = mm_tn(d_scores, spread_queries[image]).astype(BF)
        DQKV[rows, 2 * D : 3 * D] = mm_tn(probs.astype(BF), ups).astype(BF)
    d_query = jnp.concatenate(d_queries, axis=0).astype(BF)
    gvec[last, :, 2 * D : 3 * D] = down_sum(d_query.astype(F32))
    from_query = mm_nt(d_query, win[last, :, 0:D])

    left[:, 0:FF] = active
    left[:, FF : FF + D] = h2
    left[:, FF + D : FF + 2 * D] = attended
    left[:, FF + 2 * D : FF + 3 * D] = h1
    left[:, FF + 3 * D : FF + 4 * D] = final
    right[:, 0:D] = low_top
    right[:, D : D + FF] = d_up
    right[:, D + FF : 2 * D + FF] = low_middle
    right[:, 2 * D + FF : 3 * D + FF] = d_query
    right[:, 3 * D + FF :] = d_logits

    X[...] = jnp.zeros((ROWS, D), F32)
    for image in range(KEPT):
        X[image * BLK + TAIL : (image + 1) * BLK, :] = d_middle[image * 16 : (image + 1) * 16]

    def store_sums(layer, parts):
        for at, part in parts:
            gvec[layer, :, at : at + part.shape[-1]] = down_sum(part)

    def first_back(layer, half, columns, extra, sums):
        base = half * HALF
        whole = pl.ds(pl.multiple_of(base, HALF), HALF)
        width = D * len(columns)
        grads = DQKV[whole, 3 * D - width : 3 * D]
        made = mm_nt(grads, win[layer, :, 3 * D - width : 3 * D])
        gain = vector(layer, 0, D)
        gain_sum, shift_sum = sums
        for at, size in pieces(HALF):
            rows = pl.ds(pl.multiple_of(base + at, 16), size)
            part = made[at : at + size]
            if extra is not None:
                part = part + extra[rows, :]
            normed = N1[layer, rows, :].astype(F32)
            inverse = I1[layer, rows, :][:, 0:1]
            gain_sum = gain_sum + fold(part * normed)
            shift_sum = shift_sum + fold(part)
            X[rows, :] = X[rows, :] + norm_back(part, normed, inverse, gain)
        return gain_sum, shift_sum

    zeros = jnp.zeros((8, D), F32)

    turned = H1[last].T
    for tile in (1, 2):
        gkv[:, (tile - 1) * D : tile * D] = mm(
            turned, DQKV[:, tile * D : (tile + 1) * D]
        ).astype(BF)
    store_sums(last, [(3 * D, fold(DQKV[:, 2 * D : 3 * D].astype(F32)))])
    SUMS[...] = jnp.zeros((ROWS, D), F32)
    for image in range(KEPT):
        SUMS[image * BLK + TAIL : (image + 1) * BLK, :] = from_query[
            image * 16 : (image + 1) * 16
        ]

    def last_back(half, sums):
        return first_back(last, half, (1, 2), SUMS, sums)

    gain_sum, shift_sum = lax.fori_loop(0, 2, last_back, (zeros, zeros))
    store_sums(last, [(0, gain_sum), (D, shift_sum)])

    def mlp_back(layer, half, sums):
        base = half * HALF
        whole = pl.ds(pl.multiple_of(base, HALF), HALF)
        bias_down, bias_up, gain_sum, shift_sum, bias_out = sums
        for at, size in pieces(HALF):
            rows = pl.ds(pl.multiple_of(base + at, 16), size)
            up = X[rows, :]
            DXB[rows, :] = up.astype(BF)
            bias_down = bias_down + fold(up)
        low = DXB[whole, :]
        ups = []
        for tile in range(4):
            columns = slice(tile * D, (tile + 1) * D)
            made = mm_nt(low, wdn[layer, columns, :])
            total = bias_up[tile]
            for at, size in pieces(HALF):
                rows = pl.ds(pl.multiple_of(base + at, 16), size)
                grad = (made[at : at + size] * SLOPE[layer, rows, columns].astype(F32)).astype(BF)
                DH[rows, columns] = grad
                total = total + fold(grad.astype(F32))
            ups.append(total)
        made = mm_nt(DH[whole, :], win[layer, :, 4 * D :])
        gain = vector(layer, 5 * D, D)
        for at, size in pieces(HALF):
            rows = pl.ds(pl.multiple_of(base + at, 16), size)
            part = made[at : at + size]
            normed = N2[layer, rows, :].astype(F32)
            inverse = I2[layer, rows, :][:, 0:1]
            gain_sum = gain_sum + fold(part * normed)
            shift_sum = shift_sum + fold(part)
            grad = X[rows, :] + norm_back(part, normed, inverse, gain)
            X[rows, :] = grad
            DMB[rows, :] = grad.astype(BF)
            bias_out = bias_out + fold(grad)
        DA[whole, :] = mm_nt(DMB[whole, :], win[layer, :, 3 * D : 4 * D]).astype(BF)
        return bias_down, tuple(ups), gain_sum, shift_sum, bias_out

    def attend_back(layer, image):
        rows = pl.ds(pl.multiple_of(image * BLK, BLK), BLK)
        for pair in range(3):
            at = pair * 128
            query = QKV[layer, rows, at : at + 128] * BF(0.125)
            keys = QKV[layer, rows, D + at : D + at + 128]
            values = QKV[layer, rows, 2 * D + at : 2 * D + at + 128]
            ups = DA[rows, at : at + 128]
            keys_both = jnp.concatenate([keys * even, keys * odd], axis=0)
            values_both = jnp.concatenate([values * even, values * odd], axis=0)
            scores = mm_nt(keys_both, query).reshape(2, BLK, BLK) + key_column[None]
            raw = jnp.exp(scores - jnp.max(scores, axis=1, keepdims=True))
            probs = raw * (1.0 / jnp.sum(raw, axis=1, keepdims=True))
            d_probs = mm_nt(values_both, ups).reshape(2, BLK, BLK)
            inner = jnp.sum(d_probs * probs, axis=1, keepdims=True)
            d_scores = (probs * (d_probs - inner)).astype(BF).reshape(2 * BLK, BLK)
            probs = probs.astype(BF).reshape(2 * BLK, BLK)
            d_values = mm(probs, ups)
            d_keys = mm(d_scores, query)
            d_query = mm_tn(d_scores, keys_both) * 0.125
            DQKV[rows, at : at + 128] = d_query.astype(BF)
            DQKV[rows, D + at : D + at + 128] = jnp.where(
                low_lane, d_keys[:BLK], d_keys[BLK:]
            ).astype(BF)
            DQKV[rows, 2 * D + at : 2 * D + at + 128] = jnp.where(
                low_lane, d_values[:BLK], d_values[BLK:]
            ).astype(BF)

    def backward(step, carry):
        layer = LAYERS - 2 - step

        def one(half, sums):
            return mlp_back(layer, half, sums)

        bias_down, bias_up, gain_sum, shift_sum, bias_out = lax.fori_loop(
            0, 2, one, (zeros, (zeros,) * 4, zeros, zeros, zeros)
        )
        store_sums(
            layer,
            [(7 * D + FF, bias_down), (5 * D, gain_sum), (6 * D, shift_sum), (4 * D, bias_out)]
            + [(7 * D + tile * D, bias_up[tile]) for tile in range(4)],
        )
        turned = DXB[...].T
        for tile in range(4):
            columns = slice(tile * D, (tile + 1) * D)
            gdn[layer, :, columns] = mm(turned, ACT[layer, :, columns]).astype(BF)
        turned = H2[layer].T
        for tile in range(4):
            gin[layer, :, (4 + tile) * D : (5 + tile) * D] = mm(
                turned, DH[:, tile * D : (tile + 1) * D]
            ).astype(BF)
        gin[layer, :, 3 * D : 4 * D] = mm(ATT[layer].T, DMB[...]).astype(BF)

        def two(image, c):
            attend_back(layer, image)
            return c

        lax.fori_loop(0, KEPT, two, 0)
        store_sums(
            layer,
            [
                (2 * D, fold(DQKV[:, 0:D].astype(F32))),
                (3 * D, fold(DQKV[:, 2 * D : 3 * D].astype(F32))),
            ],
        )
        turned = H1[layer].T
        for tile in range(3):
            gin[layer, :, tile * D : (tile + 1) * D] = mm(
                turned, DQKV[:, tile * D : (tile + 1) * D]
            ).astype(BF)

        def three(half, sums):
            return first_back(layer, half, (0, 1, 2), None, sums)

        gain_sum, shift_sum = lax.fori_loop(0, 2, three, (zeros, zeros))
        store_sums(layer, [(0, gain_sum), (D, shift_sum)])
        return carry

    lax.fori_loop(0, LAYERS - 1, backward, 0)

    for at, size in pieces(BLK):
        total = None
        for image in range(KEPT):
            part = X[image * BLK + at : image * BLK + at + size, :]
            DXB[image * BLK + at : image * BLK + at + size, :] = part.astype(BF)
            total = part if total is None else total + part
        gpos[at : at + size, :] = total
    low = DXB[...]
    for tile in range(2):
        columns = slice(tile * D, (tile + 1) * D)
        gpatch[columns, :] = mm_tn(pix[:, columns], low).astype(BF)


def run_compute(pix, wp, win, wdn, vecs, glob, addend, head, hbias, lab):
    def buf(*shape, dtype=BF):
        return pltpu.VMEM(shape, dtype)

    full = pl.BlockSpec(memory_space=pltpu.VMEM)
    keep = LAYERS - 1
    return pl.pallas_call(
        compute,
        out_shape=[
            jax.ShapeDtypeStruct((keep, D, 4 * D + FF), BF),
            jax.ShapeDtypeStruct((keep, D, FF), BF),
            jax.ShapeDtypeStruct((D, 2 * D), BF),
            jax.ShapeDtypeStruct((PATCH_DIM, D), BF),
            jax.ShapeDtypeStruct((LAYERS, 1, WIDE), F32),
            jax.ShapeDtypeStruct((1, 2 * D + 128), F32),
            jax.ShapeDtypeStruct((BLK, D), F32),
            jax.ShapeDtypeStruct((CROWS, FF + 4 * D), BF),
            jax.ShapeDtypeStruct((CROWS, FF + 3 * D + CPAD), BF),
        ],
        in_specs=[full] * 10,
        out_specs=[full] * 9,
        scratch_shapes=[
            buf(ROWS, D, dtype=F32),
            buf(LAYERS, ROWS, D),
            buf(LAYERS, ROWS, D),
            buf(LAYERS, ROWS, 128, dtype=F32),
            buf(keep, ROWS, 3 * D),
            buf(keep, ROWS, D),
            buf(keep, ROWS, D),
            buf(keep, ROWS, D),
            buf(keep, ROWS, 128, dtype=F32),
            buf(keep, ROWS, FF),
            buf(keep, ROWS, FF),
            buf(ROWS, D),
            buf(ROWS, FF),
            buf(ROWS, D),
            buf(ROWS, D),
            buf(ROWS, 3 * D),
            buf(ROWS, 2 * D),
            buf(ROWS, D, dtype=F32),
        ],
        compiler_params=pltpu.CompilerParams(vmem_limit_bytes=60 * 1024 * 1024),
        cost_estimate=pl.CostEstimate(
            flops=24_000_000_000, bytes_accessed=30_000_000, transcendentals=10_000_000
        ),
        name="train_step",
    )(pix, wp, win, wdn, vecs, glob, addend, head, hbias, lab)


def adam_update(weight, first, second, grad, factor, rate):
    grad = grad * factor
    first = BETA_FIRST * first + (1.0 - BETA_FIRST) * grad
    second = BETA_SECOND * second + (1.0 - BETA_SECOND) * grad * grad
    first_hat = first / (1.0 - BETA_FIRST**ADAM_STEP)
    second_hat = second / (1.0 - BETA_SECOND**ADAM_STEP)
    weight = weight - rate * (first_hat / (jnp.sqrt(second_hat) + ADAM_EPS) + WEIGHT_DECAY * weight)
    return (weight, first, second)


def tile_rows(values):
    return jnp.concatenate(
        [
            values[1:],
            jnp.zeros((CLS - PATCHES, D), F32),
            values[:1],
            jnp.zeros((BLK - CLS - 1, D), F32),
        ],
        axis=0,
    )


def shards(
    n_rep,
    n_shard,
    patches,
    labels,
    counts,
    patch_w,
    layer_in,
    layer_down,
    layer_vecs,
    glob_vecs,
    pos_embed,
    head,
    m_patch,
    v_patch,
    m_in,
    v_in,
    m_down,
    v_down,
    m_vecs,
    v_vecs,
    m_glob,
    v_glob,
    m_pos,
    v_pos,
    m_head,
    v_head,
):
    rep = lax.axis_index("rep")
    shard = lax.axis_index("shard")
    half = n_rep // 2
    slot_count = patches.shape[0]
    moves = [(source, source - half) for source in range(half, n_rep)]
    lower = rep < half
    marked = jnp.where(jnp.arange(slot_count) < counts[0], labels, -1)
    came = lax.ppermute(patches[KEPT:], "rep", moves)
    came_marked = lax.ppermute(marked[KEPT:], "rep", moves)
    pix = jnp.where(
        lower, jnp.concatenate([patches[: slot_count - KEPT], came], axis=0), patches[:KEPT]
    )
    pix = jnp.pad(pix, ((0, 0), (0, BLK - PATCHES), (0, 0))).reshape(ROWS, PATCH_DIM)
    chosen = jnp.where(
        lower, jnp.concatenate([marked[: slot_count - KEPT], came_marked]), marked[:KEPT]
    )
    lab = jnp.full((KEPT, 16), -1, jnp.int32).at[:, CLS - TAIL].set(chosen).reshape(CROWS, 1)

    wp = lax.all_gather(patch_w.astype(BF), "shard", axis=0, tiled=True)
    win = lax.all_gather(layer_in.astype(BF), "shard", axis=1, tiled=True)
    wdn = lax.all_gather(layer_down.astype(BF), "shard", axis=1, tiled=True)

    rows = jnp.arange(BLK)[:, None]
    addend = tile_rows(pos_embed) + jnp.where(rows < PATCHES, glob_vecs[0][None], 0.0)
    addend = addend + jnp.where(rows == CLS, glob_vecs[1][None], 0.0)
    head_low = jnp.pad(head[:D].astype(BF), ((0, 0), (0, CPAD - NCLS)))
    head_bias = jnp.pad(head[D:], ((0, 0), (0, CPAD - NCLS)))

    gin, gdn, gkv, gpatch, gvec, gfin, gpos, left, right = run_compute(
        pix, wp, win, wdn, layer_vecs[:, None, :], glob_vecs, addend, head_low, head_bias, lab
    )

    own_in = D // n_shard
    own_down = FF // n_shard
    own_patch = PATCH_DIM // n_shard
    keep = LAYERS - 1
    flat = jnp.concatenate(
        [
            gin.reshape(keep, n_shard, own_in, 4 * D + FF).swapaxes(0, 1).reshape(n_shard, -1),
            gkv.reshape(n_shard, -1),
            gpatch.reshape(n_shard, -1),
            gdn.reshape(keep, D, n_shard, own_down).transpose(2, 0, 1, 3).reshape(n_shard, -1),
        ],
        axis=1,
    )
    mine = lax.psum_scatter(flat, "shard", scatter_dimension=0, tiled=True)
    mine = lax.psum(mine, "rep").reshape(-1).astype(F32)
    sizes = [keep * own_in * (4 * D + FF), own_in * 2 * D, own_patch * D, keep * D * own_down]
    cut = [sum(sizes[:index]) for index in range(5)]
    sum_in = mine[cut[0] : cut[1]].reshape(keep, own_in, 4 * D + FF)
    sum_kv = mine[cut[1] : cut[2]].reshape(own_in, 2 * D)
    grad_patch = mine[cut[2] : cut[3]].reshape(own_patch, D)
    sum_down = mine[cut[3] : cut[4]].reshape(keep, D, own_down).swapaxes(1, 2)
    gvec, gfin, gpos, total = lax.psum(
        (gvec.reshape(LAYERS, WIDE), gfin[0], gpos, counts.astype(F32)), ("rep", "shard")
    )

    picked = slice(CLS - TAIL, None, 16)
    left = lax.all_gather(left[picked], ("rep", "shard"), axis=0, tiled=True)
    right = lax.all_gather(right[picked], ("rep", "shard"), axis=0, tiled=True)

    def rows_of(at, width, count):
        block = lax.dynamic_slice_in_dim(left[:, at : at + width], shard * count, count, axis=1)
        return block

    last_down = mm_tn(rows_of(0, FF, own_down), right[:, 0:D])
    last_up = mm_tn(rows_of(FF, D, own_in), right[:, D : D + FF])
    last_out = mm_tn(rows_of(FF + D, D, own_in), right[:, D + FF : 2 * D + FF])
    last_query = mm_tn(rows_of(FF + 2 * D, D, own_in), right[:, 2 * D + FF : 3 * D + FF])
    d_logits = right[:, 3 * D + FF : 3 * D + FF + NCLS]
    grad_head = jnp.concatenate(
        [
            mm_tn(left[:, FF + 3 * D :], d_logits),
            jnp.sum(d_logits.astype(F32), axis=0, keepdims=True),
        ],
        axis=0,
    )
    last_in = jnp.concatenate([last_query, sum_kv, last_out, last_up], axis=1)
    grad_in = jnp.concatenate([sum_in, last_in[None]], axis=0)
    grad_down = jnp.concatenate([sum_down, last_down[None]], axis=0)
    grad_pos = jnp.concatenate([gpos[CLS : CLS + 1], gpos[:PATCHES]], axis=0)
    grad_glob = jnp.stack(
        [jnp.sum(gpos[:PATCHES], axis=0), gpos[CLS], gfin[:D], gfin[D : 2 * D]]
    )

    inv_count = 1.0 / total[0]
    own_squares = (
        jnp.sum(grad_patch * grad_patch)
        + jnp.sum(grad_in * grad_in)
        + jnp.sum(grad_down * grad_down)
    )
    small_squares = (
        jnp.sum(gvec * gvec)
        + jnp.sum(grad_glob * grad_glob)
        + jnp.sum(grad_pos * grad_pos)
        + jnp.sum(grad_head * grad_head)
    )
    grad_norm = jnp.sqrt(lax.psum(own_squares, "shard") + small_squares) * inv_count
    factor = jnp.minimum(1.0, CLIP_NORM / grad_norm) * inv_count
    loss = gfin[2 * D] * inv_count
    new_patch = adam_update(patch_w, m_patch, v_patch, grad_patch, factor, LEARNING_RATE)
    new_in = adam_update(layer_in, m_in, v_in, grad_in, factor, LEARNING_RATE)
    new_down = adam_update(layer_down, m_down, v_down, grad_down, factor, LEARNING_RATE)
    new_vecs = adam_update(layer_vecs, m_vecs, v_vecs, gvec, factor, VECTOR_RATE)
    new_glob = adam_update(glob_vecs, m_glob, v_glob, grad_glob, factor, VECTOR_RATE)
    new_pos = adam_update(pos_embed, m_pos, v_pos, grad_pos, factor, VECTOR_RATE)
    new_head = adam_update(head, m_head, v_head, grad_head, factor, LEARNING_RATE)
    return (
        loss, grad_norm, *new_patch, *new_in, *new_down, *new_vecs, *new_glob, *new_pos, *new_head
    )


def solution(mesh):
    everywhere = P()
    rows = P("shard", None)
    middle = P(None, "shard", None)
    return jax.shard_map(
        functools.partial(shards, mesh.shape["rep"], mesh.shape["shard"]),
        mesh=mesh,
        in_specs=(
            P(("rep", "shard"), None, None),
            P(("rep", "shard")),
            P(("rep", "shard")),
            rows,
            middle,
            middle,
            *(everywhere,) * 4,
            *(rows,) * 2,
            *(middle,) * 4,
            *(everywhere,) * 8,
        ),
        out_specs=(
            *(everywhere,) * 2,
            *(rows,) * 3,
            *(middle,) * 6,
            *(everywhere,) * 12,
        ),
        check_vma=False,
    )
```

time: 1040 us -> 875 us (0.84); the launches traced: 1040 us -> 859 us
  matrix products: 248 us -> 4.51 us
  local copies, waits for them, and re-layouts: 281 us -> 57.2 us
  other arithmetic: 90.3 us -> 180 us
  Pallas kernels: 0 us -> 85.5 us
  waiting for transfers between devices: 288 us -> 360 us
  blocking collectives: 97.9 us -> 145 us
    dot_general x118 -> x5, matrix products: 248 us -> 4.51 us  [mm_tn(): lax.dot_general(left, right, (((0,), (0,)), ((), ())), preferred_element_...]
    concatenate x1, other arithmetic: 0.62 us -> 97.9 us  [shards(): jnp.concatenate([gin.reshape(keep, n_shard, own_in, 4 * D + FF).swapaxes(...]
    all_gather x1 -> x3, blocking collectives: 9 us -> 97 us  [the longest x1 44.8 us: shards(): right = lax.all_gather(right[picked], ('rep', 'shard'), axis=0, tiled=True)]
    pallas_call x0 -> x1, Pallas kernels: none -> 85.5 us  [run_compute(): pl.pallas_call(compute, out_shape=[jax.ShapeDtypeStruct((keep, D, 4 * D +...]
    convert_element_type x31 -> x0, local copies, waits for them, and re-layouts: 81.1 us -> none  [the longest x12 50.3 us: layer_backward(): jnp.stack([d_query, d_keys, d_values], axis=2).reshape(-1, 3 * D)]
    reduce_scatter x2 -> x0, waiting for transfers between devices: 74.5 us -> none  [the longest x1 66.2 us: shards(): lax.psum_scatter(full_in.astype(jnp.bfloat16), 'shard', scatter_dimension...]
    unnamed x799 -> x97, local copies, waits for them, and re-layouts: 91 us -> 28.2 us
    reshape x24 -> x6, local copies, waits for them, and re-layouts: 69.9 us -> 11.7 us  [the longest x1 4.21 us: shards(): gdn.reshape(keep, D, n_shard, own_down).transpose(2, 0, 1, 3)]
  transfers between devices with their start and end apart: 7 -> 7, of which waited for: 4 -> 5; matrix products, arithmetic and copies ran while one was open for 12% -> 5% of each run, Pallas kernels for 0% -> 0%
where the time goes in v1:
time: 875 us; the launch traced here: 859 us
  waiting for transfers between devices  360 us (41%)
  other arithmetic  180 us (21%)
  blocking collectives  145 us (17%)
  Pallas kernels  85.5 us (10%)
  local copies, waits for them, and re-layouts  57.2 us (7%)
  between operations  24.1 us (3%)
    psum x1, waiting for transfers between devices, shards(): mine = lax.psum(mine, 'rep').reshape(-1).astype(F32)  154 us
    psum x1, waiting for transfers between devices, shards(): lax.psum((gvec.reshape(LAYERS, WIDE), gfin[0], gpos, counts.astype(F32)),...  116 us
    concatenate x1, other arithmetic, shards(): jnp.concatenate([gin.reshape(keep, n_shard, own_in, 4 * D + FF).swapaxes(...  97.9 us
    pallas_call x1, Pallas kernels, run_compute(): pl.pallas_call(compute, out_shape=[jax.ShapeDtypeStruct((keep, D, 4 * D +...  85.5 us
    all_gather x1, waiting for transfers between devices, shards(): win = lax.all_gather(layer_in.astype(BF), 'shard', axis=1, tiled=True)  48.2 us
    all_gather x1, blocking collectives, shards(): right = lax.all_gather(right[picked], ('rep', 'shard'), axis=0, tiled=True)  44.8 us
    psum x1, blocking collectives, shards(): lax.psum((gvec.reshape(LAYERS, WIDE), gfin[0], gpos, counts.astype(F32)),...  40.9 us
    all_gather x1, blocking collectives, shards(): left = lax.all_gather(left[picked], ('rep', 'shard'), axis=0, tiled=True)  39.6 us
  transfers between devices with their start and end apart: 7, of which 5 were waited for; matrix products, arithmetic and copies ran while one was open for 5% of the time, Pallas kernels for 0%

profile of v1, /device:TPU:0, one launch (start us, length us, event | category | flops | bytes accessed | tf_op | source)
XLA Modules:
  0.0 859.4 jit_solution(2747811271456292601)
XLA Ops:
  7.2 2.6 convert_element_type.32
  10.0 1.4 convert_element_type.31
  11.5 2.5 fusion.37
  14.0 1.4 collective-permute-start
  16.7 1.3 collective-permute-start.1
  18.0 12.6 %all_gather.15.wp = bf16[768,384]{1,0:T(8,128)(2,1)} all-gather(bf16[192,384]{1,0:T(8,128)(2,1)S(1)} %convert_element_type.30), channel_id=1, replica_groups=mesh['rep'=8,'shard'=4] {'shard'}, dimensions={0}, use_global_device_ids=true | all-gather | bytes 737280 | tf_op jit(solution)/shard_map/all_gather | solution.py:624
  34.3 2.1 pad.16.head
  37.1 1.6 fusion.7.addend
  38.7 8.2 collective-permute-done.1
  46.9 1.3 fusion.29
  49.1 1.4 maximum_select_fusion
  51.7 48.2 %all-gather.5.cloned.1.call-done.win = bf16[3,384,3072]{2,1,0:T(8,128)(2,1)} async-done(((bf16[3,96,3072]{2,1,0:T(8,128)(2,1)}), bf16[3,384,3072]{2,1,0:T(8,128)(2,1)}) %all-gather.5.cloned.1.call-update) | async-done | bytes 7077904 | tf_op jit(solution)/shard_map/all_gather | solution.py:625
  99.9 85.5 %train_step.1 = (bf16[2,384,3072]{2,1,0:T(8,128)(2,1)}, bf16[2,384,1536]{2,1,0:T(8,128)(2,1)}, bf16[384,768]{1,0:T(8,128)(2,1)}, bf16[768,384]{1,0:T(8,128)(2,1)...) custom-call(bf16[832,768]{1,0:T(8,128)(2,1)} %bitcast.34, ...), custom_call_target="tpu_custom_call" | custom-call | flops 24000000000 | bytes 30000000 | tf_op jit(solution)/shard_map/train_step/pallas_call | solution.py:513
  185.4 4.2 reshape.150
  189.8 1.5 reshape.148
  191.3 2.7 copy.96
  194.0 3.6 copy.109
  197.6 97.9 %pad_maximum_fusion = bf16[4,1032192]{1,0:T(4,128)(2,1)} fusion(bf16[4,294912]{1,0:T(4,128)(2,1)S(1)} %bitcast.32, bf16[4,73728]{1,0:T(4,128)(2,1)S(1)} %reshape.149, bf16[4,73728]{1,0:T(4,128)(2,1)S(1)} %reshape.148, bf16[4,589824]{1,0:T(4,128)(2,1)S(1)} %bitcast.29), kind=kLoop, calls=%fused_computation | loop fusion | flops 33030144 | bytes 16515072 | tf_op jit(solution)/shard_map/concatenate | solution.py:642
  295.6 1.4 copy-done.5
  297.0 1.8 copy.102
  298.8 1.8 copy.99
  300.6 1.8 copy.100
  303.0 40.9 %all-reduce.5 = (f32[896]{0:T(1024)S(1)}, f32[1]{0:T(128)}, f32[3,4608]{1,0:T(4,128)S(1)}) all-reduce(f32[896]{0:T(1024)S(1)} %reduce.10, f32[1]{0:T(128)S(6)} %convert_element_type.33, f32[3,4608]{1,0:T(4,128)S(1)} %bitcast.35), channel_id=1, replica_groups=mesh['rep'=8,'shard'=4] {'rep','shard'}, use_global_device_ids=true, to_apply=%region_1.2 | all-reduce | flops 14721 | bytes 117768 | tf_op jit(solution)/shard_map/psum | solution.py:659
  344.5 1.1 slice.153
  345.7 44.8 %all-gather.1 = bf16[32,4,3712]{2,1,0:T(4,128)(2,1)S(1)} all-gather(bf16[1,4,3712]{2,1,0:T(4,128)(2,1)S(1)} %bitcast.36), channel_id=1, replica_groups=mesh['rep'=8,'shard'=4] {'rep','shard'}, dimensions={0}, use_global_device_ids=true | all-gather | bytes 979968 | tf_op jit(solution)/shard_map/all_gather | solution.py:665
  391.7 39.6 %all-gather = bf16[32,4,3072]{2,1,0:T(4,128)(2,1)S(1)} all-gather(bf16[1,4,3072]{2,1,0:T(4,128)(2,1)S(1)} %bitcast.37), channel_id=1, replica_groups=mesh['rep'=8,'shard'=4] {'rep','shard'}, dimensions={0}, use_global_device_ids=true | all-gather | bytes 811008 | tf_op jit(solution)/shard_map/all_gather | solution.py:664
  431.6 33.4 %all-reduce.14.cloned.1.call-done = bf16[4,1032192]{1,0:T(4,128)(2,1)} async-done(((bf16[4,1032192]{1,0:T(4,128)(2,1)}), bf16[4,1032192]{1,0:T(4,128)(2,1)}) %all-reduce.14.cloned.1.call-update) | async-done | bytes 8257552
  465.0 7.8 constant_dynamic-slice_fusion
  479.4 1.2 fusion.5
  480.5 116.3 %all-reduce.12.cloned.1.call-done = f32[208,384]{1,0:T(8,128)} async-done(((f32[208,384]{1,0:T(8,128)}), f32[208,384]{1,0:T(8,128)}) %all-reduce.12.cloned.1.call-update) | async-done | bytes 319504 | tf_op jit(solution)/shard_map/psum | solution.py:659
  601.9 153.8 %all-reduce.10.cloned.1.call-done = bf16[1,1032192]{1,0:T(2,128)(2,1)} async-done(((bf16[1,1032192]{1,0:T(2,128)(2,1)}), bf16[1,1032192]{1,0:T(2,128)(2,1)}) %all-reduce.10.cloned.1.call-update) | async-done | bytes 2064400 | tf_op jit(solution)/shard_map/psum | solution.py:652
  755.7 2.8 fusion.10
  759.3 25.2 %fusion.1 = f32[589824]{0:T(1024)} fusion(bf16[1,1032192]{1,0:T(2,128)(2,1)} %all-reduce.10.cloned.1.call-done), kind=kLoop, calls=%fused_computation.10 | loop fusion | flops 589824 | bytes 3538944 | tf_op jit(solution)/shard_map/reshape | solution.py:655
  784.5 2.4 reshape.156
  786.9 11.8 %fusion.4 = f32[294912]{0:T(1024)} fusion(bf16[1,1032192]{1,0:T(2,128)(2,1)} %all-reduce.10.cloned.1.call-done), kind=kLoop, calls=%fused_computation.25 | loop fusion | flops 294912 | bytes 1769472 | tf_op jit(solution)/shard_map/transpose | solution.py:658
  798.7 1.7 reshape.158
  800.4 1.3 maximum_bitcast_fusion
  801.7 1.5 multiply_reduce_fusion
  804.6 2.1 multiply_reduce_fusion.1
  808.0 7.3 psum.45
  816.1 2.5 multiply_reduce_fusion.4
  818.6 1.7 mul.349
  820.3 6.0 multiply_subtract_fusion.1
  826.3 2.8 copy.103
  829.2 2.8 copy.104
  832.0 2.9 copy.105
  835.1 8.5 multiply_subtract_fusion
  846.2 3.1 multiply_subtract_fusion.2
  (147 shorter events, 22.8 us)
Async XLA Ops:
  7.2 2.8 copy-start.2
  7.2 44.5 %all-gather.7.cloned.1.call-start = ((), (), s32[]{:S(2)}) async-start(), calls=%async_computation.1 | async-start | bytes 4423680 | tf_op jit(solution)/shard_map/all_gather | solution.py:626
  9.9 89.9 %all-gather.5.cloned.1.call-start = ((), (), s32[]{:S(2)}) async-start(), calls=%async_computation | async-start | bytes 8847360 | tf_op jit(solution)/shard_map/all_gather | solution.py:625
  11.4 4.7 copy-start.40
  11.4 6.6 copy-start.18
  11.4 19.7 %copy-start.15 = (f32[197,384]{1,0:T(8,128)S(1)}, f32[197,384]{1,0:T(8,128)}, u32[]{:S(2)}) copy-start(f32[197,384]{1,0:T(8,128)} %param.34) | copy-start | bytes 907780
  11.5 20.4 %copy-start.6 = (f32[385,1000]{1,0:T(8,128)S(1)}, f32[385,1000]{1,0:T(8,128)}, u32[]{:S(2)}) copy-start(f32[385,1000]{1,0:T(8,128)} %param.35) | copy-start | bytes 4620004
  11.5 453.5 %all-reduce.14.cloned.1.call-start = ((), (), s32[]{:S(2)}) async-start(), calls=%async_computation.4 | async-start | bytes 16515072
  14.0 18.9 %copy-start.26 = (f32[3,4608]{1,0:T(4,128)S(1)}, f32[3,4608]{1,0:T(4,128)}, u32[]{:S(2)}) copy-start(f32[3,4608]{1,0:T(4,128)} %param.32) | copy-start | bytes 165892
  14.0 19.7 %slice-start = ((f32[385,1000]{1,0:T(8,128)}), f32[1,1000]{1,0:T(1,128)S(1)}, s32[]{:S(2)}) async-start(f32[385,1000]{1,0:T(8,128)} %param.35), calls=%async_computation.5 | async-start | bytes 8192 | tf_op jit(solution)/shard_map/slice | solution.py:632
  14.0 35.1 %collective-permute-start = (bf16[2,196,768]{2,1,0:T(8,128)(2,1)}, bf16[2,196,768]{2,1,0:T(8,128)(2,1)}, u32[]{:S(2)}, u32[]{:S(2)}) collective-permute-start(bf16[2,196,768]{2,1,0:T(8,128)(2,1)} %get-tuple-element.174), channel_id=1, source_target_pairs={{16,0},{20,4},{24,8},{28,12},{17,1},{21,5},{25,9},{29,13},{18,2},{... | collective-permute-start | bytes 1806344 | tf_op jit(solution)/shard_map/ppermute | solution.py:613
  16.7 30.2 %collective-permute-start.1 = (s32[2]{0:T(128)}, s32[2]{0:T(128)}, u32[]{:S(2)}, u32[]{:S(2)}) collective-permute-start(s32[2]{0:T(128)} %get-tuple-element.183), channel_id=1, source_target_pairs={{16,0},{20,4},{24,8},{28,12},{17,1},{21,5},{25,9},{29,13},{18,2},{... | collective-permute-start | bytes 32 | tf_op jit(solution)/shard_map/ppermute | solution.py:614
  31.9 5.2 copy-start.35
  31.9 5.2 slice-start.1
  31.9 17.2 %copy-start.8 = (bf16[6,196,768]{2,1,0:T(8,128)(2,1)S(1)}, bf16[6,196,768]{2,1,0:T(8,128)(2,1)}, u32[]{:S(2)}) copy-start(bf16[6,196,768]{2,1,0:T(8,128)(2,1)} %param.26) | copy-start | bytes 5419012
  32.9 4.2 copy-start.17
  185.4 4.2 copy-start.21
  295.6 301.3 %all-reduce.12.cloned.1.call-start = ((), (), s32[]{:S(2)}) async-start(), calls=%async_computation.3 | async-start | bytes 638976 | tf_op jit(solution)/shard_map/psum | solution.py:659
  298.8 1.8 copy-start.12
  300.6 1.8 copy-start.41
  300.6 2.4 copy-start.32
  300.6 2.4 copy-start.39
  344.0 131.7 %copy-start.24 = (f32[3,4608]{1,0:T(4,128)}, f32[3,4608]{1,0:T(4,128)S(1)}, u32[]{:S(2)}) copy-start(f32[3,4608]{1,0:T(4,128)S(1)} %get-tuple-element.151) | copy-start | bytes 165892
  431.6 324.1 %all-reduce.10.cloned.1.call-start = ((), (), s32[]{:S(2)}) async-start(), calls=%async_computation.2 | async-start | bytes 8257536 | tf_op jit(solution)/shard_map/psum | solution.py:652
  474.7 4.7 copy-start
  597.9 161.4 %copy-start.9 = (f32[196,384]{1,0:T(8,128)}, f32[196,384]{1,0:T(8,128)S(1)}, u32[]{:S(2)}) copy-start(f32[196,384]{1,0:T(8,128)S(1)} %get-tuple-element.178) | copy-start | bytes 903172
  597.9 4.0 copy-start.33
  832.0 2.9 copy-start.4
  835.0 8.6 %copy-start.25 = (f32[3,4608]{1,0:T(4,128)S(1)}, f32[3,4608]{1,0:T(4,128)}, u32[]{:S(2)}) copy-start(f32[3,4608]{1,0:T(4,128)} %copy-done.24) | copy-start | bytes 165892
  835.0 8.6 %copy-start.27 = (f32[3,4608]{1,0:T(4,128)S(1)}, f32[3,4608]{1,0:T(4,128)}, u32[]{:S(2)}) copy-start(f32[3,4608]{1,0:T(4,128)} %param.32) | copy-start | bytes 165892
  835.0 8.6 %copy-start.30 = (f32[3,4608]{1,0:T(4,128)S(1)}, f32[3,4608]{1,0:T(4,128)}, u32[]{:S(2)}) copy-start(f32[3,4608]{1,0:T(4,128)} %param.42) | copy-start | bytes 165892
  835.0 8.6 %copy-start.31 = (f32[3,4608]{1,0:T(4,128)S(1)}, f32[3,4608]{1,0:T(4,128)}, u32[]{:S(2)}) copy-start(f32[3,4608]{1,0:T(4,128)} %param.43) | copy-start | bytes 165892
  835.0 9.4 %copy-start.34 = (f32[1,384]{1,0:T(1,128)S(1)}, f32[1,384]{1,0:T(1,128)}, u32[]{:S(2)}) copy-start(f32[1,384]{1,0:T(1,128)} %copy-done.33) | copy-start | bytes 4612
  835.0 9.4 %copy-start.36 = (f32[4,384]{1,0:T(4,128)S(1)}, f32[4,384]{1,0:T(4,128)}, u32[]{:S(2)}) copy-start(f32[4,384]{1,0:T(4,128)} %glob.1) | copy-start | bytes 18436
  835.0 9.4 %copy-start.37 = (f32[4,384]{1,0:T(4,128)S(1)}, f32[4,384]{1,0:T(4,128)}, u32[]{:S(2)}) copy-start(f32[4,384]{1,0:T(4,128)} %param.44) | copy-start | bytes 18436
  835.0 9.4 %copy-start.38 = (f32[4,384]{1,0:T(4,128)S(1)}, f32[4,384]{1,0:T(4,128)}, u32[]{:S(2)}) copy-start(f32[4,384]{1,0:T(4,128)} %param.45) | copy-start | bytes 18436
  835.0 10.0 %copy-start.10 = (f32[196,384]{1,0:T(8,128)S(1)}, f32[196,384]{1,0:T(8,128)}, u32[]{:S(2)}) copy-start(f32[196,384]{1,0:T(8,128)} %copy-done.9) | copy-start | bytes 903172
  835.1 10.0 %copy-start.16 = (f32[197,384]{1,0:T(8,128)S(1)}, f32[197,384]{1,0:T(8,128)}, u32[]{:S(2)}) copy-start(f32[197,384]{1,0:T(8,128)} %param.34) | copy-start | bytes 907780
  835.1 10.0 %copy-start.22 = (f32[197,384]{1,0:T(8,128)S(1)}, f32[197,384]{1,0:T(8,128)}, u32[]{:S(2)}) copy-start(f32[197,384]{1,0:T(8,128)} %param.46) | copy-start | bytes 907780
  835.1 10.0 %copy-start.23 = (f32[197,384]{1,0:T(8,128)S(1)}, f32[197,384]{1,0:T(8,128)}, u32[]{:S(2)}) copy-start(f32[197,384]{1,0:T(8,128)} %param.47) | copy-start | bytes 907780
  835.1 11.1 %copy-start.7 = (f32[385,1000]{1,0:T(8,128)S(1)}, f32[385,1000]{1,0:T(8,128)}, u32[]{:S(2)}) copy-start(f32[385,1000]{1,0:T(8,128)} %param.35) | copy-start | bytes 4620004
  835.1 11.1 %copy-start.13 = (f32[385,1000]{1,0:T(8,128)S(1)}, f32[385,1000]{1,0:T(8,128)}, u32[]{:S(2)}) copy-start(f32[385,1000]{1,0:T(8,128)} %param.48) | copy-start | bytes 4620004
  835.1 11.1 %copy-start.14 = (f32[385,1000]{1,0:T(8,128)S(1)}, f32[385,1000]{1,0:T(8,128)}, u32[]{:S(2)}) copy-start(f32[385,1000]{1,0:T(8,128)} %param.49) | copy-start | bytes 4620004
  843.6 2.6 copy-start.1
  846.2 3.2 copy-start.19
  846.2 3.2 copy-start.20
  846.2 3.2 copy-start.28
  846.2 3.1 copy-start.29
  (3 other events, 4.8 us)
Sparse Core Ops, SparseCore 0:
  10.2 36.4 all-gather.6
  48.8 50.9 all-gather.4
  295.7 169.2 all-reduce.13
  471.1 125.7 all-reduce.11
  600.3 155.2 all-reduce.9

commit v2 on v1

v2 whole, which is shorter than its diff:
```python
import functools

import jax
import jax.numpy as jnp
from jax import lax
from jax.experimental import pallas as pl
from jax.experimental.pallas import tpu as pltpu
from jax.sharding import PartitionSpec as P

D = 384
HEADS = 6
HEAD_DIM = 64
FF = 1536
PATCH_DIM = 768
PATCHES = 196
NCLS = 1000
LAYERS = 3
SEQ = 197

BLK = 208
CLS = 200
TAIL = 192
KEPT = 4
ROWS = KEPT * BLK
HALF = 2 * BLK
CROWS = KEPT * 16
CPAD = 1024
WIDE = 8 * D + FF

NORM_EPS = 1e-06
SMOOTHING = 0.1
CLIP_NORM = 0.05
LEARNING_RATE = 0.05
VECTOR_RATE = 0.5
BETA_FIRST = 0.9
BETA_SECOND = 0.999
ADAM_EPS = 1e-08
WEIGHT_DECAY = 0.05
ADAM_STEP = 10
GELU_SCALE = 0.7978845608028654
GELU_CUBIC = 0.044715

F32 = jnp.float32
BF = jnp.bfloat16


def mm(left, right):
    return jnp.dot(left, right, preferred_element_type=F32)


def mm_nt(left, right):
    return lax.dot_general(left, right, (((1,), (1,)), ((), ())), preferred_element_type=F32)


def mm_tn(left, right):
    return lax.dot_general(left, right, (((0,), (0,)), ((), ())), preferred_element_type=F32)


def fold(values):
    return jnp.sum(values.reshape(-1, 8, values.shape[-1]), axis=0)


def down_sum(values):
    return jnp.sum(values, axis=0, keepdims=True)


def norm(values):
    centre = values - jnp.mean(values, axis=-1, keepdims=True)
    inverse = lax.rsqrt(jnp.mean(centre * centre, axis=-1, keepdims=True) + NORM_EPS)
    return centre * inverse, inverse


def norm_back(upstream, normed, inverse, gain):
    scaled = upstream * gain
    first = jnp.mean(scaled, axis=-1, keepdims=True)
    second = jnp.mean(scaled * normed, axis=-1, keepdims=True)
    return inverse * (scaled - first - normed * second)


def gelu_parts(hidden):
    square = hidden * hidden
    tangent = jnp.tanh(hidden * (GELU_SCALE + (GELU_SCALE * GELU_CUBIC) * square))
    share = 0.5 + 0.5 * tangent
    active = hidden * share
    inner = (2.0 * GELU_SCALE) + (6.0 * GELU_SCALE * GELU_CUBIC) * square
    slope = share + active * (1.0 - share) * inner
    return active, slope


def lane_mask(width, low, high):
    lane = lax.broadcasted_iota(jnp.int32, (1, width), 1)
    return jnp.where((lane >= low) & (lane < high), 1.0, 0.0).astype(BF)


STEP = 32


def pieces(total):
    return [(at, min(STEP, total - at)) for at in range(0, total, STEP)]


WFAC = FF + 5 * D
VEC_ROWS = 256
VEC_AT = BLK
VEC_WIDE = D + 128
MESH = pl.DeviceIdType.MESH
CHUNKS = 6


class Place:
    def __init__(self, n_rep, n_shard):
        self.n_rep, self.n_shard = n_rep, n_shard
        self.n_x = 2 ** ((n_rep.bit_length() - 2) // 2)
        self.n_z = n_rep // self.n_x
        self.n_y = n_shard // 2
        rep, shard = lax.axis_index("rep"), lax.axis_index("shard")
        self.rep, self.shard = rep, shard
        self.z, self.x = rep // self.n_x, rep % self.n_x
        self.y, self.c = shard // 2, shard % 2

    def to(self, x=None, y=None, z=None, c=None):
        x = self.x if x is None else x
        y = self.y if y is None else y
        z = self.z if z is None else z
        c = self.c if c is None else c
        return {"rep": z * self.n_x + x, "shard": y * 2 + c}


def cut(rows, parts, unit):
    return parts if rows % (parts * unit) == 0 else 1


def aligned(value, unit):
    return pl.multiple_of(value, unit)


def train(
    n_rep, n_shard,
    patches, lab_pairs, own_patch, own_in, own_down, vecs, glob, pos, head, count,
    res_out, small_out, vec_out, all_factors,
    X, N1, I1, QKV, ATT, N2, I2, ACT, SLOPE, DXB, DMB, DA,
    pix, lab, wp, win, wdn, low_head, head_bias,
    G, RC, RY, RX, RZ, RES, GS, SC, SY, SX, SZ, SRES,
    FAC, FC, FY, FALL, V, VC, VY, VX, VZ, VF, SQ, SQS, square_sum,
    ag_send, ag_recv, ag_local, rs_send, rs_recv, f_send, f_recv, v_send, v_recv,
    img_send, img_recv, img_local, out_local,
):
    here = Place(n_rep, n_shard)
    n_x, n_y, n_z = here.n_x, here.n_y, here.n_z
    x, y, z, c = here.x, here.y, here.z, here.c
    rows_in, rows_down, rows_patch = D // n_shard, FF // n_shard, PATCH_DIM // n_shard
    block = 4 * rows_in
    mate = here.to(c=1 - c)

    def push(src, dst, send, recv, device):
        pltpu.make_async_remote_copy(
            src_ref=src, dst_ref=dst, send_sem=send, recv_sem=recv,
            device_id=device, device_id_type=MESH,
        ).start()

    def arrived(dst, recv, send):
        pltpu.make_async_remote_copy(
            src_ref=dst, dst_ref=dst, send_sem=send, recv_sem=recv,
            device_id=mate, device_id_type=MESH,
        ).wait_recv()

    def left_here(src, recv, send):
        pltpu.make_async_remote_copy(
            src_ref=src, dst_ref=src, send_sem=send, recv_sem=recv,
            device_id=mate, device_id_type=MESH,
        ).wait_send()

    sent = {}

    def go(source, dst, sems, index, device):
        name, send, recv = sems
        push(source(), dst, send.at[index], recv.at[index], device)
        sent[name, index] = (source, send, recv, index)

    def gone(sems, index):
        source, send, recv, at = sent.pop((sems[0], index))
        left_here(source(), recv.at[at], send.at[at])

    def turn(at, by, size):
        return lax.rem(at + by, size)

    barrier = pltpu.get_barrier_semaphore()
    others = (
        [mate]
        + [here.to(y=turn(y, o, n_y)) for o in range(1, n_y)]
        + [here.to(x=turn(x, o, n_x)) for o in range(1, n_x)]
        + [here.to(z=turn(z, o, n_z)) for o in range(1, n_z)]
    )
    for other in others:
        pl.semaphore_signal(barrier, inc=1, device_id=other, device_id_type=MESH)
    pl.semaphore_wait(barrier, len(others))

    def weight(kind, layer, shard, part=None):
        if kind == "patch":
            parts = cut(rows_patch, n_x, 16)
            rows = rows_patch // parts
            if part is None:
                return wp.at[pl.ds(aligned(shard * rows_patch, 16), rows_patch), :]
            return wp.at[pl.ds(aligned(shard * rows_patch + part * rows, 16), rows), :]
        if kind == "down":
            parts = cut(rows_down, n_x, 16)
            rows = rows_down // parts
            if part is None:
                return wdn.at[layer, pl.ds(aligned(shard * rows_down, 16), rows_down), :]
            return wdn.at[layer, pl.ds(aligned(shard * rows_down + part * rows, 16), rows), :]
        base = 0 if kind == "attn" else 4 * D
        rows = pl.ds(aligned(shard * rows_in, 16), rows_in)
        if part is None:
            return win.at[layer, rows, pl.ds(base, 4 * D)]
        wide = 4 * D // n_x
        return win.at[layer, rows, pl.ds(aligned(base + part * wide, 128), wide)]

    def owned(kind, layer, part=None):
        if kind == "patch":
            if part is None:
                return own_patch
            rows = rows_patch // cut(rows_patch, n_x, 16)
            return own_patch.at[pl.ds(aligned(part * rows, 16), rows), :]
        if kind == "down":
            if part is None:
                return own_down.at[layer]
            rows = rows_down // cut(rows_down, n_x, 16)
            return own_down.at[layer, pl.ds(aligned(part * rows, 16), rows), :]
        base = 0 if kind == "attn" else 4 * D
        if part is None:
            return own_in.at[layer, :, pl.ds(base, 4 * D)]
        wide = 4 * D // n_x
        return own_in.at[layer, :, pl.ds(aligned(base + part * wide, 128), wide)]

    units = [("patch", 0)] + [
        (kind, layer) for layer in range(LAYERS) for kind in ("attn", "up", "down")
    ]

    def parts_of(kind):
        if kind == "patch":
            return cut(rows_patch, n_x, 16)
        if kind == "down":
            return cut(rows_down, n_x, 16)
        return n_x

    ag = ("ag", ag_send, ag_recv)
    base_x = n_y
    base_my = base_x + (n_y - 1) * (n_x - 1)
    base_mx = base_my + (n_y - 1)

    def weights_start(unit):
        kind, layer = units[unit]
        me = here.shard
        part = x if parts_of(kind) > 1 else 0
        for o in range(1, n_y):
            go(
                lambda: owned(kind, layer, part), weight(kind, layer, me, part), ag, (unit, o),
                here.to(y=turn(y, o, n_y)),
            )
        go(lambda: owned(kind, layer), weight(kind, layer, me), ag, (unit, 0), mate)
        pltpu.make_async_copy(
            owned(kind, layer), weight(kind, layer, me), ag_local.at[unit]
        ).start()

    def weights_forward(unit):
        kind, layer = units[unit]
        split = parts_of(kind) > 1
        part = x if split else 0
        for o in range(1, n_y):
            def make(o=o):
                return weight(kind, layer, turn(y, n_y - o, n_y) * 2 + c, part)

            arrived(make(), ag_recv.at[unit, o], ag_send.at[unit, o])
            if split:
                for p in range(1, n_x):
                    index = base_x + (o - 1) * (n_x - 1) + p - 1
                    go(make, make(), ag, (unit, index), here.to(x=turn(x, p, n_x)))
            go(make, make(), ag, (unit, base_my + o - 1), mate)

    def weights_ready(unit):
        kind, layer = units[unit]
        split = parts_of(kind) > 1
        part = x if split else 0
        if split:
            for o in range(1, n_y):
                for p in range(1, n_x):
                    index = (o - 1) * (n_x - 1) + p - 1

                    def make(o=o, p=p):
                        shard = turn(y, n_y - o, n_y) * 2 + c
                        return weight(kind, layer, shard, turn(x, n_x - p, n_x))

                    arrived(
                        make(), ag_recv.at[unit, base_x + index], ag_send.at[unit, base_x + index]
                    )
                    go(make, make(), ag, (unit, base_mx + index), mate)
        pltpu.make_async_copy(
            owned(kind, layer), weight(kind, layer, here.shard), ag_local.at[unit]
        ).wait()
        arrived(weight(kind, layer, y * 2 + 1 - c), ag_recv.at[unit, 0], ag_send.at[unit, 0])
        for o in range(1, n_y):
            shard = turn(y, n_y - o, n_y) * 2 + 1 - c
            index = base_my + o - 1
            arrived(weight(kind, layer, shard, part), ag_recv.at[unit, index], ag_send.at[unit, index])
            if split:
                for p in range(1, n_x):
                    index = base_mx + (o - 1) * (n_x - 1) + p - 1
                    piece = weight(kind, layer, shard, turn(x, n_x - p, n_x))
                    arrived(piece, ag_recv.at[unit, index], ag_send.at[unit, index])

    lower = here.rep < n_rep // 2
    partner = here.to(z=turn(z, n_z // 2, n_z))
    back_half = pix.at[pl.ds(2, 2)]
    given = patches.at[pl.ds(KEPT, 2)]

    def local_half(half):
        return pltpu.make_async_copy(
            patches.at[pl.ds(2 * half, 2)], pix.at[pl.ds(2 * half, 2)], img_local.at[half]
        )

    def local_lab(half):
        return pltpu.make_async_copy(lab_pairs.at[half], lab.at[half], img_local.at[2 + half])

    local_half(0).start()
    local_lab(0).start()

    @pl.when(jnp.logical_not(lower))
    def _():
        push(given, back_half, img_send.at[0], img_recv.at[0], partner)
        push(lab_pairs.at[2], lab.at[1], img_send.at[1], img_recv.at[1], partner)
        local_half(1).start()
        local_lab(1).start()

    for unit in range(4):
        weights_start(unit)

    even = lane_mask(128, 0, 64)
    odd = lane_mask(128, 64, 128)
    low_lane = lax.broadcasted_iota(jnp.int32, (1, 128), 1) < 64
    key_lane = lax.broadcasted_iota(jnp.int32, (1, BLK), 1)
    key_row = jnp.where((key_lane < PATCHES) | (key_lane == CLS), 0.0, -1e30)
    key_sub = lax.broadcasted_iota(jnp.int32, (BLK, 1), 0)
    key_column = jnp.where((key_sub < PATCHES) | (key_sub == CLS), 0.0, -1e30)
    whole_lanes = NCLS // 128 * 128
    low_head[:, 0:whole_lanes] = head[0:D, 0:whole_lanes].astype(BF)
    low_head[:, whole_lanes:] = jnp.zeros((D, CPAD - whole_lanes), BF)
    low_head[:, whole_lanes:NCLS] = head[0:D, whole_lanes:NCLS].astype(BF)
    head_bias[...] = jnp.zeros((1, CPAD), F32)
    head_bias[:, 0:NCLS] = head[D : D + 1, :]
    V[...] = jnp.zeros((VEC_ROWS, VEC_WIDE), F32)
    square_sum[...] = jnp.zeros((8, 128), F32)
    zeros = jnp.zeros((8, D), F32)
    patch_bias = glob[0:1, :]

    def vector(layer, at, size):
        return vecs[pl.ds(layer, 1), at : at + size]

    def store_vector(layer, at, row):
        for piece in range(row.shape[-1] // D):
            V[pl.ds(VEC_AT + 12 * layer + at // D + piece, 1), 0:D] = row[
                :, piece * D : (piece + 1) * D
            ]

    def store_sums(layer, parts):
        for at, part in parts:
            store_vector(layer, at, down_sum(part))

    def embed(half):
        made = mm(pix[pl.ds(2 * half, 2)].reshape(HALF, PATCH_DIM), wp[...])
        for image in range(2):
            start = aligned(half * HALF + image * BLK, 16)
            for at, size in pieces(PATCHES - 4):
                X[pl.ds(start + at, size), :] = (
                    made[image * BLK + at : image * BLK + at + size]
                    + pos[1 + at : 1 + at + size, :]
                    + patch_bias
                )
            X[pl.ds(start + TAIL, 16), :] = jnp.zeros((16, D), F32)
            X[pl.ds(start + TAIL, 4), :] = (
                made[image * BLK + TAIL : image * BLK + PATCHES]
                + pos[1 + TAIL : 1 + PATCHES, :]
                + patch_bias
            )
            X[pl.ds(start + CLS, 1), :] = glob[1:2, :] + pos[0:1, :]

    def first_norm(layer, half, columns):
        base = half * HALF
        gain, shift = vector(layer, 0, D), vector(layer, D, D)
        for at, size in pieces(HALF):
            rows = pl.ds(aligned(base + at, 16), size)
            normed, inverse = norm(X[rows, :])
            N1[layer, rows, :] = normed.astype(BF)
            I1[layer, rows, :] = jnp.broadcast_to(inverse, (size, 128))
            DXB[rows, :] = (normed * gain + shift).astype(BF)
        rows = pl.ds(aligned(base, 16), HALF)
        h1 = DXB[rows, :]
        for tile in columns:
            made = mm(h1, win[layer, :, tile * D : (tile + 1) * D])
            if tile == 0:
                made = made + vector(layer, 2 * D, D)
            if tile == 2:
                made = made + vector(layer, 3 * D, D)
            if len(columns) == 3:
                QKV[layer, rows, tile * D : (tile + 1) * D] = made.astype(BF)
            else:
                (DMB if tile == 1 else DA)[rows, :] = made.astype(BF)

    def attend(layer, image):
        rows = pl.ds(aligned(image * BLK, 16), BLK)
        for pair in range(3):
            at = pair * 128
            query = QKV[layer, rows, at : at + 128] * BF(0.125)
            keys = QKV[layer, rows, D + at : D + at + 128]
            values = QKV[layer, rows, 2 * D + at : 2 * D + at + 128]
            both = jnp.concatenate([query * even, query * odd], axis=0)
            scores = mm_nt(both, keys) + key_row
            top = jnp.max(scores, axis=-1, keepdims=True)
            raw = jnp.exp(scores - top)
            probs = (raw * (1.0 / jnp.sum(raw, axis=-1, keepdims=True))).astype(BF)
            made = mm(probs[:BLK], values * even) + mm(probs[BLK:], values * odd)
            ATT[layer, rows, at : at + 128] = made.astype(BF)

    def mlp(layer, half):
        base = half * HALF
        whole = pl.ds(aligned(base, 16), HALF)
        made = mm(ATT[layer, whole, :], win[layer, :, 3 * D : 4 * D])
        bias_out = vector(layer, 4 * D, D)
        gain, shift = vector(layer, 5 * D, D), vector(layer, 6 * D, D)
        for at, size in pieces(HALF):
            rows = pl.ds(aligned(base + at, 16), size)
            middle = X[rows, :] + made[at : at + size] + bias_out
            X[rows, :] = middle
            normed, inverse = norm(middle)
            N2[layer, rows, :] = normed.astype(BF)
            I2[layer, rows, :] = jnp.broadcast_to(inverse, (size, 128))
            DXB[rows, :] = (normed * gain + shift).astype(BF)
        h2 = DXB[whole, :]
        for tile in range(4):
            columns = slice(tile * D, (tile + 1) * D)
            made = mm(h2, win[layer, :, (4 + tile) * D : (5 + tile) * D])
            bias = vector(layer, 7 * D + tile * D, D)
            for at, size in pieces(HALF):
                rows = pl.ds(aligned(base + at, 16), size)
                active, slope = gelu_parts(made[at : at + size] + bias)
                ACT[layer, rows, columns] = active.astype(BF)
                SLOPE[layer, rows, columns] = slope.astype(BF)
        made = mm(ACT[layer, whole, :], wdn[layer])
        bias = vector(layer, 7 * D + FF, D)
        for at, size in pieces(HALF):
            rows = pl.ds(aligned(base + at, 16), size)
            X[rows, :] = X[rows, :] + made[at : at + size] + bias

    def when(condition, *steps):
        @pl.when(condition)
        def _():
            for step, unit in steps:
                step(unit)

    weights_forward(0)
    weights_ready(0)

    def forward_half(half, carry):
        start = half == 0

        @pl.when(start)
        def _():
            local_half(0).wait()

        @pl.when(jnp.logical_and(half == 1, lower))
        def _():
            arrived(back_half, img_recv.at[0], img_send.at[0])

        @pl.when(jnp.logical_and(half == 1, jnp.logical_not(lower)))
        def _():
            local_half(1).wait()

        embed(half)

        def forward_layer(layer, inner):
            first = jnp.logical_and(start, layer == 0)
            second = jnp.logical_and(start, layer == 1)
            when(first, (weights_forward, 1), (weights_start, 4), (weights_ready, 1))
            when(second, (weights_ready, 4))
            first_norm(layer, half, (0, 1, 2))
            when(first, (weights_forward, 2), (weights_start, 5))
            when(second, (weights_forward, 6), (weights_start, 9))

            def attend_one(index, nothing):
                attend(layer, 2 * half + index)
                begin = index == 0
                when(
                    jnp.logical_and(first, begin), (weights_forward, 3), (weights_start, 6)
                )
                when(jnp.logical_and(second, begin), (weights_forward, 7))
                return nothing

            lax.fori_loop(0, 2, attend_one, 0)
            when(
                first, (weights_forward, 4), (weights_start, 7), (weights_ready, 2),
                (weights_ready, 3),
            )
            when(second, (weights_forward, 8), (weights_ready, 5), (weights_ready, 6))
            mlp(layer, half)
            when(first, (weights_forward, 5), (weights_start, 8))
            when(second, (weights_forward, 9))
            return inner

        return lax.fori_loop(0, LAYERS - 1, forward_layer, carry)

    lax.fori_loop(0, 2, forward_half, 0)
    for unit in (7, 8, 9):
        weights_ready(unit)

    last = LAYERS - 1

    def last_norm(half, nothing):
        first_norm(last, half, (1, 2))
        return nothing

    lax.fori_loop(0, 2, last_norm, 0)

    fac = ("f", f_send, f_recv)
    f_y, f_x = 1, n_y
    f_z = f_x + n_x - 1
    f_m = f_z + n_z - 1
    group = KEPT * n_shard

    def factors_core():
        go(lambda: FAC.at[1 - c], FC, fac, 0, mate)

    def factors_y():
        arrived(FC, f_recv.at[0], f_send.at[0])
        FAC[c] = FAC[c] + FC[...]
        for o in range(1, n_y):
            go(lambda: FAC.at[c], FY.at[o - 1], fac, f_y + o - 1, here.to(y=turn(y, o, n_y)))

    def factors_x():
        total = FAC[c]
        for o in range(1, n_y):
            arrived(FY.at[o - 1], f_recv.at[f_y + o - 1], f_send.at[f_y + o - 1])
            total = total + FY[o - 1]
        FALL[x] = total
        for o in range(1, n_x):
            go(lambda: FALL.at[x], FALL.at[x], fac, f_x + o - 1, here.to(x=turn(x, o, n_x)))

    def all_rows(at):
        return all_factors.at[c, pl.ds(at * n_x, n_x)]

    def factors_z():
        for o in range(1, n_x):
            index = f_x + o - 1
            arrived(FALL.at[turn(x, n_x - o, n_x)], f_recv.at[index], f_send.at[index])
        pltpu.make_async_copy(FALL, all_rows(z), out_local.at[0]).start()
        for o in range(1, n_z):
            go(lambda: FALL, all_rows(z), fac, f_z + o - 1, here.to(z=turn(z, o, n_z)))

    def factors_mate():
        for o in range(1, n_z):
            index = f_z + o - 1
            arrived(all_rows(turn(z, n_z - o, n_z)), f_recv.at[index], f_send.at[index])
        pltpu.make_async_copy(FALL, all_rows(z), out_local.at[0]).wait()
        go(lambda: all_factors.at[c], all_factors.at[c], fac, f_m, mate)

    def factors_done():
        arrived(all_factors.at[1 - c], f_recv.at[f_m], f_send.at[f_m])

    rs = ("rs", rs_send, rs_recv)
    r_y, r_x = 1, n_y
    r_z = r_x + n_x - 1
    r_gz = r_z + n_z - 1
    r_gx = r_gz + n_z - 1

    def chunk(k):
        if k < CHUNKS:
            return G.at[k], RC.at[k % 3], RY.at[k % 3], RX.at[k], RZ.at[k], RES.at[k], block
        k = k - CHUNKS
        return GS.at[k], SC.at[k], SY.at[k], SX.at[k], SZ.at[k], SRES.at[k], block // 2

    def splits(rows):
        by_x = cut(rows, n_x, 16)
        by_z = cut(rows // by_x, n_z, 16)
        return by_x, rows // by_x, by_z, rows // by_x // by_z

    def add_rows(rows, target, target_at, sources):
        step = 48 if rows % 48 == 0 else 16

        def one(index, nothing):
            at = index * step
            to = pl.ds(aligned(target_at + at, 16), step)
            total = target[to, :]
            if len(sources) == 1:
                total = total + sources[0][pl.ds(aligned(at, 16), step), :]
            else:
                total = total.astype(F32)
                for source in sources:
                    total = total + source[pl.ds(aligned(at, 16), step), :].astype(F32)
                total = total.astype(BF)
            target[to, :] = total
            return nothing

        lax.fori_loop(0, rows // step, one, 0)

    def reduce_core(k):
        g, rc = chunk(k)[0:2]
        go(lambda: chunk(k)[0].at[:, 1 - c], rc, rs, (k, 0), mate)

    def reduce_y(k):
        g, rc, ry, _, _, _, rows = chunk(k)
        arrived(rc, rs_recv.at[k, 0], rs_send.at[k, 0])
        for o in list(range(1, n_y)) + [0]:
            at = turn(y, o, n_y)
            add_rows(rows, g.at[at, c], 0, [rc.at[at]])
            if o:
                go(
                    lambda o=o: chunk(k)[0].at[turn(y, o, n_y), c], ry.at[o - 1], rs,
                    (k, r_y + o - 1), here.to(y=at),
                )

    def total_of(slots, count, at, step):
        total = None
        for index in range(count):
            value = slots[index, pl.ds(aligned(at, 16), step), :].astype(F32)
            total = value if total is None else total + value
        return total

    def reduce_x(k):
        g, _, ry, rx, _, _, rows = chunk(k)
        by_x, rows_x = splits(rows)[0:2]
        for o in range(1, n_y):
            arrived(ry.at[o - 1], rs_recv.at[k, r_y + o - 1], rs_send.at[k, r_y + o - 1])
        mine = g.at[y, c]
        add_rows(rows, mine, 0, [ry.at[o - 1] for o in range(1, n_y)])
        for o in range(1, n_x):
            to = turn(x, o, n_x)
            if by_x > 1:

                def make(o=o):
                    at = turn(x, o, n_x) * rows_x
                    return chunk(k)[0].at[y, c, pl.ds(aligned(at, 16), rows_x), :]

                go(make, rx.at[o - 1], rs, (k, r_x + o - 1), here.to(x=to))
            else:
                go(lambda: chunk(k)[0].at[y, c], rx.at[x], rs, (k, r_x + o - 1), here.to(x=to))

    def reduce_z(k):
        g, _, _, rx, rz, _, rows = chunk(k)
        by_x, rows_x, by_z, rows_z = splits(rows)
        mine = g.at[y, c]
        for o in range(1, n_x):
            slot = rx.at[o - 1] if by_x > 1 else rx.at[turn(x, n_x - o, n_x)]
            arrived(slot, rs_recv.at[k, r_x + o - 1], rs_send.at[k, r_x + o - 1])
        if by_x > 1:
            start = x * rows_x
            add_rows(rows_x, mine, start, [rx.at[o - 1] for o in range(1, n_x)])
        else:
            start = 0
            rx[x] = mine[...]
            for o in range(1, n_x):
                gone(rs, (k, r_x + o - 1))
            step = 48 if rows % 48 == 0 else 16

            def one(index, nothing):
                at = pl.ds(aligned(index * step, 16), step)
                g[y, c, at, :] = total_of(rx, n_x, index * step, step).astype(BF)
                return nothing

            lax.fori_loop(0, rows // step, one, 0)
        for o in range(1, n_z):

            def make(o=o):
                at = x * rows_x if by_x > 1 else 0
                if by_z > 1:
                    at = at + turn(z, o, n_z) * rows_z
                return chunk(k)[0].at[y, c, pl.ds(aligned(at, 16), rows_z), :]

            slot = rz.at[o - 1] if by_z > 1 else rz.at[z]
            go(make, slot, rs, (k, r_z + o - 1), here.to(z=turn(z, o, n_z)))

    def gather_z(k):
        g, _, _, _, rz, res, rows = chunk(k)
        by_x, rows_x, by_z, rows_z = splits(rows)
        start = x * rows_x if by_x > 1 else 0
        if by_z > 1:
            start = start + z * rows_z
        for o in range(1, n_z):
            slot = rz.at[o - 1] if by_z > 1 else rz.at[turn(z, n_z - o, n_z)]
            arrived(slot, rs_recv.at[k, r_z + o - 1], rs_send.at[k, r_z + o - 1])
        own_slot = n_z - 1 if by_z > 1 else z
        rz[own_slot] = g[y, c, pl.ds(aligned(start, 16), rows_z), :]
        share = 1.0 / ((1 if by_x > 1 else n_x) * (1 if by_z > 1 else n_z))
        step = 48 if rows_z % 48 == 0 else 16

        def one(index, total):
            low = total_of(rz, n_z, index * step, step).astype(BF)
            res[pl.ds(aligned(start + index * step, 16), step), :] = low
            wide = low.astype(F32)
            return total + fold(wide * wide)

        total = lax.fori_loop(0, rows_z // step, one, zeros) * share
        for at in range(0, D, 128):
            square_sum[...] = square_sum[...] + total[:, at : at + 128]
        if by_z > 1:

            def make():
                at = x * rows_x if by_x > 1 else 0
                return chunk(k)[5].at[pl.ds(aligned(at + z * rows_z, 16), rows_z), :]

            for o in range(1, n_z):
                go(make, make(), rs, (k, r_gz + o - 1), here.to(z=turn(z, o, n_z)))

    def gather_x(k):
        res, rows = chunk(k)[5:7]
        by_x, rows_x, by_z, rows_z = splits(rows)
        if by_z > 1:
            for o in range(1, n_z):
                start = turn(z, n_z - o, n_z) * rows_z
                if by_x > 1:
                    start = start + x * rows_x
                arrived(
                    res.at[pl.ds(aligned(start, 16), rows_z), :],
                    rs_recv.at[k, r_gz + o - 1], rs_send.at[k, r_gz + o - 1],
                )
        if by_x > 1:

            def make():
                return chunk(k)[5].at[pl.ds(aligned(x * rows_x, 16), rows_x), :]

            for o in range(1, n_x):
                go(make, make(), rs, (k, r_gx + o - 1), here.to(x=turn(x, o, n_x)))

    def result(k):
        if k < CHUNKS:
            return pltpu.make_async_copy(RES.at[k], res_out.at[k], out_local.at[1 + k])
        return pltpu.make_async_copy(
            SRES.at[k - CHUNKS], small_out.at[k - CHUNKS], out_local.at[1 + k]
        )

    def gather_done(k):
        res, rows = chunk(k)[5:7]
        by_x, rows_x = splits(rows)[0:2]
        if by_x > 1:
            for o in range(1, n_x):
                start = turn(x, n_x - o, n_x) * rows_x
                arrived(
                    res.at[pl.ds(aligned(start, 16), rows_x), :],
                    rs_recv.at[k, r_gx + o - 1], rs_send.at[k, r_gx + o - 1],
                )
        result(k).start()

    def tails(ref, layer=None):
        found = []
        for image in range(KEPT):
            rows = slice(image * BLK + TAIL, (image + 1) * BLK)
            found.append(ref[rows, :] if layer is None else ref[layer, rows, :])
        return jnp.concatenate(found, axis=0)

    @pl.when(lower)
    def _():
        arrived(lab.at[1], img_recv.at[1], img_send.at[1])

    @pl.when(jnp.logical_not(lower))
    def _():
        local_lab(1).wait()

    local_lab(0).wait()
    labels = lab[...].reshape(CROWS, 128)[:, 0:1]

    h1 = tails(DXB)
    stream = tails(X)
    query = ((mm(h1, win[last, :, 0:D]) + vector(last, 2 * D, D)).astype(BF)) * BF(0.125)
    head_masks = [lane_mask(D, index * 64, (index + 1) * 64) for index in range(HEADS)]

    def spread(values):
        return jnp.concatenate([values * mask for mask in head_masks], axis=0)

    def gather_heads(values):
        total = None
        for index in range(HEADS):
            part = values[index * 16 : (index + 1) * 16] * head_masks[index].astype(F32)
            total = part if total is None else total + part
        return total

    spread_queries, probabilities, outs = [], [], []
    for image in range(KEPT):
        rows = slice(image * BLK, (image + 1) * BLK)
        queries = spread(query[image * 16 : (image + 1) * 16])
        scores = mm_nt(queries, DMB[rows, :]) + key_row
        raw = jnp.exp(scores - jnp.max(scores, axis=-1, keepdims=True))
        probs = raw * (1.0 / jnp.sum(raw, axis=-1, keepdims=True))
        spread_queries.append(queries)
        probabilities.append(probs)
        outs.append(gather_heads(mm(probs.astype(BF), DA[rows, :])))
    attended = jnp.concatenate(outs, axis=0).astype(BF)
    middle = stream + mm(attended, win[last, :, 3 * D : 4 * D]) + vector(last, 4 * D, D)
    n2, i2 = norm(middle)
    h2 = (n2 * vector(last, 5 * D, D) + vector(last, 6 * D, D)).astype(BF)
    active, slope = gelu_parts(mm(h2, win[last, :, 4 * D :]) + vector(last, 7 * D, FF))
    active = active.astype(BF)
    top = middle + mm(active, wdn[last]) + vector(last, 7 * D + FF, D)
    gain_final = glob[2:3, :]
    nf, inf = norm(top)
    final = (nf * gain_final + glob[3:4, :]).astype(BF)
    class_lane = lax.broadcasted_iota(jnp.int32, (1, CPAD), 1)
    logits = mm(final, low_head[...]) + head_bias[...]
    logits = jnp.where(class_lane < NCLS, logits, -1e30)
    peak = jnp.max(logits, axis=-1, keepdims=True)
    shifted = logits - peak
    raw = jnp.exp(shifted)
    total = jnp.sum(raw, axis=-1, keepdims=True)
    alive = jnp.where(labels >= 0.0, 1.0, 0.0)
    target = jnp.where(class_lane.astype(F32) == labels, 1.0 - SMOOTHING, 0.0) + jnp.where(
        class_lane < NCLS, SMOOTHING / NCLS, 0.0
    )
    log_probs = jnp.where(class_lane < NCLS, shifted - jnp.log(total), 0.0)
    losses = -jnp.sum(target * log_probs, axis=-1, keepdims=True) * alive
    d_logits = ((raw * (1.0 / total) - target) * alive).astype(BF)
    d_final = mm_nt(d_logits, low_head[...])
    last_row = VEC_AT + 12 * LAYERS
    V[last_row : last_row + 1, 0:D] = down_sum(d_final * nf)
    V[last_row + 1 : last_row + 2, 0:D] = down_sum(d_final)
    V[last_row + 2 : last_row + 3, 0:128] = jnp.broadcast_to(down_sum(losses), (1, 128))
    V[last_row + 3 : last_row + 4, 0:128] = count[...]
    d_top = norm_back(d_final, nf, inf, gain_final)
    low_top = d_top.astype(BF)
    store_vector(last, 7 * D + FF, down_sum(d_top))
    d_up = (mm_nt(low_top, wdn[last]) * slope).astype(BF)
    store_vector(last, 7 * D, down_sum(d_up.astype(F32)))
    d_h2 = mm_nt(d_up, win[last, :, 4 * D :])
    store_vector(last, 5 * D, down_sum(d_h2 * n2))
    store_vector(last, 6 * D, down_sum(d_h2))
    d_middle = d_top + norm_back(d_h2, n2, i2, vector(last, 5 * D, D))
    low_middle = d_middle.astype(BF)
    store_vector(last, 4 * D, down_sum(d_middle))
    d_heads = mm_nt(low_middle, win[last, :, 3 * D : 4 * D]).astype(BF)
    d_queries = []
    for image in range(KEPT):
        rows = slice(image * BLK, (image + 1) * BLK)
        ups = spread(d_heads[image * 16 : (image + 1) * 16])
        probs = probabilities[image]
        d_probs = mm_nt(ups, DA[rows, :])
        inner = jnp.sum(d_probs * probs, axis=-1, keepdims=True)
        d_scores = (probs * (d_probs - inner)).astype(BF)
        d_queries.append(gather_heads(mm(d_scores, DMB[rows, :])) * 0.125)
        DMB[rows, :] = mm_tn(d_scores, spread_queries[image]).astype(BF)
        DA[rows, :] = mm_tn(probs.astype(BF), ups).astype(BF)
    d_query = jnp.concatenate(d_queries, axis=0).astype(BF)
    store_vector(last, 2 * D, down_sum(d_query.astype(F32)))
    from_query = mm_nt(d_query, win[last, :, 0:D])

    pick_row = lax.broadcasted_iota(jnp.int32, (group, CROWS), 0)
    pick_lane = lax.broadcasted_iota(jnp.int32, (group, CROWS), 1)
    pick = jnp.where(
        ((pick_row - KEPT * here.shard) * 16 + (CLS - TAIL)) == pick_lane, 1.0, 0.0
    ).astype(BF)
    at = 0
    for piece in (active, h2, attended, h1, final, low_top):
        FAC[0, :, at : at + piece.shape[-1]] = mm(pick, piece).astype(BF)
        at += piece.shape[-1]
    at = 0
    for piece in (d_up, low_middle, d_query, d_logits):
        FAC[1, :, at : at + piece.shape[-1]] = mm(pick, piece).astype(BF)
        at += piece.shape[-1]
    FAC[1, :, at:] = jnp.zeros((group, WFAC - at), BF)
    factors_core()

    turned = DXB[...].T
    for tile, grads in enumerate((DMB, DA)):
        made = mm(turned, grads[...]).astype(BF)
        for shard in range(n_shard):
            GS[0, shard // 2, shard % 2, tile * rows_in : (tile + 1) * rows_in, :] = made[
                shard * rows_in : (shard + 1) * rows_in
            ]
    reduce_core(CHUNKS)
    factors_y()
    store_sums(last, [(3 * D, fold(DA[...].astype(F32)))])

    X[...] = jnp.zeros((ROWS, D), F32)
    gain = vector(last, 0, D)
    gain_sum, shift_sum = zeros, zeros
    for image in range(KEPT):
        rows = slice(image * BLK + TAIL, (image + 1) * BLK)
        part = from_query[image * 16 : (image + 1) * 16]
        normed = N1[last, rows, :].astype(F32)
        gain_sum = gain_sum + fold(part * normed)
        shift_sum = shift_sum + fold(part)
        X[rows, :] = d_middle[image * 16 : (image + 1) * 16] + norm_back(
            part, normed, I1[last, rows, :][:, 0:1], gain
        )

    def first_back(layer, half, made, sums):
        base = half * HALF
        gain = vector(layer, 0, D)
        gain_sum, shift_sum = sums
        for at, size in pieces(HALF):
            rows = pl.ds(aligned(base + at, 16), size)
            part = made[at : at + size]
            normed = N1[layer, rows, :].astype(F32)
            inverse = I1[layer, rows, :][:, 0:1]
            gain_sum = gain_sum + fold(part * normed)
            shift_sum = shift_sum + fold(part)
            X[rows, :] = X[rows, :] + norm_back(part, normed, inverse, gain)
        return gain_sum, shift_sum

    def last_back(half, sums):
        rows = pl.ds(aligned(half * HALF, 16), HALF)
        made = mm_nt(DMB[rows, :], win[last, :, D : 2 * D])
        made = made + mm_nt(DA[rows, :], win[last, :, 2 * D : 3 * D])
        return first_back(last, half, made, sums)

    gain_sum, shift_sum = lax.fori_loop(0, 2, last_back, (gain_sum, shift_sum))
    store_sums(last, [(0, gain_sum), (D, shift_sum)])
    reduce_y(CHUNKS)
    factors_x()

    def mlp_back(layer, half, sums):
        base = half * HALF
        whole = pl.ds(aligned(base, 16), HALF)
        bias_down, bias_up, gain_sum, shift_sum, bias_out = sums
        for at, size in pieces(HALF):
            rows = pl.ds(aligned(base + at, 16), size)
            up = X[rows, :]
            DXB[rows, :] = up.astype(BF)
            bias_down = bias_down + fold(up)
        low = DXB[whole, :]
        ups = []
        for tile in range(4):
            columns = slice(tile * D, (tile + 1) * D)
            made = mm_nt(low, wdn[layer, columns, :])
            total = bias_up[tile]
            for at, size in pieces(HALF):
                rows = pl.ds(aligned(base + at, 16), size)
                grad = (made[at : at + size] * SLOPE[layer, rows, columns].astype(F32)).astype(BF)
                SLOPE[layer, rows, columns] = grad
                total = total + fold(grad.astype(F32))
            ups.append(total)
        made = mm_nt(SLOPE[layer, whole, :], win[layer, :, 4 * D :])
        gain = vector(layer, 5 * D, D)
        for at, size in pieces(HALF):
            rows = pl.ds(aligned(base + at, 16), size)
            part = made[at : at + size]
            normed = N2[layer, rows, :].astype(F32)
            inverse = I2[layer, rows, :][:, 0:1]
            gain_sum = gain_sum + fold(part * normed)
            shift_sum = shift_sum + fold(part)
            grad = X[rows, :] + norm_back(part, normed, inverse, gain)
            X[rows, :] = grad
            DMB[rows, :] = grad.astype(BF)
            bias_out = bias_out + fold(grad)
        DA[whole, :] = mm_nt(DMB[whole, :], win[layer, :, 3 * D : 4 * D]).astype(BF)
        return bias_down, tuple(ups), gain_sum, shift_sum, bias_out

    def attend_back(layer, image):
        rows = pl.ds(aligned(image * BLK, 16), BLK)
        for pair in range(3):
            at = pair * 128
            query = QKV[layer, rows, at : at + 128] * BF(0.125)
            keys = QKV[layer, rows, D + at : D + at + 128]
            values = QKV[layer, rows, 2 * D + at : 2 * D + at + 128]
            ups = DA[rows, at : at + 128]
            keys_both = jnp.concatenate([keys * even, keys * odd], axis=0)
            values_both = jnp.concatenate([values * even, values * odd], axis=0)
            scores = mm_nt(keys_both, query).reshape(2, BLK, BLK) + key_column[None]
            raw = jnp.exp(scores - jnp.max(scores, axis=1, keepdims=True))
            probs = raw * (1.0 / jnp.sum(raw, axis=1, keepdims=True))
            d_probs = mm_nt(values_both, ups).reshape(2, BLK, BLK)
            inner = jnp.sum(d_probs * probs, axis=1, keepdims=True)
            d_scores = (probs * (d_probs - inner)).astype(BF).reshape(2 * BLK, BLK)
            probs = probs.astype(BF).reshape(2 * BLK, BLK)
            d_values = mm(probs, ups)
            d_keys = mm(d_scores, query)
            d_query = mm_tn(d_scores, keys_both) * 0.125
            QKV[layer, rows, at : at + 128] = d_query.astype(BF)
            QKV[layer, rows, D + at : D + at + 128] = jnp.where(
                low_lane, d_keys[:BLK], d_keys[BLK:]
            ).astype(BF)
            QKV[layer, rows, 2 * D + at : 2 * D + at + 128] = jnp.where(
                low_lane, d_values[:BLK], d_values[BLK:]
            ).astype(BF)

    def renew(ref, layer, at):
        gain, shift = vector(layer, at, D), vector(layer, at + D, D)

        def one(index, nothing):
            rows = pl.ds(aligned(index * 64, 16), 64)
            DXB[rows, :] = (ref[layer, rows, :].astype(F32) * gain + shift).astype(BF)
            return nothing

        lax.fori_loop(0, ROWS // 64, one, 0)
        return DXB[...].T

    def keep_in(k, tile, made):
        for shard in range(n_shard):
            G[k, shard // 2, shard % 2, tile * rows_in : (tile + 1) * rows_in, :] = made[
                shard * rows_in : (shard + 1) * rows_in
            ]

    def backward(step, carry):
        layer = LAYERS - 2 - step
        kd, ku, kq = 3 * step, 3 * step + 1, 3 * step + 2
        upper_layer, bottom = step == 0, step == 1

        def one(half, sums):
            sums = mlp_back(layer, half, sums)
            begin = half == 0

            @pl.when(jnp.logical_and(upper_layer, begin))
            def _():
                factors_z()

            @pl.when(jnp.logical_and(bottom, begin))
            def _():
                reduce_x(2)
                gather_x(1)

            return sums

        bias_down, bias_up, gain_sum, shift_sum, bias_out = lax.fori_loop(
            0, 2, one, (zeros, (zeros,) * 4, zeros, zeros, zeros)
        )
        when(upper_layer, (reduce_x, CHUNKS))
        when(bottom, (reduce_z, 2), (gather_done, 0))
        store_sums(
            layer,
            [(7 * D + FF, bias_down), (5 * D, gain_sum), (6 * D, shift_sum), (4 * D, bias_out)]
            + [(7 * D + tile * D, bias_up[tile]) for tile in range(4)],
        )
        turned = DXB[...].T
        per = min(rows_down, D)
        for tile in range(4):
            columns = slice(tile * D, (tile + 1) * D)
            made = mm(turned, ACT[layer, :, columns]).astype(BF).T
            for piece in range(D // per):
                shard, at = divmod(tile * D + piece * per, rows_down)
                G[kd, shard // 2, shard % 2, at : at + per, :] = made[
                    piece * per : (piece + 1) * per
                ]
        when(upper_layer, (reduce_core, 0))
        when(bottom, (reduce_core, 3), (gather_z, 2))
        turned = renew(N2, layer, 5 * D)
        for tile in range(4):
            keep_in(
                ku, tile, mm(turned, SLOPE[layer, :, tile * D : (tile + 1) * D]).astype(BF)
            )
        when(upper_layer, (reduce_core, 1), (reduce_y, 0), (reduce_z, CHUNKS))
        when(bottom, (reduce_core, 4), (reduce_y, 3), (gather_x, 2), (gather_done, 1))
        keep_in(kq, 3, mm(ATT[layer].T, DMB[...]).astype(BF))

        def two(image, nothing):
            attend_back(layer, image)
            first = jnp.logical_and(upper_layer, image == 0)
            when(first, (gather_z, CHUNKS))

            @pl.when(first)
            def _():
                factors_mate()

            when(jnp.logical_and(upper_layer, image == 1), (reduce_y, 1), (reduce_x, 0))
            when(jnp.logical_and(upper_layer, image == 2), (reduce_z, 0), (gather_x, CHUNKS))
            when(jnp.logical_and(upper_layer, image == 3), (reduce_x, 1), (gather_done, CHUNKS))
            when(jnp.logical_and(bottom, image == 0), (reduce_x, 3))
            when(jnp.logical_and(bottom, image == 1), (reduce_y, 4), (gather_done, 2))
            when(jnp.logical_and(bottom, image == 2), (reduce_z, 3), (reduce_x, 4))
            when(jnp.logical_and(bottom, image == 3), (gather_z, 3), (reduce_z, 4))
            return nothing

        lax.fori_loop(0, KEPT, two, 0)
        turned = renew(N1, layer, 0)
        for tile in range(3):
            keep_in(
                kq, tile, mm(turned, QKV[layer, :, tile * D : (tile + 1) * D]).astype(BF)
            )
        when(upper_layer, (reduce_core, 2), (gather_z, 0), (reduce_z, 1))
        when(bottom, (reduce_core, 5), (gather_x, 3), (gather_z, 4))
        store_sums(
            layer,
            [
                (2 * D, fold(QKV[layer, :, 0:D].astype(F32))),
                (3 * D, fold(QKV[layer, :, 2 * D : 3 * D].astype(F32))),
            ],
        )

        def three(half, sums):
            rows = pl.ds(aligned(half * HALF, 16), HALF)
            made = mm_nt(QKV[layer, rows, :], win[layer, :, 0 : 3 * D])
            return first_back(layer, half, made, sums)

        gain_sum, shift_sum = lax.fori_loop(0, 2, three, (zeros, zeros))
        store_sums(layer, [(0, gain_sum), (D, shift_sum)])
        when(upper_layer, (reduce_y, 2), (gather_x, 0), (gather_z, 1))
        when(bottom, (reduce_y, 5), (gather_done, 3), (gather_x, 4))
        return carry

    lax.fori_loop(0, LAYERS - 1, backward, 0)
    factors_done()

    for at, size in pieces(BLK):
        total = None
        for image in range(KEPT):
            part = X[image * BLK + at : image * BLK + at + size, :]
            DXB[image * BLK + at : image * BLK + at + size, :] = part.astype(BF)
            total = part if total is None else total + part
        V[at : at + size, 0:D] = total

    vec = ("v", v_send, v_recv)
    v_y, v_x = 1, n_y
    v_z = v_x + n_x - 1
    v_gz = v_z + n_z - 1
    v_q = v_gz + n_z - 1
    v_gx = v_q + n_z - 1
    v_gy = v_gx + n_x - 1
    v_gc = v_gy + n_y - 1
    rows_c = VEC_ROWS // 2
    rows_y = rows_c // n_y
    rows_x = rows_y // n_x
    split_z = cut(rows_x, n_z, 8)
    rows_z = rows_x // split_z
    at_c = c * rows_c
    at_y = at_c + y * rows_y
    at_x = at_y + x * rows_x
    at_z = at_x + z * rows_z if split_z > 1 else at_x

    def vrows(ref, at, rows):
        return ref.at[pl.ds(aligned(at, 8), rows), :]

    def narrow(at, rows):
        return VF.at[pl.ds(aligned(at, 8), rows), pl.ds(0, D)]

    def vadd(at, rows, sources):
        target = pl.ds(aligned(at, 8), rows)
        total = V[target, :]
        for source in sources:
            total = total + source
        V[target, :] = total

    def vectors_core():
        go(lambda: vrows(V, (1 - c) * rows_c, rows_c), VC, vec, 0, mate)

    def vectors_y():
        arrived(VC, v_recv.at[0], v_send.at[0])
        vadd(at_c, rows_c, [VC[...]])
        for o in range(1, n_y):
            to = turn(y, o, n_y)
            go(
                lambda o=o: vrows(V, at_c + turn(y, o, n_y) * rows_y, rows_y), VY.at[o - 1],
                vec, v_y + o - 1, here.to(y=to),
            )

    def vectors_x():
        for o in range(1, n_y):
            arrived(VY.at[o - 1], v_recv.at[v_y + o - 1], v_send.at[v_y + o - 1])
        vadd(at_y, rows_y, [VY[o - 1] for o in range(1, n_y)])
        for o in range(1, n_x):
            to = turn(x, o, n_x)
            go(
                lambda o=o: vrows(V, at_y + turn(x, o, n_x) * rows_x, rows_x), VX.at[o - 1],
                vec, v_x + o - 1, here.to(x=to),
            )

    def vectors_z():
        for o in range(1, n_x):
            arrived(VX.at[o - 1], v_recv.at[v_x + o - 1], v_send.at[v_x + o - 1])
        vadd(at_x, rows_x, [VX[o - 1] for o in range(1, n_x)])
        for o in range(1, n_z):

            def make(o=o):
                at = at_x + turn(z, o, n_z) * rows_z if split_z > 1 else at_x
                return vrows(V, at, rows_z)

            go(make, VZ.at[z], vec, v_z + o - 1, here.to(z=turn(z, o, n_z)))

    def vectors_gather_z():
        for o in range(1, n_z):
            arrived(
                VZ.at[turn(z, n_z - o, n_z)], v_recv.at[v_z + o - 1], v_send.at[v_z + o - 1]
            )
        target = pl.ds(aligned(at_z, 8), rows_z)
        VZ[z] = V[target, :]
        total = VZ[0]
        for index in range(1, n_z):
            total = total + VZ[index]
        VF[target, 0:D] = total[:, 0:D]
        if split_z > 1:
            for o in range(1, n_z):
                go(
                    lambda: narrow(at_z, rows_z), narrow(at_z, rows_z), vec, v_gz + o - 1,
                    here.to(z=turn(z, o, n_z)),
                )

    def squares_send():
        SQ[...] = square_sum[...]
        SQS[z] = square_sum[...]
        for o in range(1, n_z):
            go(lambda: SQ, SQS.at[z], vec, v_q + o - 1, here.to(z=turn(z, o, n_z)))

    def vectors_gather_x():
        for o in range(1, n_z):
            came = turn(z, n_z - o, n_z)
            if split_z > 1:
                arrived(
                    narrow(at_x + came * rows_z, rows_z), v_recv.at[v_gz + o - 1],
                    v_send.at[v_gz + o - 1],
                )
            arrived(SQS.at[came], v_recv.at[v_q + o - 1], v_send.at[v_q + o - 1])
        total = SQS[0]
        for index in range(1, n_z):
            total = total + SQS[index]
        for at in range(0, rows_x, 8):
            VF[pl.ds(aligned(at_x + at, 8), 8), D:] = total
        for o in range(1, n_x):
            go(
                lambda: vrows(VF, at_x, rows_x), vrows(VF, at_x, rows_x), vec, v_gx + o - 1,
                here.to(x=turn(x, o, n_x)),
            )

    def vectors_gather_y():
        for o in range(1, n_x):
            at = at_y + turn(x, n_x - o, n_x) * rows_x
            arrived(vrows(VF, at, rows_x), v_recv.at[v_gx + o - 1], v_send.at[v_gx + o - 1])
        for o in range(1, n_y):
            go(
                lambda: vrows(VF, at_y, rows_y), vrows(VF, at_y, rows_y), vec, v_gy + o - 1,
                here.to(y=turn(y, o, n_y)),
            )

    def vectors_gather_core():
        for o in range(1, n_y):
            at = at_c + turn(y, n_y - o, n_y) * rows_y
            arrived(vrows(VF, at, rows_y), v_recv.at[v_gy + o - 1], v_send.at[v_gy + o - 1])
        go(lambda: vrows(VF, at_c, rows_c), vrows(VF, at_c, rows_c), vec, v_gc, mate)

    def vectors_done():
        arrived(vrows(VF, (1 - c) * rows_c, rows_c), v_recv.at[v_gc], v_send.at[v_gc])

    vectors_core()
    low = DXB[...]
    for tile in range(2):
        made = mm_tn(pix[:, :, tile * D : (tile + 1) * D].reshape(ROWS, D), low).astype(BF)
        for piece in range(D // rows_patch):
            shard = tile * (D // rows_patch) + piece
            GS[1, shard // 2, shard % 2] = made[piece * rows_patch : (piece + 1) * rows_patch]

    kp = CHUNKS + 1
    reduce_core(kp)
    reduce_x(5)
    vectors_y()
    gather_done(4)
    reduce_y(kp)
    reduce_z(5)
    vectors_x()
    reduce_x(kp)
    gather_z(5)
    vectors_z()
    reduce_z(kp)
    vectors_gather_z()
    gather_x(5)
    gather_z(kp)
    squares_send()
    gather_x(kp)
    vectors_gather_x()
    gather_done(5)
    gather_done(kp)
    vectors_gather_y()
    vectors_gather_core()
    vectors_done()
    last_copy = pltpu.make_async_copy(VF, vec_out, out_local.at[1 + CHUNKS + 2])
    last_copy.start()
    for source, send, recv, at in list(sent.values()):
        left_here(source(), recv.at[at], send.at[at])
    for k in range(CHUNKS + 2):
        result(k).wait()
    last_copy.wait()

    @pl.when(jnp.logical_not(lower))
    def _():
        left_here(given, img_recv.at[0], img_send.at[0])
        left_here(lab_pairs.at[2], img_recv.at[1], img_send.at[1])


def run_train(n_rep, n_shard, patches, lab_pairs, own_patch, own_in, own_down, vecs, glob, pos, head, count):
    n_x = 2 ** ((n_rep.bit_length() - 2) // 2)
    n_z, n_y = n_rep // n_x, n_shard // 2
    block = 4 * (D // n_shard)
    group = KEPT * n_shard
    keep = LAYERS - 1
    units = 1 + 3 * LAYERS
    chunks = CHUNKS + 2

    def buf(*shape, dtype=BF):
        return pltpu.VMEM(shape, dtype)

    def sems(*shape):
        return pltpu.SemaphoreType.DMA(shape)

    def reduction(count, rows):
        by_x = cut(rows, n_x, 16)
        by_z = cut(rows // by_x, n_z, 16)
        return [
            buf(count, n_y, 2, rows, D),
            buf(min(count, 3), n_y, rows, D),
            buf(min(count, 3), n_y - 1, rows, D),
            buf(count, n_x - 1 if by_x > 1 else n_x, rows // by_x, D),
            buf(count, n_z, rows // by_x // by_z, D),
            buf(count, rows, D),
        ]

    rows_y = VEC_ROWS // 2 // n_y
    rows_x = rows_y // n_x
    rows_z = rows_x // cut(rows_x, n_z, 8)
    ag_count = n_y + (n_y - 1) * (n_x - 1) * 2 + n_y - 1
    rs_count = 1 + (n_y - 1) + 2 * (n_x - 1) + 2 * (n_z - 1)
    f_count = 1 + (n_y - 1) + (n_x - 1) + (n_z - 1) + 1
    v_count = 1 + 2 * (n_y - 1) + 2 * (n_x - 1) + 3 * (n_z - 1) + 1
    whole = pl.BlockSpec(memory_space=pltpu.VMEM)
    there = pl.BlockSpec(memory_space=pl.ANY)
    return pl.pallas_call(
        functools.partial(train, n_rep, n_shard),
        out_shape=[
            jax.ShapeDtypeStruct((CHUNKS, block, D), BF),
            jax.ShapeDtypeStruct((2, block // 2, D), BF),
            jax.ShapeDtypeStruct((VEC_ROWS, VEC_WIDE), F32),
            jax.ShapeDtypeStruct((2, n_rep, group, WFAC), BF),
        ],
        in_specs=[there] * 5 + [whole] * 5,
        out_specs=[there] * 4,
        scratch_shapes=[
            buf(ROWS, D, dtype=F32),
            buf(LAYERS, ROWS, D),
            buf(LAYERS, ROWS, 128, dtype=F32),
            buf(keep, ROWS, 3 * D),
            buf(keep, ROWS, D),
            buf(keep, ROWS, D),
            buf(keep, ROWS, 128, dtype=F32),
            buf(keep, ROWS, FF),
            buf(keep, ROWS, FF),
            buf(ROWS, D),
            buf(ROWS, D),
            buf(ROWS, D),
            buf(KEPT, BLK, PATCH_DIM),
            buf(2, 32, 128, dtype=F32),
            buf(PATCH_DIM, D),
            buf(LAYERS, D, 4 * D + FF),
            buf(LAYERS, FF, D),
            buf(D, CPAD),
            buf(1, CPAD, dtype=F32),
            *reduction(CHUNKS, block),
            *reduction(2, block // 2),
            buf(2, group, WFAC),
            buf(group, WFAC),
            buf(n_y - 1, group, WFAC),
            buf(n_x, group, WFAC),
            buf(VEC_ROWS, VEC_WIDE, dtype=F32),
            buf(VEC_ROWS // 2, VEC_WIDE, dtype=F32),
            buf(n_y - 1, rows_y, VEC_WIDE, dtype=F32),
            buf(n_x - 1, rows_x, VEC_WIDE, dtype=F32),
            buf(n_z, rows_z, VEC_WIDE, dtype=F32),
            buf(VEC_ROWS, VEC_WIDE, dtype=F32),
            buf(8, 128, dtype=F32),
            buf(n_z, 8, 128, dtype=F32),
            buf(8, 128, dtype=F32),
            sems(units, ag_count),
            sems(units, ag_count),
            sems(units),
            sems(chunks, rs_count),
            sems(chunks, rs_count),
            sems(f_count),
            sems(f_count),
            sems(v_count),
            sems(v_count),
            sems(2),
            sems(2),
            sems(4),
            sems(2 + chunks),
        ],
        compiler_params=pltpu.CompilerParams(
            vmem_limit_bytes=65400 * 1024, collective_id=0, has_side_effects=True
        ),
        cost_estimate=pl.CostEstimate(
            flops=24_000_000_000, bytes_accessed=30_000_000, transcendentals=10_000_000
        ),
        name="train_step",
    )(patches, lab_pairs, own_patch, own_in, own_down, vecs, glob, pos, head, count)


def adam(weight, first, second, grad, factor, rate):
    grad = grad * factor
    first = BETA_FIRST * first + (1.0 - BETA_FIRST) * grad
    second = BETA_SECOND * second + (1.0 - BETA_SECOND) * grad * grad
    first_hat = first * (1.0 / (1.0 - BETA_FIRST**ADAM_STEP))
    second_hat = second * (1.0 / (1.0 - BETA_SECOND**ADAM_STEP))
    step = first_hat / (jnp.sqrt(second_hat) + ADAM_EPS) + WEIGHT_DECAY * weight
    return weight - rate * step, first, second


def update(n_rep, n_shard, *refs):
    res, small, vec, factors = refs[0:4]
    sources = refs[4:25]
    loss_out, norm_out = refs[25:27]
    targets = refs[27:48]
    buffers = refs[48:69]
    last_in, last_down, grad_head, in_sems, out_sems = refs[69:]
    shard = lax.axis_index("shard")
    rows_in = D // n_shard
    rows_down = FF // n_shard
    keep = LAYERS - 1

    def moves(array, layer=None, out=False):
        found = []
        for kind in range(3):
            index = 3 * array + kind
            if out:
                src, dst, sem = buffers[index], targets[index], out_sems
            else:
                src, dst, sem = sources[index], buffers[index], in_sems
            slot = 0 if layer is None else layer
            if layer is not None:
                src, dst = src.at[layer], dst.at[layer]
            found.append(pltpu.make_async_copy(src, dst, sem.at[index, slot]))
        return found

    layered = [(1, layer) for layer in range(LAYERS)] + [(2, layer) for layer in range(LAYERS)]
    order = layered + [(0, None), (6, None), (5, None), (3, None), (4, None)]
    for array, layer in order:
        for move in moves(array, layer):
            move.start()

    n_rows = factors.shape[1] * factors.shape[2]

    def factor(half, at, size):
        return factors[half, :, :, at : at + size].reshape(n_rows, size)

    def squares(values):
        return fold(values * values)

    total = jnp.zeros((8, D), F32)
    h2 = factor(0, FF, D)
    for tile in range(4):
        made = mm_tn(h2, factor(1, tile * D, D))
        last_in[:, (2 + tile) * D : (3 + tile) * D] = made
        total = total + squares(made)
    made = mm_tn(factor(0, FF + 2 * D, D), factor(1, FF + D, D))
    last_in[:, 0:D] = made
    total = total + squares(made)
    made = mm_tn(factor(0, FF + D, D), factor(1, FF, D))
    last_in[:, D : 2 * D] = made
    total = total + squares(made)
    d_top = factor(0, FF + 4 * D, D)
    for tile in range(4):
        made = mm_tn(factor(0, tile * D, D), d_top)
        last_down[tile * D : (tile + 1) * D, :] = made
        total = total + squares(made)
    final = factor(0, FF + 3 * D, D)
    wide = jnp.zeros((8, 128), F32)
    for at in range(0, CPAD, 512):
        d_logits = factor(1, FF + 2 * D + at, 512)
        made = mm_tn(final, d_logits)
        grad_head[0:D, at : at + 512] = made
        bias = down_sum(d_logits.astype(F32))
        grad_head[D : D + 1, at : at + 512] = bias
        sums = squares(made)
        for lane in range(0, 512, 128):
            wide = wide + sums[:, lane : lane + 128]
            row = bias[:, lane : lane + 128]
            wide = wide + (row * row) * 0.125
    for lane in range(0, D, 128):
        wide = wide + total[:, lane : lane + 128]
    used = VEC_AT + 12 * LAYERS + 2
    parts = jnp.zeros((8, D), F32)
    kept_rows = lax.broadcasted_iota(jnp.int32, (8, 1), 0)
    for at in range(0, used, 8):
        value = vec[at : at + 8, 0:D]
        if at + 8 > used:
            value = jnp.where(kept_rows + at < used, value, 0.0)
        parts = parts + value * value
    patch_bias = down_sum(vec[0:PATCHES, 0:D])
    class_row = vec[CLS : CLS + 1, 0:D]
    rest = (patch_bias * patch_bias + class_row * class_row) * 0.125
    parts = parts + rest
    for lane in range(0, D, 128):
        wide = wide + parts[:, lane : lane + 128]
    n_x = 2 ** ((n_rep.bit_length() - 2) // 2)
    rows_x = VEC_ROWS // n_shard // n_x
    wide = wide + fold(vec[:, D:]) * (8.0 / rows_x)
    sum_squares = jnp.sum(jnp.sum(wide, axis=1, keepdims=True), axis=0, keepdims=True)
    inv_count = 1.0 / vec[used + 1 : used + 2, 0:1]
    grad_norm = jnp.sqrt(sum_squares) * inv_count
    norm_out[...] = grad_norm
    loss_out[...] = vec[used : used + 1, 0:1] * inv_count
    scale = jnp.minimum(1.0, CLIP_NORM / grad_norm) * inv_count

    def apply(array, where, grad, rate):
        refs = [buffers[3 * array + kind] for kind in range(3)]
        made = adam(refs[0][where], refs[1][where], refs[2][where], grad, scale, rate)
        for ref, value in zip(refs, made):
            ref[where] = value

    def begin(array, layer=None):
        for move in moves(array, layer):
            move.wait()

    def finish(array, layer=None):
        for move in moves(array, layer, out=True):
            move.start()

    def in_place(layer, column, at, size):
        return (layer, slice(at, at + size), slice(column * D, (column + 1) * D))

    def in_step(tile_rows):
        return 32 if tile_rows % 32 == 0 else 16

    step = in_step(rows_in)
    own_rows = pl.multiple_of(shard * rows_in, 8)
    for layer in range(LAYERS):
        begin(1, layer)
        for column in range(8):
            for at in range(0, rows_in, step):
                if layer < keep:
                    k = 3 * (keep - 1 - layer) + (2 if column < 4 else 1)
                    row = (column % 4) * rows_in + at
                    grad = res[k, row : row + step, :].astype(F32)
                elif column in (1, 2):
                    row = (column - 1) * rows_in + at
                    grad = small[0, row : row + step, :].astype(F32)
                else:
                    held = 0 if column == 0 else column - 2
                    grad = last_in[
                        pl.ds(own_rows + at, step), held * D : (held + 1) * D
                    ]
                apply(1, in_place(layer, column, at, step), grad, LEARNING_RATE)
        finish(1, layer)
    down_rows = pl.multiple_of(shard * rows_down, 8)
    for layer in range(LAYERS):
        begin(2, layer)
        for at in range(0, rows_down, 32):
            if layer < keep:
                grad = res[3 * (keep - 1 - layer), at : at + 32, :].astype(F32)
            else:
                grad = last_down[pl.ds(down_rows + at, 32), :]
            apply(2, (layer, slice(at, at + 32), slice(0, D)), grad, LEARNING_RATE)
        finish(2, layer)
    begin(0)
    for at in range(0, PATCH_DIM // n_shard, 32):
        grad = small[1, at : at + 32, :].astype(F32)
        apply(0, (slice(at, at + 32), slice(0, D)), grad, LEARNING_RATE)
    finish(0)
    begin(6)
    for at in range(0, D, 32):
        rows = slice(at, at + 32)
        apply(6, (rows, slice(0, NCLS)), grad_head[rows, 0:NCLS], LEARNING_RATE)
    apply(6, (slice(D, D + 1), slice(0, NCLS)), grad_head[D : D + 1, 0:NCLS], LEARNING_RATE)
    finish(6)
    begin(5)
    apply(5, (slice(0, 1), slice(0, D)), class_row, VECTOR_RATE)
    for at in range(0, PATCHES, 28):
        apply(
            5, (slice(1 + at, 29 + at), slice(0, D)), vec[at : at + 28, 0:D], VECTOR_RATE
        )
    finish(5)
    begin(3)
    for layer in range(LAYERS):
        for piece in range(12):
            row = VEC_AT + 12 * layer + piece
            where = (slice(layer, layer + 1), slice(piece * D, (piece + 1) * D))
            apply(3, where, vec[row : row + 1, 0:D], VECTOR_RATE)
    finish(3)
    begin(4)
    rows = [patch_bias, class_row, vec[used - 2 : used - 1, 0:D], vec[used - 1 : used, 0:D]]
    for index, row in enumerate(rows):
        apply(4, (slice(index, index + 1), slice(0, D)), row, VECTOR_RATE)
    finish(4)
    for array, layer in order:
        for move in moves(array, layer, out=True):
            move.wait()


def run_update(n_rep, n_shard, res, small, vec, factors, arrays):
    whole = pl.BlockSpec(memory_space=pltpu.VMEM)
    there = pl.BlockSpec(memory_space=pl.ANY)
    one = jax.ShapeDtypeStruct((1, 1), F32)
    made = pl.pallas_call(
        functools.partial(update, n_rep, n_shard),
        out_shape=[one, one] + [jax.ShapeDtypeStruct(a.shape, F32) for a in arrays],
        in_specs=[whole] * 4 + [there] * 21,
        out_specs=[whole] * 2 + [there] * 21,
        scratch_shapes=[pltpu.VMEM(a.shape, F32) for a in arrays]
        + [
            pltpu.VMEM((D, 2 * D + FF), F32),
            pltpu.VMEM((FF, D), F32),
            pltpu.VMEM((D + 8, CPAD), F32),
            pltpu.SemaphoreType.DMA((21, LAYERS)),
            pltpu.SemaphoreType.DMA((21, LAYERS)),
        ],
        compiler_params=pltpu.CompilerParams(vmem_limit_bytes=62 * 1024 * 1024),
        cost_estimate=pl.CostEstimate(
            flops=200_000_000, bytes_accessed=50_000_000, transcendentals=4_000_000
        ),
        name="adamw",
    )(res, small, vec, factors, *arrays)
    return made[0].reshape(()), made[1].reshape(()), made[2:]


def shards(
    n_rep, n_shard,
    patches, labels, counts, patch_w, layer_in, layer_down, layer_vecs, glob_vecs, pos_embed, head,
    m_patch, v_patch, m_in, v_in, m_down, v_down, m_vecs, v_vecs, m_glob, v_glob, m_pos, v_pos,
    m_head, v_head,
):
    slots = patches.shape[0]
    marked = jnp.where(jnp.arange(slots) < counts[0], labels, -1).astype(F32)
    lab_pairs = jnp.where(
        jnp.arange(16)[None, :, None] == CLS - TAIL, marked[:, None, None], -1.0
    )
    lab_pairs = jnp.broadcast_to(lab_pairs, (slots, 16, 128)).reshape(slots // 2, 32, 128)
    count = jnp.broadcast_to(counts.astype(F32)[None], (1, 128))
    padded = jnp.pad(patches, ((0, 0), (0, BLK - PATCHES), (0, 0)))
    res, small, vec, factors = run_train(
        n_rep, n_shard, padded, lab_pairs, patch_w.astype(BF), layer_in.astype(BF),
        layer_down.astype(BF), layer_vecs, glob_vecs, pos_embed, head, count,
    )
    arrays = [
        patch_w, m_patch, v_patch, layer_in, m_in, v_in, layer_down, m_down, v_down,
        layer_vecs, m_vecs, v_vecs, glob_vecs, m_glob, v_glob, pos_embed, m_pos, v_pos,
        head, m_head, v_head,
    ]
    loss, grad_norm, new = run_update(n_rep, n_shard, res, small, vec, factors, arrays)
    return (loss, grad_norm, *new)


def solution(mesh):
    everywhere = P()
    rows = P("shard", None)
    middle = P(None, "shard", None)
    return jax.shard_map(
        functools.partial(shards, mesh.shape["rep"], mesh.shape["shard"]),
        mesh=mesh,
        in_specs=(
            P(("rep", "shard"), None, None),
            P(("rep", "shard")),
            P(("rep", "shard")),
            rows,
            middle,
            middle,
            *(everywhere,) * 4,
            *(rows,) * 2,
            *(middle,) * 4,
            *(everywhere,) * 8,
        ),
        out_specs=(
            *(everywhere,) * 2,
            *(rows,) * 3,
            *(middle,) * 6,
            *(everywhere,) * 12,
        ),
        check_vma=False,
    )
```

time: 875 us -> 249 us (0.28); the launches traced: 859 us -> 248 us
  waiting for transfers between devices: 360 us -> 0 us
  other arithmetic: 180 us -> 8.38 us
  Pallas kernels: 85.5 us -> 235 us
  blocking collectives: 145 us -> 0 us
  local copies, waits for them, and re-layouts: 57.2 us -> 2.94 us
  between operations: 24.1 us -> 1.5 us
    psum x2 -> x0, waiting for transfers between devices: 270 us -> none  [the longest x1 154 us: shards(): mine = lax.psum(mine, 'rep').reshape(-1).astype(F32)]
    pallas_call x1 -> x2, Pallas kernels: 85.5 us -> 235 us  [the longest x1 214 us: run_train(): pl.pallas_call(functools.partial(train, n_rep, n_shard), out_shape=[jax.S...]
    concatenate x1 -> x0, other arithmetic: 97.9 us -> none  [shards(): jnp.concatenate([gin.reshape(keep, n_shard, own_in, 4 * D + FF).swapaxes(...]
    all_gather x3 -> x0, blocking collectives: 97 us -> none  [the longest x1 44.8 us: shards(): right = lax.all_gather(right[picked], ('rep', 'shard'), axis=0, tiled=True)]
    psum x2 -> x0, blocking collectives: 48.3 us -> none  [the longest x1 40.9 us: shards(): lax.psum((gvec.reshape(LAYERS, WIDE), gfin[0], gpos, counts.astype(F32)),...]
    all_gather x2 -> x0, waiting for transfers between devices: 48.2 us -> none  [the longest x1 48.2 us: shards(): win = lax.all_gather(layer_in.astype(BF), 'shard', axis=1, tiled=True)]
    unnamed x6 -> x0, waiting for transfers between devices: 33.5 us -> none
    unnamed x97 -> x2, local copies, waits for them, and re-layouts: 28.2 us -> 0.01 us
  transfers between devices with their start and end apart: 7 -> 0, of which waited for: 5 -> 0; matrix products, arithmetic and copies ran while one was open for 5% -> 0% of each run, Pallas kernels for 0% -> 0%
where the time goes in v2:
time: 249 us; the launch traced here: 248 us
  Pallas kernels  235 us (94%)
  other arithmetic  8.38 us (3%)
  local copies, waits for them, and re-layouts  2.94 us (1%)
    pallas_call x1, Pallas kernels, run_train(): pl.pallas_call(functools.partial(train, n_rep, n_shard), out_shape=[jax.S...  214 us
    pallas_call x1, Pallas kernels, run_update(): pl.pallas_call(functools.partial(update, n_rep, n_shard), out_shape=[one,...  20.8 us

profile of v2, /device:TPU:0, one launch (start us, length us, event | category | flops | bytes accessed | tf_op | source)
XLA Modules:
  0.0 247.7 jit_solution(965941051814196672)
XLA Ops:
  1.3 0.5 broadcast_in_dim.54.count
  1.8 0.7 fusion
  2.5 0.1 broadcast_in_dim.46
  2.6 0.1 broadcast_in_dim.48
  2.7 0.1 broadcast_in_dim.49
  2.7 0.1 broadcast_in_dim.50
  2.8 0.7 broadcast_in_dim.52.lab_pairs
  3.5 1.6 convert_element_type.18.own_patch
  5.2 2.5 %convert_element_type.20.own_down = bf16[3,384,384]{2,1,0:T(8,128)(2,1)} convert(f32[3,384,384]{2,1,0:T(8,128)} %refs_10_.1) | non-fusion elementwise | flops 442368 | bytes 2654208 | tf_op jit(solution)/shard_map/convert_element_type | solution.py:1617
  7.7 0.0 copy-start
  7.7 3.6 %convert_element_type.19.own_in = bf16[3,96,3072]{2,1,0:T(8,128)(2,1)} convert(f32[3,96,3072]{2,1,0:T(8,128)} %refs_7_.1) | non-fusion elementwise | flops 884736 | bytes 5308416 | tf_op jit(solution)/shard_map/convert_element_type | solution.py:1616
  11.2 0.0 copy-done
  11.2 1.4 pad.4.patches
  12.6 214.1 %train_step.1 = (bf16[6,384,384]{2,1,0:T(8,128)(2,1)}, bf16[2,192,384]{2,1,0:T(8,128)(2,1)}, f32[256,512]{1,0:T(8,128)}, bf16[2,8,16,3456]{3,2,1,0:T(8,128)(2,1)}) custom-call(bf16[6,208,768]{2,1,0:T(8,128)(2,1)} %pad.4.patches, f32[3,32,128]{2,1,0:T(8,128)} %broadcast_in_dim.52.lab_pairs, bf16[192,384]{1,0:T(8,128)(2,1)} %convert_element_type.18.own_patch, ...), custom_call_target="tpu_custom_call" | custom-call | flops 24000000000 | bytes 30000000 | tf_op jit(solution)/shard_map/train_step/pallas_call | solution.py:1315
  226.7 20.8 %adamw.1 = (f32[1,1]{1,0:T(1,128)}, f32[1,1]{1,0:T(1,128)}, f32[192,384]{1,0:T(8,128)}, f32[192,384]{1,0:T(8,128)}, f32[192,384]{1,0:T(8,128)}, /*index=5*/f32[3...) custom-call(bf16[6,384,384]{2,1,0:T(8,128)(2,1)} %get-tuple-element., ...), custom_call_target="tpu_custom_call" | custom-call | flops 200000000 | bytes 50000000 | tf_op jit(solution)/shard_map/adamw/pallas_call | solution.py:1579
  (3 shorter events, 0.0 us)
Async XLA Ops:
  7.7 3.6 %copy-start = (bf16[6,196,768]{2,1,0:T(8,128)(2,1)S(1)}, bf16[6,196,768]{2,1,0:T(8,128)(2,1)}, u32[]{:S(2)}) copy-start(bf16[6,196,768]{2,1,0:T(8,128)(2,1)} %param.24) | copy-start | bytes 5419012

commit v3 on v2

--- a/solution.py
+++ b/solution.py
@@ -413,10 +413,14 @@
             keys = QKV[layer, rows, D + at : D + at + 128]
             values = QKV[layer, rows, 2 * D + at : 2 * D + at + 128]
             both = jnp.concatenate([query * even, query * odd], axis=0)
-            scores = mm_nt(both, keys) + key_row
-            top = jnp.max(scores, axis=-1, keepdims=True)
-            raw = jnp.exp(scores - top)
-            probs = (raw * (1.0 / jnp.sum(raw, axis=-1, keepdims=True))).astype(BF)
+            scores = mm_nt(both, keys)
+            probs = []
+            for row, size in pieces(HALF):
+                part = scores[row : row + size] + key_row
+                raw = jnp.exp(part - jnp.max(part, axis=-1, keepdims=True))
+                share = 1.0 / jnp.sum(raw, axis=-1, keepdims=True)
+                probs.append((raw * share).astype(BF))
+            probs = jnp.concatenate(probs, axis=0)
             made = mm(probs[:BLK], values * even) + mm(probs[BLK:], values * odd)
             ATT[layer, rows, at : at + 128] = made.astype(BF)
 
@@ -959,13 +963,29 @@
             ups = DA[rows, at : at + 128]
             keys_both = jnp.concatenate([keys * even, keys * odd], axis=0)
             values_both = jnp.concatenate([values * even, values * odd], axis=0)
-            scores = mm_nt(keys_both, query).reshape(2, BLK, BLK) + key_column[None]
-            raw = jnp.exp(scores - jnp.max(scores, axis=1, keepdims=True))
-            probs = raw * (1.0 / jnp.sum(raw, axis=1, keepdims=True))
-            d_probs = mm_nt(values_both, ups).reshape(2, BLK, BLK)
-            inner = jnp.sum(d_probs * probs, axis=1, keepdims=True)
-            d_scores = (probs * (d_probs - inner)).astype(BF).reshape(2 * BLK, BLK)
-            probs = probs.astype(BF).reshape(2 * BLK, BLK)
+            scores = mm_nt(keys_both, query)
+            d_probs = mm_nt(values_both, ups)
+            probs, d_scores = [], []
+            for base in (0, BLK):
+                low_probs, low_grads = [], []
+                for first, end in ((0, 128), (128, BLK)):
+                    part = jnp.concatenate(
+                        [
+                            scores[base : base + TAIL, first:end],
+                            scores[base + TAIL : base + BLK, first:end] + key_column[TAIL:],
+                        ],
+                        axis=0,
+                    )
+                    raw = jnp.exp(part - jnp.max(part, axis=0, keepdims=True))
+                    prob = raw * (1.0 / jnp.sum(raw, axis=0, keepdims=True))
+                    grad = d_probs[base : base + BLK, first:end]
+                    inner = jnp.sum(grad * prob, axis=0, keepdims=True)
+                    low_grads.append((prob * (grad - inner)).astype(BF))
+                    low_probs.append(prob.astype(BF))
+                probs.append(jnp.concatenate(low_probs, axis=1))
+                d_scores.append(jnp.concatenate(low_grads, axis=1))
+            probs = jnp.concatenate(probs, axis=0)
+            d_scores = jnp.concatenate(d_scores, axis=0)
             d_values = mm(probs, ups)
             d_keys = mm(d_scores, query)
             d_query = mm_tn(d_scores, keys_both) * 0.125
@@ -1007,18 +1027,14 @@
             def _():
                 factors_z()
 
-            @pl.when(jnp.logical_and(bottom, begin))
-            def _():
-                reduce_x(2)
-                gather_x(1)
-
+            when(jnp.logical_and(bottom, begin), (gather_z, CHUNKS))
             return sums
 
         bias_down, bias_up, gain_sum, shift_sum, bias_out = lax.fori_loop(
             0, 2, one, (zeros, (zeros,) * 4, zeros, zeros, zeros)
         )
         when(upper_layer, (reduce_x, CHUNKS))
-        when(bottom, (reduce_z, 2), (gather_done, 0))
+        when(bottom, (reduce_x, 2), (reduce_z, 1))
         store_sums(
             layer,
             [(7 * D + FF, bias_down), (5 * D, gain_sum), (6 * D, shift_sum), (4 * D, bias_out)]
@@ -1035,32 +1051,30 @@
                     piece * per : (piece + 1) * per
                 ]
         when(upper_layer, (reduce_core, 0))
-        when(bottom, (reduce_core, 3), (gather_z, 2))
+        when(bottom, (reduce_core, 3), (gather_z, 0), (gather_x, CHUNKS))
         turned = renew(N2, layer, 5 * D)
         for tile in range(4):
             keep_in(
                 ku, tile, mm(turned, SLOPE[layer, :, tile * D : (tile + 1) * D]).astype(BF)
             )
         when(upper_layer, (reduce_core, 1), (reduce_y, 0), (reduce_z, CHUNKS))
-        when(bottom, (reduce_core, 4), (reduce_y, 3), (gather_x, 2), (gather_done, 1))
+        when(bottom, (reduce_core, 4), (reduce_y, 3), (reduce_z, 2))
         keep_in(kq, 3, mm(ATT[layer].T, DMB[...]).astype(BF))
 
         def two(image, nothing):
             attend_back(layer, image)
-            first = jnp.logical_and(upper_layer, image == 0)
-            when(first, (gather_z, CHUNKS))
-
-            @pl.when(first)
+            when(jnp.logical_and(upper_layer, image == 0), (reduce_y, 1))
+            when(jnp.logical_and(upper_layer, image == 2), (reduce_x, 0))
+            when(jnp.logical_and(bottom, image == 0), (reduce_y, 4), (gather_z, 1))
+
+            @pl.when(jnp.logical_and(bottom, image == 1))
             def _():
                 factors_mate()
-
-            when(jnp.logical_and(upper_layer, image == 1), (reduce_y, 1), (reduce_x, 0))
-            when(jnp.logical_and(upper_layer, image == 2), (reduce_z, 0), (gather_x, CHUNKS))
-            when(jnp.logical_and(upper_layer, image == 3), (reduce_x, 1), (gather_done, CHUNKS))
-            when(jnp.logical_and(bottom, image == 0), (reduce_x, 3))
-            when(jnp.logical_and(bottom, image == 1), (reduce_y, 4), (gather_done, 2))
-            when(jnp.logical_and(bottom, image == 2), (reduce_z, 3), (reduce_x, 4))
-            when(jnp.logical_and(bottom, image == 3), (gather_z, 3), (reduce_z, 4))
+                gather_done(CHUNKS)
+                gather_x(0)
+
+            when(jnp.logical_and(bottom, image == 2), (reduce_x, 3), (gather_z, 2))
+            when(jnp.logical_and(bottom, image == 3), (gather_x, 1), (reduce_z, 3))
             return nothing
 
         lax.fori_loop(0, KEPT, two, 0)
@@ -1069,8 +1083,8 @@
             keep_in(
                 kq, tile, mm(turned, QKV[layer, :, tile * D : (tile + 1) * D]).astype(BF)
             )
-        when(upper_layer, (reduce_core, 2), (gather_z, 0), (reduce_z, 1))
-        when(bottom, (reduce_core, 5), (gather_x, 3), (gather_z, 4))
+        when(upper_layer, (reduce_core, 2))
+        when(bottom, (reduce_core, 5), (gather_x, 2), (gather_done, 0))
         store_sums(
             layer,
             [
@@ -1086,12 +1100,11 @@
 
         gain_sum, shift_sum = lax.fori_loop(0, 2, three, (zeros, zeros))
         store_sums(layer, [(0, gain_sum), (D, shift_sum)])
-        when(upper_layer, (reduce_y, 2), (gather_x, 0), (gather_z, 1))
-        when(bottom, (reduce_y, 5), (gather_done, 3), (gather_x, 4))
+        when(upper_layer, (reduce_x, 1), (reduce_y, 2), (reduce_z, 0))
+        when(bottom, (reduce_y, 5), (reduce_x, 4), (gather_z, 3), (gather_done, 1))
         return carry
 
     lax.fori_loop(0, LAYERS - 1, backward, 0)
-    factors_done()
 
     for at, size in pieces(BLK):
         total = None
@@ -1241,26 +1254,33 @@
 
     kp = CHUNKS + 1
     reduce_core(kp)
+    reduce_z(4)
+    vectors_y()
+    reduce_y(kp)
+    gather_x(3)
     reduce_x(5)
-    vectors_y()
-    gather_done(4)
-    reduce_y(kp)
+    vectors_x()
+    gather_z(4)
+    reduce_x(kp)
     reduce_z(5)
-    vectors_x()
-    reduce_x(kp)
+    vectors_z()
+    gather_done(2)
+    gather_x(4)
+    gather_done(3)
+    reduce_z(kp)
     gather_z(5)
-    vectors_z()
-    reduce_z(kp)
     vectors_gather_z()
-    gather_x(5)
     gather_z(kp)
     squares_send()
+    gather_x(5)
     gather_x(kp)
     vectors_gather_x()
+    gather_done(4)
+    vectors_gather_y()
     gather_done(5)
     gather_done(kp)
-    vectors_gather_y()
     vectors_gather_core()
+    factors_done()
     vectors_done()
     last_copy = pltpu.make_async_copy(VF, vec_out, out_local.at[1 + CHUNKS + 2])
     last_copy.start()

time: 249 us -> 219 us (0.88)
  Pallas kernels: 235 us -> 205 us
    pallas_call x1, Pallas kernels: 214 us -> 184 us  [run_train(): pl.pallas_call(functools.partial(train, n_rep, n_shard), out_shape=[jax.S...]
where the time goes in v3:
time: 219 us; the launch traced here: 218 us
  Pallas kernels  205 us (94%)
  other arithmetic  8.38 us (4%)
  local copies, waits for them, and re-layouts  2.94 us (1%)
    pallas_call x1, Pallas kernels, run_train(): pl.pallas_call(functools.partial(train, n_rep, n_shard), out_shape=[jax.S...  184 us
    pallas_call x1, Pallas kernels, run_update(): pl.pallas_call(functools.partial(update, n_rep, n_shard), out_shape=[one,...  20.8 us

profile of v3, /device:TPU:0, one launch (start us, length us, event | category | flops | bytes accessed | tf_op | source)
XLA Modules:
  0.0 217.6 jit_solution(1138736377261819460)
XLA Ops:
  1.3 0.5 broadcast_in_dim.54.count
  1.8 0.7 fusion
  2.5 0.1 broadcast_in_dim.46
  2.6 0.1 broadcast_in_dim.48
  2.7 0.1 broadcast_in_dim.49
  2.7 0.1 broadcast_in_dim.50
  2.8 0.7 broadcast_in_dim.52.lab_pairs
  3.5 1.6 convert_element_type.18.own_patch
  5.2 2.5 %convert_element_type.20.own_down = bf16[3,384,384]{2,1,0:T(8,128)(2,1)} convert(f32[3,384,384]{2,1,0:T(8,128)} %refs_10_.1) | non-fusion elementwise | flops 442368 | bytes 2654208 | tf_op jit(solution)/shard_map/convert_element_type | solution.py:1637
  7.7 0.0 copy-start
  7.7 3.6 %convert_element_type.19.own_in = bf16[3,96,3072]{2,1,0:T(8,128)(2,1)} convert(f32[3,96,3072]{2,1,0:T(8,128)} %refs_7_.1) | non-fusion elementwise | flops 884736 | bytes 5308416 | tf_op jit(solution)/shard_map/convert_element_type | solution.py:1636
  11.2 0.0 copy-done
  11.2 1.4 pad.4.patches
  12.6 184.0 %train_step.1 = (bf16[6,384,384]{2,1,0:T(8,128)(2,1)}, bf16[2,192,384]{2,1,0:T(8,128)(2,1)}, f32[256,512]{1,0:T(8,128)}, bf16[2,8,16,3456]{3,2,1,0:T(8,128)(2,1)}) custom-call(bf16[6,208,768]{2,1,0:T(8,128)(2,1)} %pad.4.patches, f32[3,32,128]{2,1,0:T(8,128)} %broadcast_in_dim.52.lab_pairs, bf16[192,384]{1,0:T(8,128)(2,1)} %convert_element_type.18.own_patch, ...), custom_call_target="tpu_custom_call" | custom-call | flops 24000000000 | bytes 30000000 | tf_op jit(solution)/shard_map/train_step/pallas_call | solution.py:1335
  196.6 20.8 %adamw.1 = (f32[1,1]{1,0:T(1,128)}, f32[1,1]{1,0:T(1,128)}, f32[192,384]{1,0:T(8,128)}, f32[192,384]{1,0:T(8,128)}, f32[192,384]{1,0:T(8,128)}, /*index=5*/f32[3...) custom-call(bf16[6,384,384]{2,1,0:T(8,128)(2,1)} %get-tuple-element., ...), custom_call_target="tpu_custom_call" | custom-call | flops 200000000 | bytes 50000000 | tf_op jit(solution)/shard_map/adamw/pallas_call | solution.py:1599
  (3 shorter events, 0.0 us)
Async XLA Ops:
  7.7 3.6 %copy-start = (bf16[6,196,768]{2,1,0:T(8,128)(2,1)S(1)}, bf16[6,196,768]{2,1,0:T(8,128)(2,1)}, u32[]{:S(2)}) copy-start(bf16[6,196,768]{2,1,0:T(8,128)(2,1)} %param.24) | copy-start | bytes 5419012

commit v4 on v3

--- a/solution.py
+++ b/solution.py
@@ -136,10 +136,10 @@
 
 def train(
     n_rep, n_shard,
-    patches, lab_pairs, own_patch, own_in, own_down, vecs, glob, pos, head, count,
+    patches, labels, counts, own_patch, own_in, own_down, vecs, glob, pos, head,
     res_out, small_out, vec_out, all_factors,
     X, N1, I1, QKV, ATT, N2, I2, ACT, SLOPE, DXB, DMB, DA,
-    pix, lab, wp, win, wdn, low_head, head_bias,
+    pix, lab, lab_given, wp, win, wdn, low_head, head_bias,
     G, RC, RY, RX, RZ, RES, GS, SC, SY, SX, SZ, SRES,
     FAC, FC, FY, FALL, V, VC, VY, VX, VZ, VF, SQ, SQS, square_sum,
     ag_send, ag_recv, ag_local, rs_send, rs_recv, f_send, f_recv, v_send, v_recv,
@@ -215,23 +215,6 @@
         wide = 4 * D // n_x
         return win.at[layer, rows, pl.ds(aligned(base + part * wide, 128), wide)]
 
-    def owned(kind, layer, part=None):
-        if kind == "patch":
-            if part is None:
-                return own_patch
-            rows = rows_patch // cut(rows_patch, n_x, 16)
-            return own_patch.at[pl.ds(aligned(part * rows, 16), rows), :]
-        if kind == "down":
-            if part is None:
-                return own_down.at[layer]
-            rows = rows_down // cut(rows_down, n_x, 16)
-            return own_down.at[layer, pl.ds(aligned(part * rows, 16), rows), :]
-        base = 0 if kind == "attn" else 4 * D
-        if part is None:
-            return own_in.at[layer, :, pl.ds(base, 4 * D)]
-        wide = 4 * D // n_x
-        return own_in.at[layer, :, pl.ds(aligned(base + part * wide, 128), wide)]
-
     units = [("patch", 0)] + [
         (kind, layer) for layer in range(LAYERS) for kind in ("attn", "up", "down")
     ]
@@ -248,19 +231,64 @@
     base_my = base_x + (n_y - 1) * (n_x - 1)
     base_mx = base_my + (n_y - 1)
 
+    stage = 4 * rows_in
+
+    def weights_copies(unit):
+        kind, layer = units[unit]
+        base = (unit % 2) * stage
+        if kind == "patch":
+            pairs = [(own_patch, X.at[pl.ds(base, rows_patch)])]
+        elif kind == "down":
+            pairs = [(own_down.at[layer], X.at[pl.ds(base, rows_down)])]
+        else:
+            start = 0 if kind == "attn" else 4 * D
+            pairs = [
+                (
+                    own_in.at[layer, :, pl.ds(start + tile * D, D)],
+                    X.at[pl.ds(base + tile * rows_in, rows_in)],
+                )
+                for tile in range(4)
+            ]
+        return [
+            pltpu.make_async_copy(src, dst, ag_local.at[unit, index])
+            for index, (src, dst) in enumerate(pairs)
+        ]
+
+    def weights_cast(unit):
+        kind, layer = units[unit]
+        base = (unit % 2) * stage
+        for copy in weights_copies(unit):
+            copy.wait()
+        if kind == "patch":
+            rows = pl.ds(aligned(here.shard * rows_patch, 16), rows_patch)
+            wp[rows, :] = X[base : base + rows_patch, :].astype(BF)
+        elif kind == "down":
+            rows = pl.ds(aligned(here.shard * rows_down, 16), rows_down)
+            wdn[layer, rows, :] = X[base : base + rows_down, :].astype(BF)
+        else:
+            start = 0 if kind == "attn" else 4 * D
+            rows = pl.ds(aligned(here.shard * rows_in, 16), rows_in)
+            for tile in range(4):
+                win[layer, rows, start + tile * D : start + (tile + 1) * D] = X[
+                    base + tile * rows_in : base + (tile + 1) * rows_in, :
+                ].astype(BF)
+        if unit + 2 < len(units):
+            for copy in weights_copies(unit + 2):
+                copy.start()
+
     def weights_start(unit):
         kind, layer = units[unit]
-        me = here.shard
         part = x if parts_of(kind) > 1 else 0
         for o in range(1, n_y):
             go(
-                lambda: owned(kind, layer, part), weight(kind, layer, me, part), ag, (unit, o),
+                lambda: weight(kind, layer, here.shard, part),
+                weight(kind, layer, here.shard, part), ag, (unit, o),
                 here.to(y=turn(y, o, n_y)),
             )
-        go(lambda: owned(kind, layer), weight(kind, layer, me), ag, (unit, 0), mate)
-        pltpu.make_async_copy(
-            owned(kind, layer), weight(kind, layer, me), ag_local.at[unit]
-        ).start()
+        go(
+            lambda: weight(kind, layer, here.shard), weight(kind, layer, here.shard), ag,
+            (unit, 0), mate,
+        )
 
     def weights_forward(unit):
         kind, layer = units[unit]
@@ -294,9 +322,6 @@
                         make(), ag_recv.at[unit, base_x + index], ag_send.at[unit, base_x + index]
                     )
                     go(make, make(), ag, (unit, base_mx + index), mate)
-        pltpu.make_async_copy(
-            owned(kind, layer), weight(kind, layer, here.shard), ag_local.at[unit]
-        ).wait()
         arrived(weight(kind, layer, y * 2 + 1 - c), ag_recv.at[unit, 0], ag_send.at[unit, 0])
         for o in range(1, n_y):
             shard = turn(y, n_y - o, n_y) * 2 + 1 - c
@@ -318,21 +343,35 @@
             patches.at[pl.ds(2 * half, 2)], pix.at[pl.ds(2 * half, 2)], img_local.at[half]
         )
 
-    def local_lab(half):
-        return pltpu.make_async_copy(lab_pairs.at[half], lab.at[half], img_local.at[2 + half])
+    def marks(pair):
+        row = lax.broadcasted_iota(jnp.int32, (32, 128), 0)
+        found = jnp.full((32, 128), -1.0, F32)
+        for index in range(2):
+            slot = 2 * pair + index
+            value = jnp.where(slot < counts[0], labels[slot], -1).astype(F32)
+            found = jnp.where(row == CLS - TAIL + 16 * index, value, found)
+        return found
 
     local_half(0).start()
-    local_lab(0).start()
+    for unit in range(2):
+        for copy in weights_copies(unit):
+            copy.start()
+    lab[0] = marks(0)
+    lab_given[...] = marks(2)
 
     @pl.when(jnp.logical_not(lower))
     def _():
         push(given, back_half, img_send.at[0], img_recv.at[0], partner)
-        push(lab_pairs.at[2], lab.at[1], img_send.at[1], img_recv.at[1], partner)
+        push(lab_given, lab.at[1], img_send.at[1], img_recv.at[1], partner)
         local_half(1).start()
-        local_lab(1).start()
+        lab[1] = marks(1)
 
     for unit in range(4):
+        weights_cast(unit)
         weights_start(unit)
+    weights_forward(0)
+    for unit in range(4, len(units)):
+        weights_cast(unit)
 
     even = lane_mask(128, 0, 64)
     odd = lane_mask(128, 64, 128)
@@ -460,7 +499,6 @@
             for step, unit in steps:
                 step(unit)
 
-    weights_forward(0)
     weights_ready(0)
 
     def forward_half(half, carry):
@@ -762,12 +800,7 @@
     def _():
         arrived(lab.at[1], img_recv.at[1], img_send.at[1])
 
-    @pl.when(jnp.logical_not(lower))
-    def _():
-        local_lab(1).wait()
-
-    local_lab(0).wait()
-    labels = lab[...].reshape(CROWS, 128)[:, 0:1]
+    marked = lab[...].reshape(CROWS, 128)[:, 0:1]
 
     h1 = tails(DXB)
     stream = tails(X)
@@ -811,8 +844,8 @@
     shifted = logits - peak
     raw = jnp.exp(shifted)
     total = jnp.sum(raw, axis=-1, keepdims=True)
-    alive = jnp.where(labels >= 0.0, 1.0, 0.0)
-    target = jnp.where(class_lane.astype(F32) == labels, 1.0 - SMOOTHING, 0.0) + jnp.where(
+    alive = jnp.where(marked >= 0.0, 1.0, 0.0)
+    target = jnp.where(class_lane.astype(F32) == marked, 1.0 - SMOOTHING, 0.0) + jnp.where(
         class_lane < NCLS, SMOOTHING / NCLS, 0.0
     )
     log_probs = jnp.where(class_lane < NCLS, shifted - jnp.log(total), 0.0)
@@ -823,7 +856,7 @@
     V[last_row : last_row + 1, 0:D] = down_sum(d_final * nf)
     V[last_row + 1 : last_row + 2, 0:D] = down_sum(d_final)
     V[last_row + 2 : last_row + 3, 0:128] = jnp.broadcast_to(down_sum(losses), (1, 128))
-    V[last_row + 3 : last_row + 4, 0:128] = count[...]
+    V[last_row + 3 : last_row + 4, 0:128] = jnp.full((1, 128), counts[0].astype(F32), F32)
     d_top = norm_back(d_final, nf, inf, gain_final)
     low_top = d_top.astype(BF)
     store_vector(last, 7 * D + FF, down_sum(d_top))
@@ -1293,10 +1326,12 @@
     @pl.when(jnp.logical_not(lower))
     def _():
         left_here(given, img_recv.at[0], img_send.at[0])
-        left_here(lab_pairs.at[2], img_recv.at[1], img_send.at[1])
-
-
-def run_train(n_rep, n_shard, patches, lab_pairs, own_patch, own_in, own_down, vecs, glob, pos, head, count):
+        left_here(lab_given, img_recv.at[1], img_send.at[1])
+
+
+def run_train(
+    n_rep, n_shard, patches, labels, counts, own_patch, own_in, own_down, vecs, glob, pos, head
+):
     n_x = 2 ** ((n_rep.bit_length() - 2) // 2)
     n_z, n_y = n_rep // n_x, n_shard // 2
     block = 4 * (D // n_shard)
@@ -1340,7 +1375,7 @@
             jax.ShapeDtypeStruct((VEC_ROWS, VEC_WIDE), F32),
             jax.ShapeDtypeStruct((2, n_rep, group, WFAC), BF),
         ],
-        in_specs=[there] * 5 + [whole] * 5,
+        in_specs=[there] + [pl.BlockSpec(memory_space=pltpu.SMEM)] * 2 + [there] * 3 + [whole] * 4,
         out_specs=[there] * 4,
         scratch_shapes=[
             buf(ROWS, D, dtype=F32),
@@ -1357,6 +1392,7 @@
             buf(ROWS, D),
             buf(KEPT, BLK, PATCH_DIM),
             buf(2, 32, 128, dtype=F32),
+            buf(32, 128, dtype=F32),
             buf(PATCH_DIM, D),
             buf(LAYERS, D, 4 * D + FF),
             buf(LAYERS, FF, D),
@@ -1379,7 +1415,7 @@
             buf(8, 128, dtype=F32),
             sems(units, ag_count),
             sems(units, ag_count),
-            sems(units),
+            sems(units, 4),
             sems(chunks, rs_count),
             sems(chunks, rs_count),
             sems(f_count),
@@ -1398,17 +1434,19 @@
             flops=24_000_000_000, bytes_accessed=30_000_000, transcendentals=10_000_000
         ),
         name="train_step",
-    )(patches, lab_pairs, own_patch, own_in, own_down, vecs, glob, pos, head, count)
+    )(patches, labels, counts, own_patch, own_in, own_down, vecs, glob, pos, head)
 
 
 def adam(weight, first, second, grad, factor, rate):
     grad = grad * factor
     first = BETA_FIRST * first + (1.0 - BETA_FIRST) * grad
-    second = BETA_SECOND * second + (1.0 - BETA_SECOND) * grad * grad
-    first_hat = first * (1.0 / (1.0 - BETA_FIRST**ADAM_STEP))
-    second_hat = second * (1.0 / (1.0 - BETA_SECOND**ADAM_STEP))
-    step = first_hat / (jnp.sqrt(second_hat) + ADAM_EPS) + WEIGHT_DECAY * weight
-    return weight - rate * step, first, second
+    second = BETA_SECOND * second + (1.0 - BETA_SECOND) * (grad * grad)
+    first_scale = 1.0 / (1.0 - BETA_FIRST**ADAM_STEP)
+    root_scale = (1.0 / (1.0 - BETA_SECOND**ADAM_STEP)) ** 0.5
+    bottom = second * lax.rsqrt(second) * root_scale + ADAM_EPS
+    step = first * lax.rsqrt(bottom * bottom)
+    weight = weight * (1.0 - rate * WEIGHT_DECAY) - step * (rate * first_scale)
+    return weight, first, second
 
 
 def update(n_rep, n_shard, *refs):
@@ -1455,13 +1493,18 @@
     h2 = factor(0, FF, D)
     for tile in range(4):
         made = mm_tn(h2, factor(1, tile * D, D))
-        last_in[:, (2 + tile) * D : (3 + tile) * D] = made
+        last_in[:, (4 + tile) * D : (5 + tile) * D] = made
         total = total + squares(made)
+    own_rows = pl.multiple_of(shard * rows_in, 8)
+    for tile in range(2):
+        last_in[pl.ds(own_rows, rows_in), (1 + tile) * D : (2 + tile) * D] = small[
+            0, tile * rows_in : (tile + 1) * rows_in, :
+        ].astype(F32)
     made = mm_tn(factor(0, FF + 2 * D, D), factor(1, FF + D, D))
     last_in[:, 0:D] = made
     total = total + squares(made)
     made = mm_tn(factor(0, FF + D, D), factor(1, FF, D))
-    last_in[:, D : 2 * D] = made
+    last_in[:, 3 * D : 4 * D] = made
     total = total + squares(made)
     d_top = factor(0, FF + 4 * D, D)
     for tile in range(4):
@@ -1521,51 +1564,62 @@
         for move in moves(array, layer, out=True):
             move.start()
 
-    def in_place(layer, column, at, size):
-        return (layer, slice(at, at + size), slice(column * D, (column + 1) * D))
-
-    def in_step(tile_rows):
-        return 32 if tile_rows % 32 == 0 else 16
-
-    step = in_step(rows_in)
+    def loop(count, body):
+        def one(index, nothing):
+            body(index)
+            return nothing
+
+        lax.fori_loop(0, count, one, 0)
+
+    step = 32 if rows_in % 32 == 0 else 16
     own_rows = pl.multiple_of(shard * rows_in, 8)
     for layer in range(LAYERS):
         begin(1, layer)
-        for column in range(8):
+
+        def column_of(column):
+            lanes = pl.ds(pl.multiple_of(column * D, 128), D)
             for at in range(0, rows_in, step):
                 if layer < keep:
-                    k = 3 * (keep - 1 - layer) + (2 if column < 4 else 1)
-                    row = (column % 4) * rows_in + at
-                    grad = res[k, row : row + step, :].astype(F32)
-                elif column in (1, 2):
-                    row = (column - 1) * rows_in + at
-                    grad = small[0, row : row + step, :].astype(F32)
+                    k = 3 * (keep - 1 - layer) + jnp.where(column < 4, 2, 1)
+                    row = pl.multiple_of(lax.rem(column, 4) * rows_in + at, 16)
+                    grad = res[k, pl.ds(row, step), :].astype(F32)
                 else:
-                    held = 0 if column == 0 else column - 2
-                    grad = last_in[
-                        pl.ds(own_rows + at, step), held * D : (held + 1) * D
-                    ]
-                apply(1, in_place(layer, column, at, step), grad, LEARNING_RATE)
+                    grad = last_in[pl.ds(own_rows + at, step), lanes]
+                apply(1, (layer, slice(at, at + step), lanes), grad, LEARNING_RATE)
+
+        loop(8, column_of)
         finish(1, layer)
     down_rows = pl.multiple_of(shard * rows_down, 8)
     for layer in range(LAYERS):
         begin(2, layer)
-        for at in range(0, rows_down, 32):
-            if layer < keep:
-                grad = res[3 * (keep - 1 - layer), at : at + 32, :].astype(F32)
-            else:
-                grad = last_down[pl.ds(down_rows + at, 32), :]
-            apply(2, (layer, slice(at, at + 32), slice(0, D)), grad, LEARNING_RATE)
+
+        def rows_of(index):
+            for half in range(2):
+                at = pl.multiple_of(index * 64 + half * 32, 16)
+                if layer < keep:
+                    grad = res[3 * (keep - 1 - layer), pl.ds(at, 32), :].astype(F32)
+                else:
+                    grad = last_down[pl.ds(down_rows + at, 32), :]
+                apply(2, (layer, pl.ds(at, 32), slice(0, D)), grad, LEARNING_RATE)
+
+        loop(rows_down // 64, rows_of)
         finish(2, layer)
     begin(0)
-    for at in range(0, PATCH_DIM // n_shard, 32):
-        grad = small[1, at : at + 32, :].astype(F32)
-        apply(0, (slice(at, at + 32), slice(0, D)), grad, LEARNING_RATE)
+
+    def patch_rows(index):
+        at = pl.multiple_of(index * 32, 16)
+        grad = small[1, pl.ds(at, 32), :].astype(F32)
+        apply(0, (pl.ds(at, 32), slice(0, D)), grad, LEARNING_RATE)
+
+    loop(PATCH_DIM // n_shard // 32, patch_rows)
     finish(0)
     begin(6)
-    for at in range(0, D, 32):
-        rows = slice(at, at + 32)
+
+    def head_rows(index):
+        rows = pl.ds(pl.multiple_of(index * 16, 16), 16)
         apply(6, (rows, slice(0, NCLS)), grad_head[rows, 0:NCLS], LEARNING_RATE)
+
+    loop(D // 16, head_rows)
     apply(6, (slice(D, D + 1), slice(0, NCLS)), grad_head[D : D + 1, 0:NCLS], LEARNING_RATE)
     finish(6)
     begin(5)
@@ -1603,7 +1657,7 @@
         out_specs=[whole] * 2 + [there] * 21,
         scratch_shapes=[pltpu.VMEM(a.shape, F32) for a in arrays]
         + [
-            pltpu.VMEM((D, 2 * D + FF), F32),
+            pltpu.VMEM((D, 4 * D + FF), F32),
             pltpu.VMEM((FF, D), F32),
             pltpu.VMEM((D + 8, CPAD), F32),
             pltpu.SemaphoreType.DMA((21, LAYERS)),
@@ -1624,17 +1678,10 @@
     m_patch, v_patch, m_in, v_in, m_down, v_down, m_vecs, v_vecs, m_glob, v_glob, m_pos, v_pos,
     m_head, v_head,
 ):
-    slots = patches.shape[0]
-    marked = jnp.where(jnp.arange(slots) < counts[0], labels, -1).astype(F32)
-    lab_pairs = jnp.where(
-        jnp.arange(16)[None, :, None] == CLS - TAIL, marked[:, None, None], -1.0
-    )
-    lab_pairs = jnp.broadcast_to(lab_pairs, (slots, 16, 128)).reshape(slots // 2, 32, 128)
-    count = jnp.broadcast_to(counts.astype(F32)[None], (1, 128))
     padded = jnp.pad(patches, ((0, 0), (0, BLK - PATCHES), (0, 0)))
     res, small, vec, factors = run_train(
-        n_rep, n_shard, padded, lab_pairs, patch_w.astype(BF), layer_in.astype(BF),
-        layer_down.astype(BF), layer_vecs, glob_vecs, pos_embed, head, count,
+        n_rep, n_shard, padded, labels, counts, patch_w, layer_in, layer_down, layer_vecs,
+        glob_vecs, pos_embed, head,
     )
     arrays = [
         patch_w, m_patch, v_patch, layer_in, m_in, v_in, layer_down, m_down, v_down,

time: 219 us -> 213 us (0.973)
  other arithmetic: 8.38 us -> 0 us
  Pallas kernels: 205 us -> 208 us
    convert_element_type x4 -> x0, other arithmetic: 8.37 us -> none  [the longest x1 3.59 us: shards(): layer_in.astype(BF)]
where the time goes in v4:
time: 213 us; the launch traced here: 212 us
  Pallas kernels  208 us (98%)
  local copies, waits for them, and re-layouts  2.89 us (1%)
    pallas_call x1, Pallas kernels, run_train(): pl.pallas_call(functools.partial(train, n_rep, n_shard), out_shape=[jax.S...  186 us
    pallas_call x1, Pallas kernels, run_update(): pl.pallas_call(functools.partial(update, n_rep, n_shard), out_shape=[one,...  22.3 us

profile of v4, /device:TPU:0, one launch (start us, length us, event | category | flops | bytes accessed | tf_op | source)
XLA Modules:
  0.0 212.2 jit_solution(4681373510395848707)
XLA Ops:
  1.3 2.9 %pad.4.patches = bf16[6,208,768]{2,1,0:T(8,128)(2,1)} pad(bf16[6,196,768]{2,1,0:T(8,128)(2,1)} %param.24, bf16[]{:T(256)} %constant.2.clone.1), padding=0_0x0_12x0_0 | pad | bytes 3723266 | tf_op jit(solution)/shard_map/jit(_pad)/pad | solution.py:1681
  4.2 185.5 %train_step.1 = (bf16[6,384,384]{2,1,0:T(8,128)(2,1)}, bf16[2,192,384]{2,1,0:T(8,128)(2,1)}, f32[256,512]{1,0:T(8,128)}, bf16[2,8,16,3456]{3,2,1,0:T(8,128)(2,1)}) custom-call(bf16[6,208,768]{2,1,0:T(8,128)(2,1)} %pad.4.patches, s32[6]{0:T(128)} %labels.1, s32[1]{0:T(128)S(6)} %copy.47.counts, f32[192,384]{1,0:T(8,128)} %refs_4_.1, f32[3,96,3072]{2,1,0:T(8,128)} %refs_7_.1, ...), custom_call_target="tpu_custom_call" | custom-call | flops 24000000000 | bytes 30000000 | tf_op jit(solution)/shard_map/train_step/pallas_call | solution.py:1370
  189.7 22.3 %adamw.1 = (f32[1,1]{1,0:T(1,128)}, f32[1,1]{1,0:T(1,128)}, f32[192,384]{1,0:T(8,128)}, f32[192,384]{1,0:T(8,128)}, f32[192,384]{1,0:T(8,128)}, /*index=5*/f32[3...) custom-call(bf16[6,384,384]{2,1,0:T(8,128)(2,1)} %get-tuple-element., ...), custom_call_target="tpu_custom_call" | custom-call | flops 200000000 | bytes 50000000 | tf_op jit(solution)/shard_map/adamw/pallas_call | solution.py:1653

commit v5 on v4

--- a/solution.py
+++ b/solution.py
@@ -102,7 +102,7 @@
 WFAC = FF + 5 * D
 VEC_ROWS = 256
 VEC_AT = BLK
-VEC_WIDE = D + 128
+VEC_WIDE = D
 MESH = pl.DeviceIdType.MESH
 CHUNKS = 6
 
@@ -137,12 +137,13 @@
 def train(
     n_rep, n_shard,
     patches, labels, counts, own_patch, own_in, own_down, vecs, glob, pos, head,
-    res_out, small_out, vec_out, all_factors,
-    X, N1, I1, QKV, ATT, N2, I2, ACT, SLOPE, DXB, DMB, DA,
+    res_out, small_out, vec_out, square_out, all_factors,
+    X, N1, I1, QKV, ATT, N2, I2, ACT, SLOPE, DXB, DMB, DA, DH,
     pix, lab, lab_given, wp, win, wdn, low_head, head_bias,
     G, RC, RY, RX, RZ, RES, GS, SC, SY, SX, SZ, SRES,
-    FAC, FC, FY, FALL, V, VC, VY, VX, VZ, VF, SQ, SQS, square_sum,
+    FAC, FC, FY, FALL, V, VC, VY, VX, VZ, VF, SQ, SQZ, SQP, square_sum,
     ag_send, ag_recv, ag_local, rs_send, rs_recv, f_send, f_recv, v_send, v_recv,
+    q_send, q_recv,
     img_send, img_recv, img_local, out_local,
 ):
     here = Place(n_rep, n_shard)
@@ -185,12 +186,16 @@
         return lax.rem(at + by, size)
 
     barrier = pltpu.get_barrier_semaphore()
-    others = (
-        [mate]
-        + [here.to(y=turn(y, o, n_y)) for o in range(1, n_y)]
-        + [here.to(x=turn(x, o, n_x)) for o in range(1, n_x)]
-        + [here.to(z=turn(z, o, n_z)) for o in range(1, n_z)]
-    )
+    plane = [
+        (i, j, k) for i in range(n_x) for j in range(n_y) for k in range(2) if i or j or k
+    ]
+
+    def in_plane(step):
+        i, j, k = step
+        return here.to(x=turn(x, i, n_x), y=turn(y, j, n_y), c=lax.rem(c + k, 2))
+
+    others = [in_plane(step) for step in plane]
+    others += [here.to(z=turn(z, o, n_z)) for o in range(1, n_z)]
     for other in others:
         pl.semaphore_signal(barrier, inc=1, device_id=other, device_id_type=MESH)
     pl.semaphore_wait(barrier, len(others))
@@ -391,6 +396,9 @@
     zeros = jnp.zeros((8, D), F32)
     patch_bias = glob[0:1, :]
 
+    def whole_lanes_of(tile):
+        return jnp.concatenate([tile] * (D // 128), axis=1)
+
     def vector(layer, at, size):
         return vecs[pl.ds(layer, 1), at : at + size]
 
@@ -444,6 +452,8 @@
             else:
                 (DMB if tile == 1 else DA)[rows, :] = made.astype(BF)
 
+    ones = jnp.full((BLK, 128), 1.0, BF)
+
     def attend(layer, image):
         rows = pl.ds(aligned(image * BLK, 16), BLK)
         for pair in range(3):
@@ -456,11 +466,12 @@
             probs = []
             for row, size in pieces(HALF):
                 part = scores[row : row + size] + key_row
-                raw = jnp.exp(part - jnp.max(part, axis=-1, keepdims=True))
-                share = 1.0 / jnp.sum(raw, axis=-1, keepdims=True)
-                probs.append((raw * share).astype(BF))
+                probs.append(jnp.exp(part - jnp.max(part, axis=-1, keepdims=True)).astype(BF))
             probs = jnp.concatenate(probs, axis=0)
-            made = mm(probs[:BLK], values * even) + mm(probs[BLK:], values * odd)
+            first = mm(probs[:BLK], jnp.concatenate([values * even, ones], axis=1))
+            second = mm(probs[BLK:], jnp.concatenate([values * odd, ones], axis=1))
+            made = first[:, :128] * (1.0 / first[:, 128:])
+            made = made + second[:, :128] * (1.0 / second[:, 128:])
             ATT[layer, rows, at : at + 128] = made.astype(BF)
 
     def mlp(layer, half):
@@ -614,9 +625,12 @@
 
     def chunk(k):
         if k < CHUNKS:
-            return G.at[k], RC.at[k % 3], RY.at[k % 3], RX.at[k], RZ.at[k], RES.at[k], block
+            slot = k % 3
+            return (
+                G.at[k], RC.at[slot], RY.at[slot], RX.at[slot], RZ.at[slot], RES.at[k], block
+            )
         k = k - CHUNKS
-        return GS.at[k], SC.at[k], SY.at[k], SX.at[k], SZ.at[k], SRES.at[k], block // 2
+        return GS.at[k], SC.at[0], SY.at[0], SX.at[0], SZ.at[0], SRES.at[k], block // 2
 
     def splits(rows):
         by_x = cut(rows, n_x, 16)
@@ -921,7 +935,7 @@
         gain_sum = gain_sum + fold(part * normed)
         shift_sum = shift_sum + fold(part)
         X[rows, :] = d_middle[image * 16 : (image + 1) * 16] + norm_back(
-            part, normed, I1[last, rows, :][:, 0:1], gain
+            part, normed, whole_lanes_of(I1[last, rows, :]), gain
         )
 
     def first_back(layer, half, made, sums):
@@ -932,7 +946,7 @@
             rows = pl.ds(aligned(base + at, 16), size)
             part = made[at : at + size]
             normed = N1[layer, rows, :].astype(F32)
-            inverse = I1[layer, rows, :][:, 0:1]
+            inverse = whole_lanes_of(I1[layer, rows, :])
             gain_sum = gain_sum + fold(part * normed)
             shift_sum = shift_sum + fold(part)
             X[rows, :] = X[rows, :] + norm_back(part, normed, inverse, gain)
@@ -949,34 +963,41 @@
     reduce_y(CHUNKS)
     factors_x()
 
-    def mlp_back(layer, half, sums):
-        base = half * HALF
-        whole = pl.ds(aligned(base, 16), HALF)
-        bias_down, bias_up, gain_sum, shift_sum, bias_out = sums
+    def round_up(half, total):
         for at, size in pieces(HALF):
-            rows = pl.ds(aligned(base + at, 16), size)
+            rows = pl.ds(aligned(half * HALF + at, 16), size)
             up = X[rows, :]
             DXB[rows, :] = up.astype(BF)
-            bias_down = bias_down + fold(up)
-        low = DXB[whole, :]
+            total = total + fold(up)
+        return total
+
+    def act_back(layer, half, totals):
+        base = half * HALF
+        low = DXB[pl.ds(aligned(base, 16), HALF), :]
         ups = []
         for tile in range(4):
             columns = slice(tile * D, (tile + 1) * D)
             made = mm_nt(low, wdn[layer, columns, :])
-            total = bias_up[tile]
+            total = totals[tile]
             for at, size in pieces(HALF):
                 rows = pl.ds(aligned(base + at, 16), size)
                 grad = (made[at : at + size] * SLOPE[layer, rows, columns].astype(F32)).astype(BF)
-                SLOPE[layer, rows, columns] = grad
+                DH[rows, columns] = grad
                 total = total + fold(grad.astype(F32))
             ups.append(total)
-        made = mm_nt(SLOPE[layer, whole, :], win[layer, :, 4 * D :])
+        return tuple(ups)
+
+    def mlp_back(layer, half, sums):
+        base = half * HALF
+        whole = pl.ds(aligned(base, 16), HALF)
+        gain_sum, shift_sum, bias_out = sums
+        made = mm_nt(DH[whole, :], win[layer, :, 4 * D :])
         gain = vector(layer, 5 * D, D)
         for at, size in pieces(HALF):
             rows = pl.ds(aligned(base + at, 16), size)
             part = made[at : at + size]
             normed = N2[layer, rows, :].astype(F32)
-            inverse = I2[layer, rows, :][:, 0:1]
+            inverse = whole_lanes_of(I2[layer, rows, :])
             gain_sum = gain_sum + fold(part * normed)
             shift_sum = shift_sum + fold(part)
             grad = X[rows, :] + norm_back(part, normed, inverse, gain)
@@ -984,7 +1005,7 @@
             DMB[rows, :] = grad.astype(BF)
             bias_out = bias_out + fold(grad)
         DA[whole, :] = mm_nt(DMB[whole, :], win[layer, :, 3 * D : 4 * D]).astype(BF)
-        return bias_down, tuple(ups), gain_sum, shift_sum, bias_out
+        return gain_sum, shift_sum, bias_out
 
     def attend_back(layer, image):
         rows = pl.ds(aligned(image * BLK, 16), BLK)
@@ -1022,11 +1043,11 @@
             d_values = mm(probs, ups)
             d_keys = mm(d_scores, query)
             d_query = mm_tn(d_scores, keys_both) * 0.125
-            QKV[layer, rows, at : at + 128] = d_query.astype(BF)
-            QKV[layer, rows, D + at : D + at + 128] = jnp.where(
+            DH[rows, at : at + 128] = d_query.astype(BF)
+            DH[rows, D + at : D + at + 128] = jnp.where(
                 low_lane, d_keys[:BLK], d_keys[BLK:]
             ).astype(BF)
-            QKV[layer, rows, 2 * D + at : 2 * D + at + 128] = jnp.where(
+            DH[rows, 2 * D + at : 2 * D + at + 128] = jnp.where(
                 low_lane, d_values[:BLK], d_values[BLK:]
             ).astype(BF)
 
@@ -1052,27 +1073,13 @@
         kd, ku, kq = 3 * step, 3 * step + 1, 3 * step + 2
         upper_layer, bottom = step == 0, step == 1
 
-        def one(half, sums):
-            sums = mlp_back(layer, half, sums)
-            begin = half == 0
-
-            @pl.when(jnp.logical_and(upper_layer, begin))
-            def _():
-                factors_z()
-
-            when(jnp.logical_and(bottom, begin), (gather_z, CHUNKS))
-            return sums
-
-        bias_down, bias_up, gain_sum, shift_sum, bias_out = lax.fori_loop(
-            0, 2, one, (zeros, (zeros,) * 4, zeros, zeros, zeros)
-        )
+        bias_down = lax.fori_loop(0, 2, round_up, zeros)
         when(upper_layer, (reduce_x, CHUNKS))
-        when(bottom, (reduce_x, 2), (reduce_z, 1))
-        store_sums(
-            layer,
-            [(7 * D + FF, bias_down), (5 * D, gain_sum), (6 * D, shift_sum), (4 * D, bias_out)]
-            + [(7 * D + tile * D, bias_up[tile]) for tile in range(4)],
-        )
+
+        @pl.when(upper_layer)
+        def _():
+            factors_z()
+
         turned = DXB[...].T
         per = min(rows_down, D)
         for tile in range(4):
@@ -1084,57 +1091,75 @@
                     piece * per : (piece + 1) * per
                 ]
         when(upper_layer, (reduce_core, 0))
-        when(bottom, (reduce_core, 3), (gather_z, 0), (gather_x, CHUNKS))
+        when(bottom, (reduce_core, 3), (gather_z, CHUNKS))
+
+        def one(half, totals):
+            return act_back(layer, half, totals)
+
+        bias_up = lax.fori_loop(0, 2, one, (zeros,) * 4)
+        when(upper_layer, (reduce_y, 0))
+        when(bottom, (reduce_x, 2), (reduce_y, 3), (reduce_z, 1))
         turned = renew(N2, layer, 5 * D)
         for tile in range(4):
-            keep_in(
-                ku, tile, mm(turned, SLOPE[layer, :, tile * D : (tile + 1) * D]).astype(BF)
-            )
-        when(upper_layer, (reduce_core, 1), (reduce_y, 0), (reduce_z, CHUNKS))
-        when(bottom, (reduce_core, 4), (reduce_y, 3), (reduce_z, 2))
+            keep_in(ku, tile, mm(turned, DH[:, tile * D : (tile + 1) * D]).astype(BF))
+        when(upper_layer, (reduce_core, 1))
+        when(bottom, (reduce_core, 4), (gather_z, 0), (gather_x, CHUNKS))
+
+        def one_more(half, sums):
+            return mlp_back(layer, half, sums)
+
+        gain_sum, shift_sum, bias_out = lax.fori_loop(0, 2, one_more, (zeros, zeros, zeros))
+        when(upper_layer, (reduce_y, 1), (reduce_z, CHUNKS))
+        when(bottom, (reduce_y, 4), (reduce_z, 2), (gather_z, 1))
+        store_sums(
+            layer,
+            [(7 * D + FF, bias_down), (5 * D, gain_sum), (6 * D, shift_sum), (4 * D, bias_out)]
+            + [(7 * D + tile * D, bias_up[tile]) for tile in range(4)],
+        )
         keep_in(kq, 3, mm(ATT[layer].T, DMB[...]).astype(BF))
 
         def two(image, nothing):
             attend_back(layer, image)
-            when(jnp.logical_and(upper_layer, image == 0), (reduce_y, 1))
-            when(jnp.logical_and(upper_layer, image == 2), (reduce_x, 0))
-            when(jnp.logical_and(bottom, image == 0), (reduce_y, 4), (gather_z, 1))
-
-            @pl.when(jnp.logical_and(bottom, image == 1))
+            when(jnp.logical_and(upper_layer, image == 0), (reduce_x, 0))
+            when(jnp.logical_and(upper_layer, image == 2), (reduce_x, 1))
+            when(jnp.logical_and(upper_layer, image == 3), (reduce_z, 0))
+
+            @pl.when(jnp.logical_and(bottom, image == 0))
             def _():
                 factors_mate()
                 gather_done(CHUNKS)
                 gather_x(0)
 
-            when(jnp.logical_and(bottom, image == 2), (reduce_x, 3), (gather_z, 2))
-            when(jnp.logical_and(bottom, image == 3), (gather_x, 1), (reduce_z, 3))
+            when(jnp.logical_and(bottom, image == 1), (reduce_x, 3), (gather_z, 2))
+            when(jnp.logical_and(bottom, image == 2), (gather_x, 1), (reduce_z, 3))
+            when(jnp.logical_and(bottom, image == 3), (reduce_x, 4), (gather_x, 2), (gather_done, 0))
             return nothing
 
         lax.fori_loop(0, KEPT, two, 0)
         turned = renew(N1, layer, 0)
         for tile in range(3):
             keep_in(
-                kq, tile, mm(turned, QKV[layer, :, tile * D : (tile + 1) * D]).astype(BF)
+                kq, tile, mm(turned, DH[:, tile * D : (tile + 1) * D]).astype(BF)
             )
         when(upper_layer, (reduce_core, 2))
-        when(bottom, (reduce_core, 5), (gather_x, 2), (gather_done, 0))
+        when(bottom, (reduce_core, 5), (gather_z, 3))
         store_sums(
             layer,
             [
-                (2 * D, fold(QKV[layer, :, 0:D].astype(F32))),
-                (3 * D, fold(QKV[layer, :, 2 * D : 3 * D].astype(F32))),
+                (2 * D, fold(DH[:, 0:D].astype(F32))),
+                (3 * D, fold(DH[:, 2 * D : 3 * D].astype(F32))),
             ],
         )
 
         def three(half, sums):
             rows = pl.ds(aligned(half * HALF, 16), HALF)
-            made = mm_nt(QKV[layer, rows, :], win[layer, :, 0 : 3 * D])
+            made = mm_nt(DH[rows, 0 : 3 * D], win[layer, :, 0 : 3 * D])
             return first_back(layer, half, made, sums)
 
         gain_sum, shift_sum = lax.fori_loop(0, 2, three, (zeros, zeros))
         store_sums(layer, [(0, gain_sum), (D, shift_sum)])
-        when(upper_layer, (reduce_x, 1), (reduce_y, 2), (reduce_z, 0))
-        when(bottom, (reduce_y, 5), (reduce_x, 4), (gather_z, 3), (gather_done, 1))
+        when(upper_layer, (reduce_y, 2))
+        when(bottom, (reduce_y, 5), (reduce_z, 4), (gather_done, 1))
         return carry
 
     lax.fori_loop(0, LAYERS - 1, backward, 0)
@@ -1151,8 +1176,7 @@
     v_y, v_x = 1, n_y
     v_z = v_x + n_x - 1
     v_gz = v_z + n_z - 1
-    v_q = v_gz + n_z - 1
-    v_gx = v_q + n_z - 1
+    v_gx = v_gz + n_z - 1
     v_gy = v_gx + n_x - 1
     v_gc = v_gy + n_y - 1
     rows_c = VEC_ROWS // 2
@@ -1168,9 +1192,6 @@
     def vrows(ref, at, rows):
         return ref.at[pl.ds(aligned(at, 8), rows), :]
 
-    def narrow(at, rows):
-        return VF.at[pl.ds(aligned(at, 8), rows), pl.ds(0, D)]
-
     def vadd(at, rows, sources):
         target = pl.ds(aligned(at, 8), rows)
         total = V[target, :]
@@ -1224,39 +1245,63 @@
         total = VZ[0]
         for index in range(1, n_z):
             total = total + VZ[index]
-        VF[target, 0:D] = total[:, 0:D]
+        VF[target, :] = total
         if split_z > 1:
             for o in range(1, n_z):
                 go(
-                    lambda: narrow(at_z, rows_z), narrow(at_z, rows_z), vec, v_gz + o - 1,
+                    lambda: vrows(VF, at_z, rows_z), vrows(VF, at_z, rows_z), vec, v_gz + o - 1,
                     here.to(z=turn(z, o, n_z)),
                 )
 
-    def squares_send():
-        SQ[...] = square_sum[...]
-        SQS[z] = square_sum[...]
-        for o in range(1, n_z):
-            go(lambda: SQ, SQS.at[z], vec, v_q + o - 1, here.to(z=turn(z, o, n_z)))
-
     def vectors_gather_x():
-        for o in range(1, n_z):
-            came = turn(z, n_z - o, n_z)
-            if split_z > 1:
+        if split_z > 1:
+            for o in range(1, n_z):
+                came = turn(z, n_z - o, n_z)
                 arrived(
-                    narrow(at_x + came * rows_z, rows_z), v_recv.at[v_gz + o - 1],
+                    vrows(VF, at_x + came * rows_z, rows_z), v_recv.at[v_gz + o - 1],
                     v_send.at[v_gz + o - 1],
                 )
-            arrived(SQS.at[came], v_recv.at[v_q + o - 1], v_send.at[v_q + o - 1])
-        total = SQS[0]
-        for index in range(1, n_z):
-            total = total + SQS[index]
-        for at in range(0, rows_x, 8):
-            VF[pl.ds(aligned(at_x + at, 8), 8), D:] = total
         for o in range(1, n_x):
             go(
                 lambda: vrows(VF, at_x, rows_x), vrows(VF, at_x, rows_x), vec, v_gx + o - 1,
                 here.to(x=turn(x, o, n_x)),
             )
+
+    sq = ("q", q_send, q_recv)
+
+    def squares_z():
+        SQ[0] = square_sum[...]
+        SQZ[z] = square_sum[...]
+        for o in range(1, n_z):
+            go(lambda: SQ.at[0], SQZ.at[z], sq, o - 1, here.to(z=turn(z, o, n_z)))
+
+    def slot_of(i, j, k):
+        return (i * n_y + j) * 2 + k
+
+    def squares_plane():
+        for o in range(1, n_z):
+            arrived(SQZ.at[turn(z, n_z - o, n_z)], q_recv.at[o - 1], q_send.at[o - 1])
+        total = SQZ[0]
+        for index in range(1, n_z):
+            total = total + SQZ[index]
+        SQ[1] = total
+        SQP[slot_of(x, y, c)] = total
+        for index, step in enumerate(plane):
+            go(
+                lambda: SQ.at[1], SQP.at[slot_of(x, y, c)], sq, n_z - 1 + index,
+                in_plane(step),
+            )
+
+    def squares_done():
+        for index, (i, j, k) in enumerate(plane):
+            slot = slot_of(
+                turn(x, n_x - i, n_x), turn(y, n_y - j, n_y), lax.rem(c + k, 2)
+            )
+            arrived(SQP.at[slot], q_recv.at[n_z - 1 + index], q_send.at[n_z - 1 + index])
+        total = SQP[0]
+        for index in range(1, 2 * n_x * n_y):
+            total = total + SQP[index]
+        SQ[2] = total
 
     def vectors_gather_y():
         for o in range(1, n_x):
@@ -1287,41 +1332,47 @@
 
     kp = CHUNKS + 1
     reduce_core(kp)
-    reduce_z(4)
     vectors_y()
+    gather_done(2)
+    gather_x(3)
     reduce_y(kp)
-    gather_x(3)
-    reduce_x(5)
     vectors_x()
     gather_z(4)
+    reduce_x(5)
+    vectors_z()
     reduce_x(kp)
+    gather_x(4)
+    vectors_gather_z()
     reduce_z(5)
-    vectors_z()
-    gather_done(2)
-    gather_x(4)
+    reduce_z(kp)
+    vectors_gather_x()
     gather_done(3)
-    reduce_z(kp)
     gather_z(5)
-    vectors_gather_z()
+    vectors_gather_y()
+    gather_done(4)
+    gather_x(5)
     gather_z(kp)
-    squares_send()
-    gather_x(5)
+    squares_z()
     gather_x(kp)
-    vectors_gather_x()
-    gather_done(4)
-    vectors_gather_y()
+    vectors_gather_core()
+    factors_done()
+    squares_plane()
+    vectors_done()
     gather_done(5)
     gather_done(kp)
-    vectors_gather_core()
-    factors_done()
-    vectors_done()
-    last_copy = pltpu.make_async_copy(VF, vec_out, out_local.at[1 + CHUNKS + 2])
-    last_copy.start()
+    squares_done()
+    last_copies = [
+        pltpu.make_async_copy(VF, vec_out, out_local.at[1 + CHUNKS + 2]),
+        pltpu.make_async_copy(SQ.at[2], square_out, out_local.at[2 + CHUNKS + 2]),
+    ]
+    for copy in last_copies:
+        copy.start()
     for source, send, recv, at in list(sent.values()):
         left_here(source(), recv.at[at], send.at[at])
     for k in range(CHUNKS + 2):
         result(k).wait()
-    last_copy.wait()
+    for copy in last_copies:
+        copy.wait()
 
     @pl.when(jnp.logical_not(lower))
     def _():
@@ -1346,15 +1397,15 @@
     def sems(*shape):
         return pltpu.SemaphoreType.DMA(shape)
 
-    def reduction(count, rows):
+    def reduction(count, slots, rows):
         by_x = cut(rows, n_x, 16)
         by_z = cut(rows // by_x, n_z, 16)
         return [
             buf(count, n_y, 2, rows, D),
-            buf(min(count, 3), n_y, rows, D),
-            buf(min(count, 3), n_y - 1, rows, D),
-            buf(count, n_x - 1 if by_x > 1 else n_x, rows // by_x, D),
-            buf(count, n_z, rows // by_x // by_z, D),
+            buf(slots, n_y, rows, D),
+            buf(slots, n_y - 1, rows, D),
+            buf(slots, n_x - 1 if by_x > 1 else n_x, rows // by_x, D),
+            buf(slots, n_z, rows // by_x // by_z, D),
             buf(count, rows, D),
         ]
 
@@ -1364,7 +1415,8 @@
     ag_count = n_y + (n_y - 1) * (n_x - 1) * 2 + n_y - 1
     rs_count = 1 + (n_y - 1) + 2 * (n_x - 1) + 2 * (n_z - 1)
     f_count = 1 + (n_y - 1) + (n_x - 1) + (n_z - 1) + 1
-    v_count = 1 + 2 * (n_y - 1) + 2 * (n_x - 1) + 3 * (n_z - 1) + 1
+    v_count = 1 + 2 * (n_y - 1) + 2 * (n_x - 1) + 2 * (n_z - 1) + 1
+    q_count = n_z - 1 + 2 * n_x * n_y - 1
     whole = pl.BlockSpec(memory_space=pltpu.VMEM)
     there = pl.BlockSpec(memory_space=pl.ANY)
     return pl.pallas_call(
@@ -1373,10 +1425,11 @@
             jax.ShapeDtypeStruct((CHUNKS, block, D), BF),
             jax.ShapeDtypeStruct((2, block // 2, D), BF),
             jax.ShapeDtypeStruct((VEC_ROWS, VEC_WIDE), F32),
+            jax.ShapeDtypeStruct((8, 128), F32),
             jax.ShapeDtypeStruct((2, n_rep, group, WFAC), BF),
         ],
         in_specs=[there] + [pl.BlockSpec(memory_space=pltpu.SMEM)] * 2 + [there] * 3 + [whole] * 4,
-        out_specs=[there] * 4,
+        out_specs=[there] * 5,
         scratch_shapes=[
             buf(ROWS, D, dtype=F32),
             buf(LAYERS, ROWS, D),
@@ -1390,6 +1443,7 @@
             buf(ROWS, D),
             buf(ROWS, D),
             buf(ROWS, D),
+            buf(ROWS, FF),
             buf(KEPT, BLK, PATCH_DIM),
             buf(2, 32, 128, dtype=F32),
             buf(32, 128, dtype=F32),
@@ -1398,8 +1452,8 @@
             buf(LAYERS, FF, D),
             buf(D, CPAD),
             buf(1, CPAD, dtype=F32),
-            *reduction(CHUNKS, block),
-            *reduction(2, block // 2),
+            *reduction(CHUNKS, 3, block),
+            *reduction(2, 1, block // 2),
             buf(2, group, WFAC),
             buf(group, WFAC),
             buf(n_y - 1, group, WFAC),
@@ -1410,8 +1464,9 @@
             buf(n_x - 1, rows_x, VEC_WIDE, dtype=F32),
             buf(n_z, rows_z, VEC_WIDE, dtype=F32),
             buf(VEC_ROWS, VEC_WIDE, dtype=F32),
-            buf(8, 128, dtype=F32),
+            buf(3, 8, 128, dtype=F32),
             buf(n_z, 8, 128, dtype=F32),
+            buf(2 * n_x * n_y, 8, 128, dtype=F32),
             buf(8, 128, dtype=F32),
             sems(units, ag_count),
             sems(units, ag_count),
@@ -1422,10 +1477,12 @@
             sems(f_count),
             sems(v_count),
             sems(v_count),
+            sems(q_count),
+            sems(q_count),
             sems(2),
             sems(2),
             sems(4),
-            sems(2 + chunks),
+            sems(3 + chunks),
         ],
         compiler_params=pltpu.CompilerParams(
             vmem_limit_bytes=65400 * 1024, collective_id=0, has_side_effects=True
@@ -1450,12 +1507,13 @@
 
 
 def update(n_rep, n_shard, *refs):
-    res, small, vec, factors = refs[0:4]
-    sources = refs[4:25]
-    loss_out, norm_out = refs[25:27]
-    targets = refs[27:48]
-    buffers = refs[48:69]
-    last_in, last_down, grad_head, in_sems, out_sems = refs[69:]
+    res, small, vec, exchanged, factors = refs[0:5]
+    sources = refs[5:26]
+    loss_out, norm_out = refs[26:28]
+    targets = refs[28:49]
+    buffers = refs[49:70]
+    results = refs[70:91]
+    last_in, last_down, passing, grad_head, in_sems, out_sems = refs[91:]
     shard = lax.axis_index("shard")
     rows_in = D // n_shard
     rows_down = FF // n_shard
@@ -1466,7 +1524,7 @@
         for kind in range(3):
             index = 3 * array + kind
             if out:
-                src, dst, sem = buffers[index], targets[index], out_sems
+                src, dst, sem = results[index], targets[index], out_sems
             else:
                 src, dst, sem = sources[index], buffers[index], in_sems
             slot = 0 if layer is None else layer
@@ -1490,27 +1548,40 @@
         return fold(values * values)
 
     total = jnp.zeros((8, D), F32)
+    own_rows = pl.multiple_of(shard * rows_in, 8)
+
+    def keep_in(column, made):
+        slot = column % 2
+        passing[slot] = made
+        last_in[:, column * D : (column + 1) * D] = passing[slot, pl.ds(own_rows, rows_in), :]
+
     h2 = factor(0, FF, D)
     for tile in range(4):
         made = mm_tn(h2, factor(1, tile * D, D))
-        last_in[:, (4 + tile) * D : (5 + tile) * D] = made
+        keep_in(4 + tile, made)
         total = total + squares(made)
-    own_rows = pl.multiple_of(shard * rows_in, 8)
     for tile in range(2):
-        last_in[pl.ds(own_rows, rows_in), (1 + tile) * D : (2 + tile) * D] = small[
+        last_in[:, (1 + tile) * D : (2 + tile) * D] = small[
             0, tile * rows_in : (tile + 1) * rows_in, :
         ].astype(F32)
     made = mm_tn(factor(0, FF + 2 * D, D), factor(1, FF + D, D))
-    last_in[:, 0:D] = made
+    keep_in(0, made)
     total = total + squares(made)
     made = mm_tn(factor(0, FF + D, D), factor(1, FF, D))
-    last_in[:, 3 * D : 4 * D] = made
+    keep_in(3, made)
     total = total + squares(made)
     d_top = factor(0, FF + 4 * D, D)
+    per = min(rows_down, D)
     for tile in range(4):
         made = mm_tn(factor(0, tile * D, D), d_top)
-        last_down[tile * D : (tile + 1) * D, :] = made
         total = total + squares(made)
+        for piece in range(D // per):
+            owner, at = divmod(tile * D + piece * per, rows_down)
+
+            def keep_down(made=made, piece=piece, at=at):
+                last_down[at : at + per, :] = made[piece * per : (piece + 1) * per]
+
+            pl.when(shard == owner)(keep_down)
     final = factor(0, FF + 3 * D, D)
     wide = jnp.zeros((8, 128), F32)
     for at in range(0, CPAD, 512):
@@ -1540,9 +1611,7 @@
     parts = parts + rest
     for lane in range(0, D, 128):
         wide = wide + parts[:, lane : lane + 128]
-    n_x = 2 ** ((n_rep.bit_length() - 2) // 2)
-    rows_x = VEC_ROWS // n_shard // n_x
-    wide = wide + fold(vec[:, D:]) * (8.0 / rows_x)
+    wide = wide + exchanged[...]
     sum_squares = jnp.sum(jnp.sum(wide, axis=1, keepdims=True), axis=0, keepdims=True)
     inv_count = 1.0 / vec[used + 1 : used + 2, 0:1]
     grad_norm = jnp.sqrt(sum_squares) * inv_count
@@ -1553,8 +1622,8 @@
     def apply(array, where, grad, rate):
         refs = [buffers[3 * array + kind] for kind in range(3)]
         made = adam(refs[0][where], refs[1][where], refs[2][where], grad, scale, rate)
-        for ref, value in zip(refs, made):
-            ref[where] = value
+        for kind, value in enumerate(made):
+            results[3 * array + kind][where] = value
 
     def begin(array, layer=None):
         for move in moves(array, layer):
@@ -1572,7 +1641,6 @@
         lax.fori_loop(0, count, one, 0)
 
     step = 32 if rows_in % 32 == 0 else 16
-    own_rows = pl.multiple_of(shard * rows_in, 8)
     for layer in range(LAYERS):
         begin(1, layer)
 
@@ -1584,42 +1652,43 @@
                     row = pl.multiple_of(lax.rem(column, 4) * rows_in + at, 16)
                     grad = res[k, pl.ds(row, step), :].astype(F32)
                 else:
-                    grad = last_in[pl.ds(own_rows + at, step), lanes]
+                    grad = last_in[at : at + step, lanes]
                 apply(1, (layer, slice(at, at + step), lanes), grad, LEARNING_RATE)
 
         loop(8, column_of)
         finish(1, layer)
-    down_rows = pl.multiple_of(shard * rows_down, 8)
     for layer in range(LAYERS):
         begin(2, layer)
 
         def rows_of(index):
-            for half in range(2):
-                at = pl.multiple_of(index * 64 + half * 32, 16)
+            for part in range(3):
+                at = pl.multiple_of(index * 96 + part * 32, 16)
                 if layer < keep:
                     grad = res[3 * (keep - 1 - layer), pl.ds(at, 32), :].astype(F32)
                 else:
-                    grad = last_down[pl.ds(down_rows + at, 32), :]
+                    grad = last_down[pl.ds(at, 32), :]
                 apply(2, (layer, pl.ds(at, 32), slice(0, D)), grad, LEARNING_RATE)
 
-        loop(rows_down // 64, rows_of)
+        loop(rows_down // 96, rows_of)
         finish(2, layer)
     begin(0)
 
     def patch_rows(index):
-        at = pl.multiple_of(index * 32, 16)
-        grad = small[1, pl.ds(at, 32), :].astype(F32)
-        apply(0, (pl.ds(at, 32), slice(0, D)), grad, LEARNING_RATE)
-
-    loop(PATCH_DIM // n_shard // 32, patch_rows)
+        for part in range(3):
+            at = pl.multiple_of(index * 96 + part * 32, 16)
+            grad = small[1, pl.ds(at, 32), :].astype(F32)
+            apply(0, (pl.ds(at, 32), slice(0, D)), grad, LEARNING_RATE)
+
+    loop(PATCH_DIM // n_shard // 96, patch_rows)
     finish(0)
     begin(6)
 
     def head_rows(index):
-        rows = pl.ds(pl.multiple_of(index * 16, 16), 16)
-        apply(6, (rows, slice(0, NCLS)), grad_head[rows, 0:NCLS], LEARNING_RATE)
-
-    loop(D // 16, head_rows)
+        for part in range(3):
+            rows = pl.ds(pl.multiple_of(index * 48 + part * 16, 16), 16)
+            apply(6, (rows, slice(0, NCLS)), grad_head[rows, 0:NCLS], LEARNING_RATE)
+
+    loop(D // 48, head_rows)
     apply(6, (slice(D, D + 1), slice(0, NCLS)), grad_head[D : D + 1, 0:NCLS], LEARNING_RATE)
     finish(6)
     begin(5)
@@ -1646,19 +1715,20 @@
             move.wait()
 
 
-def run_update(n_rep, n_shard, res, small, vec, factors, arrays):
+def run_update(n_rep, n_shard, res, small, vec, squares, factors, arrays):
     whole = pl.BlockSpec(memory_space=pltpu.VMEM)
     there = pl.BlockSpec(memory_space=pl.ANY)
     one = jax.ShapeDtypeStruct((1, 1), F32)
     made = pl.pallas_call(
         functools.partial(update, n_rep, n_shard),
         out_shape=[one, one] + [jax.ShapeDtypeStruct(a.shape, F32) for a in arrays],
-        in_specs=[whole] * 4 + [there] * 21,
+        in_specs=[whole] * 5 + [there] * 21,
         out_specs=[whole] * 2 + [there] * 21,
-        scratch_shapes=[pltpu.VMEM(a.shape, F32) for a in arrays]
+        scratch_shapes=[pltpu.VMEM(a.shape, F32) for a in (*arrays, *arrays)]
         + [
-            pltpu.VMEM((D, 4 * D + FF), F32),
-            pltpu.VMEM((FF, D), F32),
+            pltpu.VMEM((D // n_shard, 4 * D + FF), F32),
+            pltpu.VMEM((FF // n_shard, D), F32),
+            pltpu.VMEM((2, D, D), F32),
             pltpu.VMEM((D + 8, CPAD), F32),
             pltpu.SemaphoreType.DMA((21, LAYERS)),
             pltpu.SemaphoreType.DMA((21, LAYERS)),
@@ -1668,7 +1738,7 @@
             flops=200_000_000, bytes_accessed=50_000_000, transcendentals=4_000_000
         ),
         name="adamw",
-    )(res, small, vec, factors, *arrays)
+    )(res, small, vec, squares, factors, *arrays)
     return made[0].reshape(()), made[1].reshape(()), made[2:]
 
 
@@ -1679,7 +1749,7 @@
     m_head, v_head,
 ):
     padded = jnp.pad(patches, ((0, 0), (0, BLK - PATCHES), (0, 0)))
-    res, small, vec, factors = run_train(
+    res, small, vec, squares, factors = run_train(
         n_rep, n_shard, padded, labels, counts, patch_w, layer_in, layer_down, layer_vecs,
         glob_vecs, pos_embed, head,
     )
@@ -1688,7 +1758,7 @@
         layer_vecs, m_vecs, v_vecs, glob_vecs, m_glob, v_glob, pos_embed, m_pos, v_pos,
         head, m_head, v_head,
     ]
-    loss, grad_norm, new = run_update(n_rep, n_shard, res, small, vec, factors, arrays)
+    loss, grad_norm, new = run_update(n_rep, n_shard, res, small, vec, squares, factors, arrays)
     return (loss, grad_norm, *new)
 
 

time: 213 us -> 209 us (0.981)
  Pallas kernels: 208 us -> 205 us
    pallas_call x1, Pallas kernels: 186 us -> 183 us  [run_train(): pl.pallas_call(functools.partial(train, n_rep, n_shard), out_shape=[jax.S...]
where the time goes in v5:
time: 209 us
  Pallas kernels  205 us (98%)
  local copies, waits for them, and re-layouts  2.89 us (1%)
    pallas_call x1, Pallas kernels, run_train(): pl.pallas_call(functools.partial(train, n_rep, n_shard), out_shape=[jax.S...  183 us
    pallas_call x1, Pallas kernels, run_update(): pl.pallas_call(functools.partial(update, n_rep, n_shard), out_shape=[one,...  21.3 us

profile of v5, /device:TPU:0, one launch (start us, length us, event | category | flops | bytes accessed | tf_op | source)
XLA Modules:
  0.0 208.9 jit_solution(7527563637428888480)
XLA Ops:
  1.3 2.9 %pad.4.patches = bf16[6,208,768]{2,1,0:T(8,128)(2,1)} pad(bf16[6,196,768]{2,1,0:T(8,128)(2,1)} %param.24, bf16[]{:T(256)} %constant.2.clone.1), padding=0_0x0_12x0_0 | pad | bytes 3723266 | tf_op jit(solution)/shard_map/jit(_pad)/pad | solution.py:1751
  4.2 183.2 %train_step.1 = (bf16[6,384,384]{2,1,0:T(8,128)(2,1)}, bf16[2,192,384]{2,1,0:T(8,128)(2,1)}, f32[256,384]{1,0:T(8,128)}, f32[8,128]{1,0:T(8,128)}, bf16[2,8,16,3456]{3,2,1,0:T(8,128)(2,1)}) custom-call(bf16[6,208,768]{2,1,0:T(8,128)(2,1)} %pad.4.patches, s32[6]{0:T(128)} %labels.1, s32[1]{0:T(128)S(6)} %copy.47.counts, f32[192,384]{1,0:T(8,128)} %refs_5_.1, ...), custom_call_target="tpu_custom_call" | custom-call | flops 24000000000 | bytes 30000000 | tf_op jit(solution)/shard_map/train_step/pallas_call | solution.py:1422
  187.4 21.3 %adamw.1 = (f32[1,1]{1,0:T(1,128)}, f32[1,1]{1,0:T(1,128)}, f32[192,384]{1,0:T(8,128)}, f32[192,384]{1,0:T(8,128)}, f32[192,384]{1,0:T(8,128)}, /*index=5*/f32[3...) custom-call(bf16[6,384,384]{2,1,0:T(8,128)(2,1)} %get-tuple-element., ...), custom_call_target="tpu_custom_call" | custom-call | flops 200000000 | bytes 50000000 | tf_op jit(solution)/shard_map/adamw/pallas_call | solution.py:1722

commit v6 on v5

--- a/solution.py
+++ b/solution.py
@@ -97,6 +97,53 @@
 
 def pieces(total):
     return [(at, min(STEP, total - at)) for at in range(0, total, STEP)]
+
+
+SCHEDULE = {
+    ("cast", 0): ("ws0",),
+    ("cast", 1): ("ws1",),
+    ("cast", 2): ("ws2",),
+    ("b_start",): ("wf0", "ws3", "wf1", "wr0", "ws4", "we0",),
+    ("embed", 0): ("wf2", "ws5",),
+    ("b_norm", 0, 0): ("wr1", "wf3", "ws6", "we1",),
+    ("norm", 0, 0): ("wr2", "wf4", "ws7",),
+    ("att", 0, 0, 1): ("wr3",),
+    ("mid", 0, 0): ("wf5", "ws8",),
+    ("b_up", 0, 0): ("we2",),
+    ("up", 0, 0): ("wr4", "wf6", "ws9",),
+    ("b_down", 0, 0): ("we3",),
+    ("b_norm", 0, 1): ("wr5", "we4",),
+    ("norm", 0, 1): ("wf7",),
+    ("att", 0, 1, 0): ("wr6",),
+    ("att", 0, 1, 1): ("wf8",),
+    ("b_up", 0, 1): ("we5",),
+    ("up", 0, 1): ("wr7", "wf9",),
+    ("b_down", 0, 1): ("we6",),
+    ("norm", 1, 0): ("wr8",),
+    ("att", 1, 0, 1): ("wr9",),
+    ("b_last",): ("we7", "we8", "we9",),
+    ("class",): ("fc",),
+    ("kv",): ("core6",),
+    ("lb", 1): ("fy",),
+    ("dn", 1): ("y6", "core0",),
+    ("act", 1, 1): ("fz",),
+    ("ups", 1): ("core1", "y0",),
+    ("mlpb", 1, 0): ("x6",),
+    ("attb", 1, 0): ("y1", "z6",),
+    ("attb", 1, 3): ("x0",),
+    ("qkv", 1): ("fx", "core2",),
+    ("dn", 0): ("z0", "y2", "x1", "core3",),
+    ("act", 0, 0): ("gz6", "gx6",),
+    ("mlpb", 0, 0): ("gz0",),
+    ("attb", 0, 0): ("x2", "y3", "core4", "fm",),
+    ("attb", 0, 1): ("gx0",),
+    ("attb", 0, 2): ("z1",),
+    ("attb", 0, 3): ("gd6",),
+    ("fb", 0, 1): ("z2", "fd",),
+    ("emb",): ("x3", "y4", "core5", "gz1", "vc",),
+    ("patch",): ("gd0", "core7",),
+    ("tail",): ("gz2", "z3", "vy", "y7", "gx1", "x4", "y5", "gx2", "vx", "gd1", "gz3", "x7", "z4", "gd2", "gx3", "vz", "x5", "z7", "gz4", "vgz", "gd3", "z5", "gz7", "gx7", "gx4", "gd7", "vgx", "gz5", "qz", "gd4", "vgy", "gx5", "qp", "vgc", "vd", "gd5", "qd",),
+}
 
 
 WFAC = FF + 5 * D
@@ -310,7 +357,7 @@
                     go(make, make(), ag, (unit, index), here.to(x=turn(x, p, n_x)))
             go(make, make(), ag, (unit, base_my + o - 1), mate)
 
-    def weights_ready(unit):
+    def weights_pass(unit):
         kind, layer = units[unit]
         split = parts_of(kind) > 1
         part = x if split else 0
@@ -327,6 +374,11 @@
                         make(), ag_recv.at[unit, base_x + index], ag_send.at[unit, base_x + index]
                     )
                     go(make, make(), ag, (unit, base_mx + index), mate)
+
+    def weights_whole(unit):
+        kind, layer = units[unit]
+        split = parts_of(kind) > 1
+        part = x if split else 0
         arrived(weight(kind, layer, y * 2 + 1 - c), ag_recv.at[unit, 0], ag_send.at[unit, 0])
         for o in range(1, n_y):
             shard = turn(y, n_y - o, n_y) * 2 + 1 - c
@@ -338,6 +390,35 @@
                     piece = weight(kind, layer, shard, turn(x, n_x - p, n_x))
                     arrived(piece, ag_recv.at[unit, index], ag_send.at[unit, index])
 
+    actions = {}
+
+    def perform(names):
+        for name in names:
+            actions[name]()
+
+    def at_place(place, *indices):
+        for key, names in SCHEDULE.items():
+            if key[0] != place:
+                continue
+            held = None
+            for index, value in zip(indices, key[1:], strict=True):
+                if not isinstance(index, int):
+                    same = index == value
+                    held = same if held is None else jnp.logical_and(held, same)
+                elif index != value:
+                    break
+            else:
+                if held is None:
+                    perform(names)
+                else:
+                    pl.when(held)(functools.partial(perform, names))
+
+    for unit in range(len(units)):
+        actions[f"ws{unit}"] = functools.partial(weights_start, unit)
+        actions[f"wf{unit}"] = functools.partial(weights_forward, unit)
+        actions[f"wr{unit}"] = functools.partial(weights_pass, unit)
+        actions[f"we{unit}"] = functools.partial(weights_whole, unit)
+
     lower = here.rep < n_rep // 2
     partner = here.to(z=turn(z, n_z // 2, n_z))
     back_half = pix.at[pl.ds(2, 2)]
@@ -371,12 +452,9 @@
         local_half(1).start()
         lab[1] = marks(1)
 
-    for unit in range(4):
+    for unit in range(len(units)):
         weights_cast(unit)
-        weights_start(unit)
-    weights_forward(0)
-    for unit in range(4, len(units)):
-        weights_cast(unit)
+        at_place("cast", unit)
 
     even = lane_mask(128, 0, 64)
     odd = lane_mask(128, 64, 128)
@@ -488,6 +566,8 @@
             N2[layer, rows, :] = normed.astype(BF)
             I2[layer, rows, :] = jnp.broadcast_to(inverse, (size, 128))
             DXB[rows, :] = (normed * gain + shift).astype(BF)
+        at_place("mid", half, layer)
+        at_place("b_up", half, layer)
         h2 = DXB[whole, :]
         for tile in range(4):
             columns = slice(tile * D, (tile + 1) * D)
@@ -498,24 +578,19 @@
                 active, slope = gelu_parts(made[at : at + size] + bias)
                 ACT[layer, rows, columns] = active.astype(BF)
                 SLOPE[layer, rows, columns] = slope.astype(BF)
+        at_place("up", half, layer)
+        at_place("b_down", half, layer)
         made = mm(ACT[layer, whole, :], wdn[layer])
         bias = vector(layer, 7 * D + FF, D)
         for at, size in pieces(HALF):
             rows = pl.ds(aligned(base + at, 16), size)
             X[rows, :] = X[rows, :] + made[at : at + size] + bias
-
-    def when(condition, *steps):
-        @pl.when(condition)
-        def _():
-            for step, unit in steps:
-                step(unit)
-
-    weights_ready(0)
+        at_place("down", half, layer)
+
+    at_place("b_start")
 
     def forward_half(half, carry):
-        start = half == 0
-
-        @pl.when(start)
+        @pl.when(half == 0)
         def _():
             local_half(0).wait()
 
@@ -528,54 +603,40 @@
             local_half(1).wait()
 
         embed(half)
+        at_place("embed", half)
 
         def forward_layer(layer, inner):
-            first = jnp.logical_and(start, layer == 0)
-            second = jnp.logical_and(start, layer == 1)
-            when(first, (weights_forward, 1), (weights_start, 4), (weights_ready, 1))
-            when(second, (weights_ready, 4))
+            at_place("b_norm", half, layer)
             first_norm(layer, half, (0, 1, 2))
-            when(first, (weights_forward, 2), (weights_start, 5))
-            when(second, (weights_forward, 6), (weights_start, 9))
+            at_place("norm", half, layer)
 
             def attend_one(index, nothing):
                 attend(layer, 2 * half + index)
-                begin = index == 0
-                when(
-                    jnp.logical_and(first, begin), (weights_forward, 3), (weights_start, 6)
-                )
-                when(jnp.logical_and(second, begin), (weights_forward, 7))
+                at_place("att", half, layer, index)
                 return nothing
 
             lax.fori_loop(0, 2, attend_one, 0)
-            when(
-                first, (weights_forward, 4), (weights_start, 7), (weights_ready, 2),
-                (weights_ready, 3),
-            )
-            when(second, (weights_forward, 8), (weights_ready, 5), (weights_ready, 6))
             mlp(layer, half)
-            when(first, (weights_forward, 5), (weights_start, 8))
-            when(second, (weights_forward, 9))
             return inner
 
         return lax.fori_loop(0, LAYERS - 1, forward_layer, carry)
 
     lax.fori_loop(0, 2, forward_half, 0)
-    for unit in (7, 8, 9):
-        weights_ready(unit)
+    at_place("b_last")
 
     last = LAYERS - 1
 
     def last_norm(half, nothing):
         first_norm(last, half, (1, 2))
+        at_place("ln", half)
         return nothing
 
     lax.fori_loop(0, 2, last_norm, 0)
 
     fac = ("f", f_send, f_recv)
-    f_y, f_x = 1, n_y
-    f_z = f_x + n_x - 1
-    f_m = f_z + n_z - 1
+    f_y, f_z = 1, n_y
+    f_x = f_z + n_z - 1
+    f_m = f_x + n_x - 1
     group = KEPT * n_shard
 
     def factors_core():
@@ -587,31 +648,35 @@
         for o in range(1, n_y):
             go(lambda: FAC.at[c], FY.at[o - 1], fac, f_y + o - 1, here.to(y=turn(y, o, n_y)))
 
-    def factors_x():
+    def factors_z():
         total = FAC[c]
         for o in range(1, n_y):
             arrived(FY.at[o - 1], f_recv.at[f_y + o - 1], f_send.at[f_y + o - 1])
             total = total + FY[o - 1]
-        FALL[x] = total
+        FALL[z] = total
+        for o in range(1, n_z):
+            go(
+                lambda: FALL.at[z], FALL.at[z], fac, f_z + o - 1,
+                here.to(z=turn(z, o, n_z)),
+            )
+
+    def factors_x():
+        for o in range(1, n_z):
+            index = f_z + o - 1
+            arrived(FALL.at[turn(z, n_z - o, n_z)], f_recv.at[index], f_send.at[index])
+        pltpu.make_async_copy(FALL, all_factors.at[c, x], out_local.at[0]).start()
         for o in range(1, n_x):
-            go(lambda: FALL.at[x], FALL.at[x], fac, f_x + o - 1, here.to(x=turn(x, o, n_x)))
-
-    def all_rows(at):
-        return all_factors.at[c, pl.ds(at * n_x, n_x)]
-
-    def factors_z():
+            go(
+                lambda: FALL, all_factors.at[c, x], fac, f_x + o - 1,
+                here.to(x=turn(x, o, n_x)),
+            )
+
+    def factors_mate():
         for o in range(1, n_x):
             index = f_x + o - 1
-            arrived(FALL.at[turn(x, n_x - o, n_x)], f_recv.at[index], f_send.at[index])
-        pltpu.make_async_copy(FALL, all_rows(z), out_local.at[0]).start()
-        for o in range(1, n_z):
-            go(lambda: FALL, all_rows(z), fac, f_z + o - 1, here.to(z=turn(z, o, n_z)))
-
-    def factors_mate():
-        for o in range(1, n_z):
-            index = f_z + o - 1
-            arrived(all_rows(turn(z, n_z - o, n_z)), f_recv.at[index], f_send.at[index])
-        pltpu.make_async_copy(FALL, all_rows(z), out_local.at[0]).wait()
+            came = all_factors.at[c, turn(x, n_x - o, n_x)]
+            arrived(came, f_recv.at[index], f_send.at[index])
+        pltpu.make_async_copy(FALL, all_factors.at[c, x], out_local.at[0]).wait()
         go(lambda: all_factors.at[c], all_factors.at[c], fac, f_m, mate)
 
     def factors_done():
@@ -802,6 +867,19 @@
                     rs_recv.at[k, r_gx + o - 1], rs_send.at[k, r_gx + o - 1],
                 )
         result(k).start()
+
+    for k in range(CHUNKS + 2):
+        actions[f"core{k}"] = functools.partial(reduce_core, k)
+        actions[f"y{k}"] = functools.partial(reduce_y, k)
+        actions[f"x{k}"] = functools.partial(reduce_x, k)
+        actions[f"z{k}"] = functools.partial(reduce_z, k)
+        actions[f"gz{k}"] = functools.partial(gather_z, k)
+        actions[f"gx{k}"] = functools.partial(gather_x, k)
+        actions[f"gd{k}"] = functools.partial(gather_done, k)
+    actions.update(
+        fc=factors_core, fy=factors_y, fz=factors_z, fx=factors_x, fm=factors_mate,
+        fd=factors_done,
+    )
 
     def tails(ref, layer=None):
         found = []
@@ -912,7 +990,7 @@
         FAC[1, :, at : at + piece.shape[-1]] = mm(pick, piece).astype(BF)
         at += piece.shape[-1]
     FAC[1, :, at:] = jnp.zeros((group, WFAC - at), BF)
-    factors_core()
+    at_place("class")
 
     turned = DXB[...].T
     for tile, grads in enumerate((DMB, DA)):
@@ -921,8 +999,7 @@
             GS[0, shard // 2, shard % 2, tile * rows_in : (tile + 1) * rows_in, :] = made[
                 shard * rows_in : (shard + 1) * rows_in
             ]
-    reduce_core(CHUNKS)
-    factors_y()
+    at_place("kv")
     store_sums(last, [(3 * D, fold(DA[...].astype(F32)))])
 
     X[...] = jnp.zeros((ROWS, D), F32)
@@ -956,12 +1033,12 @@
         rows = pl.ds(aligned(half * HALF, 16), HALF)
         made = mm_nt(DMB[rows, :], win[last, :, D : 2 * D])
         made = made + mm_nt(DA[rows, :], win[last, :, 2 * D : 3 * D])
-        return first_back(last, half, made, sums)
+        sums = first_back(last, half, made, sums)
+        at_place("lb", half)
+        return sums
 
     gain_sum, shift_sum = lax.fori_loop(0, 2, last_back, (gain_sum, shift_sum))
     store_sums(last, [(0, gain_sum), (D, shift_sum)])
-    reduce_y(CHUNKS)
-    factors_x()
 
     def round_up(half, total):
         for at, size in pieces(HALF):
@@ -1071,15 +1148,8 @@
     def backward(step, carry):
         layer = LAYERS - 2 - step
         kd, ku, kq = 3 * step, 3 * step + 1, 3 * step + 2
-        upper_layer, bottom = step == 0, step == 1
-
         bias_down = lax.fori_loop(0, 2, round_up, zeros)
-        when(upper_layer, (reduce_x, CHUNKS))
-
-        @pl.when(upper_layer)
-        def _():
-            factors_z()
-
+        at_place("round", layer)
         turned = DXB[...].T
         per = min(rows_down, D)
         for tile in range(4):
@@ -1090,49 +1160,36 @@
                 G[kd, shard // 2, shard % 2, at : at + per, :] = made[
                     piece * per : (piece + 1) * per
                 ]
-        when(upper_layer, (reduce_core, 0))
-        when(bottom, (reduce_core, 3), (gather_z, CHUNKS))
+        at_place("dn", layer)
 
         def one(half, totals):
-            return act_back(layer, half, totals)
+            totals = act_back(layer, half, totals)
+            at_place("act", layer, half)
+            return totals
 
         bias_up = lax.fori_loop(0, 2, one, (zeros,) * 4)
-        when(upper_layer, (reduce_y, 0))
-        when(bottom, (reduce_x, 2), (reduce_y, 3), (reduce_z, 1))
         turned = renew(N2, layer, 5 * D)
         for tile in range(4):
             keep_in(ku, tile, mm(turned, DH[:, tile * D : (tile + 1) * D]).astype(BF))
-        when(upper_layer, (reduce_core, 1))
-        when(bottom, (reduce_core, 4), (gather_z, 0), (gather_x, CHUNKS))
+        at_place("ups", layer)
 
         def one_more(half, sums):
-            return mlp_back(layer, half, sums)
+            sums = mlp_back(layer, half, sums)
+            at_place("mlpb", layer, half)
+            return sums
 
         gain_sum, shift_sum, bias_out = lax.fori_loop(0, 2, one_more, (zeros, zeros, zeros))
-        when(upper_layer, (reduce_y, 1), (reduce_z, CHUNKS))
-        when(bottom, (reduce_y, 4), (reduce_z, 2), (gather_z, 1))
         store_sums(
             layer,
             [(7 * D + FF, bias_down), (5 * D, gain_sum), (6 * D, shift_sum), (4 * D, bias_out)]
             + [(7 * D + tile * D, bias_up[tile]) for tile in range(4)],
         )
         keep_in(kq, 3, mm(ATT[layer].T, DMB[...]).astype(BF))
+        at_place("out", layer)
 
         def two(image, nothing):
             attend_back(layer, image)
-            when(jnp.logical_and(upper_layer, image == 0), (reduce_x, 0))
-            when(jnp.logical_and(upper_layer, image == 2), (reduce_x, 1))
-            when(jnp.logical_and(upper_layer, image == 3), (reduce_z, 0))
-
-            @pl.when(jnp.logical_and(bottom, image == 0))
-            def _():
-                factors_mate()
-                gather_done(CHUNKS)
-                gather_x(0)
-
-            when(jnp.logical_and(bottom, image == 1), (reduce_x, 3), (gather_z, 2))
-            when(jnp.logical_and(bottom, image == 2), (gather_x, 1), (reduce_z, 3))
-            when(jnp.logical_and(bottom, image == 3), (reduce_x, 4), (gather_x, 2), (gather_done, 0))
+            at_place("attb", layer, image)
             return nothing
 
         lax.fori_loop(0, KEPT, two, 0)
@@ -1141,8 +1198,7 @@
             keep_in(
                 kq, tile, mm(turned, DH[:, tile * D : (tile + 1) * D]).astype(BF)
             )
-        when(upper_layer, (reduce_core, 2))
-        when(bottom, (reduce_core, 5), (gather_z, 3))
+        at_place("qkv", layer)
         store_sums(
             layer,
             [
@@ -1154,12 +1210,12 @@
         def three(half, sums):
             rows = pl.ds(aligned(half * HALF, 16), HALF)
             made = mm_nt(DH[rows, 0 : 3 * D], win[layer, :, 0 : 3 * D])
-            return first_back(layer, half, made, sums)
+            sums = first_back(layer, half, made, sums)
+            at_place("fb", layer, half)
+            return sums
 
         gain_sum, shift_sum = lax.fori_loop(0, 2, three, (zeros, zeros))
         store_sums(layer, [(0, gain_sum), (D, shift_sum)])
-        when(upper_layer, (reduce_y, 2))
-        when(bottom, (reduce_y, 5), (reduce_z, 4), (gather_done, 1))
         return carry
 
     lax.fori_loop(0, LAYERS - 1, backward, 0)
@@ -1322,7 +1378,12 @@
     def vectors_done():
         arrived(vrows(VF, (1 - c) * rows_c, rows_c), v_recv.at[v_gc], v_send.at[v_gc])
 
-    vectors_core()
+    actions.update(
+        vc=vectors_core, vy=vectors_y, vx=vectors_x, vz=vectors_z, vgz=vectors_gather_z,
+        vgx=vectors_gather_x, vgy=vectors_gather_y, vgc=vectors_gather_core, vd=vectors_done,
+        qz=squares_z, qp=squares_plane, qd=squares_done,
+    )
+    at_place("emb")
     low = DXB[...]
     for tile in range(2):
         made = mm_tn(pix[:, :, tile * D : (tile + 1) * D].reshape(ROWS, D), low).astype(BF)
@@ -1330,37 +1391,8 @@
             shard = tile * (D // rows_patch) + piece
             GS[1, shard // 2, shard % 2] = made[piece * rows_patch : (piece + 1) * rows_patch]
 
-    kp = CHUNKS + 1
-    reduce_core(kp)
-    vectors_y()
-    gather_done(2)
-    gather_x(3)
-    reduce_y(kp)
-    vectors_x()
-    gather_z(4)
-    reduce_x(5)
-    vectors_z()
-    reduce_x(kp)
-    gather_x(4)
-    vectors_gather_z()
-    reduce_z(5)
-    reduce_z(kp)
-    vectors_gather_x()
-    gather_done(3)
-    gather_z(5)
-    vectors_gather_y()
-    gather_done(4)
-    gather_x(5)
-    gather_z(kp)
-    squares_z()
-    gather_x(kp)
-    vectors_gather_core()
-    factors_done()
-    squares_plane()
-    vectors_done()
-    gather_done(5)
-    gather_done(kp)
-    squares_done()
+    at_place("patch")
+    at_place("tail")
     last_copies = [
         pltpu.make_async_copy(VF, vec_out, out_local.at[1 + CHUNKS + 2]),
         pltpu.make_async_copy(SQ.at[2], square_out, out_local.at[2 + CHUNKS + 2]),
@@ -1426,7 +1458,7 @@
             jax.ShapeDtypeStruct((2, block // 2, D), BF),
             jax.ShapeDtypeStruct((VEC_ROWS, VEC_WIDE), F32),
             jax.ShapeDtypeStruct((8, 128), F32),
-            jax.ShapeDtypeStruct((2, n_rep, group, WFAC), BF),
+            jax.ShapeDtypeStruct((2, n_x, n_z, group, WFAC), BF),
         ],
         in_specs=[there] + [pl.BlockSpec(memory_space=pltpu.SMEM)] * 2 + [there] * 3 + [whole] * 4,
         out_specs=[there] * 5,
@@ -1457,7 +1489,7 @@
             buf(2, group, WFAC),
             buf(group, WFAC),
             buf(n_y - 1, group, WFAC),
-            buf(n_x, group, WFAC),
+            buf(n_z, group, WFAC),
             buf(VEC_ROWS, VEC_WIDE, dtype=F32),
             buf(VEC_ROWS // 2, VEC_WIDE, dtype=F32),
             buf(n_y - 1, rows_y, VEC_WIDE, dtype=F32),
@@ -1539,10 +1571,10 @@
         for move in moves(array, layer):
             move.start()
 
-    n_rows = factors.shape[1] * factors.shape[2]
+    n_rows = factors.shape[1] * factors.shape[2] * factors.shape[3]
 
     def factor(half, at, size):
-        return factors[half, :, :, at : at + size].reshape(n_rows, size)
+        return factors[half, :, :, :, at : at + size].reshape(n_rows, size)
 
     def squares(values):
         return fold(values * values)

time: 209 us -> 187 us (0.89)
  Pallas kernels: 205 us -> 183 us
    pallas_call x1, Pallas kernels: 183 us -> 161 us  [run_train(): pl.pallas_call(functools.partial(train, n_rep, n_shard), out_shape=[jax.S...]
where the time goes in v6:
time: 187 us
  Pallas kernels  183 us (98%)
  local copies, waits for them, and re-layouts  2.89 us (2%)
    pallas_call x1, Pallas kernels, run_train(): pl.pallas_call(functools.partial(train, n_rep, n_shard), out_shape=[jax.S...  161 us
    pallas_call x1, Pallas kernels, run_update(): pl.pallas_call(functools.partial(update, n_rep, n_shard), out_shape=[one,...  21.3 us

profile of v6, /device:TPU:0, one launch (start us, length us, event | category | flops | bytes accessed | tf_op | source)
XLA Modules:
  0.0 187.1 jit_solution(16365916136857091314)
XLA Ops:
  1.3 2.9 %pad.4.patches = bf16[6,208,768]{2,1,0:T(8,128)(2,1)} pad(bf16[6,196,768]{2,1,0:T(8,128)(2,1)} %param.24, bf16[]{:T(256)} %constant.2.clone.1), padding=0_0x0_12x0_0 | pad | bytes 3723266 | tf_op jit(solution)/shard_map/jit(_pad)/pad | solution.py:1783
  4.2 161.5 %train_step.1 = (bf16[6,384,384]{2,1,0:T(8,128)(2,1)}, bf16[2,192,384]{2,1,0:T(8,128)(2,1)}, f32[256,384]{1,0:T(8,128)}, f32[8,128]{1,0:T(8,128)}, bf16[2,2,4,16,3456]{4,3,2,1,0:T(8,128)(2,1)}) custom-call(bf16[6,208,768]{2,1,0:T(8,128)(2,1)} %pad.4.patches, s32[6]{0:T(128)} %labels.1, s32[1]{0:T(128)S(6)} %copy.47.counts, f32[192,384]{1,0:T(8,128)} %refs_5_.1, ...), custom_call_target="tpu_custom_call" | custom-call | flops 24000000000 | bytes 30000000 | tf_op jit(solution)/shard_map/train_step/pallas_call | solution.py:1454
  165.7 21.3 %adamw.1 = (f32[1,1]{1,0:T(1,128)}, f32[1,1]{1,0:T(1,128)}, f32[192,384]{1,0:T(8,128)}, f32[192,384]{1,0:T(8,128)}, f32[192,384]{1,0:T(8,128)}, /*index=5*/f32[3...) custom-call(bf16[6,384,384]{2,1,0:T(8,128)(2,1)} %get-tuple-element., ...), custom_call_target="tpu_custom_call" | custom-call | flops 200000000 | bytes 50000000 | tf_op jit(solution)/shard_map/adamw/pallas_call | solution.py:1754

commit v7 on v6

--- a/solution.py
+++ b/solution.py
@@ -128,21 +128,23 @@
     ("dn", 1): ("y6", "core0",),
     ("act", 1, 1): ("fz",),
     ("ups", 1): ("core1", "y0",),
-    ("mlpb", 1, 0): ("x6",),
-    ("attb", 1, 0): ("y1", "z6",),
+    ("mlpb", 1, 1): ("x6",),
+    ("attb", 1, 0): ("y1",),
+    ("attb", 1, 2): ("z6",),
     ("attb", 1, 3): ("x0",),
     ("qkv", 1): ("fx", "core2",),
-    ("dn", 0): ("z0", "y2", "x1", "core3",),
-    ("act", 0, 0): ("gz6", "gx6",),
+    ("fb", 1, 1): ("gz6",),
+    ("dn", 0): ("y2", "x1", "z0", "core3",),
+    ("act", 0, 0): ("gx6",),
     ("mlpb", 0, 0): ("gz0",),
     ("attb", 0, 0): ("x2", "y3", "core4", "fm",),
     ("attb", 0, 1): ("gx0",),
     ("attb", 0, 2): ("z1",),
-    ("attb", 0, 3): ("gd6",),
-    ("fb", 0, 1): ("z2", "fd",),
-    ("emb",): ("x3", "y4", "core5", "gz1", "vc",),
-    ("patch",): ("gd0", "core7",),
-    ("tail",): ("gz2", "z3", "vy", "y7", "gx1", "x4", "y5", "gx2", "vx", "gd1", "gz3", "x7", "z4", "gd2", "gx3", "vz", "x5", "z7", "gz4", "vgz", "gd3", "z5", "gz7", "gx7", "gx4", "gd7", "vgx", "gz5", "qz", "gd4", "vgy", "gx5", "qp", "vgc", "vd", "gd5", "qd",),
+    ("qkv", 0): ("gd6",),
+    ("fb", 0, 1): ("fd",),
+    ("emb",): ("z2", "x3", "y4", "core5", "gz1", "vc",),
+    ("patch",): ("core7",),
+    ("tail",): ("gd0", "gz2", "vy", "z3", "y7", "gx1", "x4", "y5", "vx", "gx2", "gd1", "gz3", "x7", "z4", "vz", "gx3", "gd2", "x5", "z7", "gz4", "vgz", "gd3", "gz7", "z5", "gx4", "vgx", "gx7", "gd4", "vgy", "gz5", "qz", "gd7", "vgc", "gx5", "qp", "vd", "gd5", "qd",),
 }
 
 
@@ -177,13 +179,19 @@
     return parts if rows % (parts * unit) == 0 else 1
 
 
+def small_rows(rows, n_x, n_z):
+    unit = 16 * n_x * n_z
+    padded = -(-rows // unit) * unit
+    return padded if 2 * padded <= 3 * rows else rows
+
+
 def aligned(value, unit):
     return pl.multiple_of(value, unit)
 
 
 def train(
     n_rep, n_shard,
-    patches, labels, counts, own_patch, own_in, own_down, vecs, glob, pos, head,
+    patches, patch_ends, labels, counts, own_patch, own_in, own_down, vecs, glob, pos, head,
     res_out, small_out, vec_out, square_out, all_factors,
     X, N1, I1, QKV, ATT, N2, I2, ACT, SLOPE, DXB, DMB, DA, DH,
     pix, lab, lab_given, wp, win, wdn, low_head, head_bias,
@@ -198,6 +206,7 @@
     x, y, z, c = here.x, here.y, here.z, here.c
     rows_in, rows_down, rows_patch = D // n_shard, FF // n_shard, PATCH_DIM // n_shard
     block = 4 * rows_in
+    small_block = small_rows(block // 2, n_x, n_z)
     mate = here.to(c=1 - c)
 
     def push(src, dst, send, recv, device):
@@ -421,12 +430,22 @@
 
     lower = here.rep < n_rep // 2
     partner = here.to(z=turn(z, n_z // 2, n_z))
-    back_half = pix.at[pl.ds(2, 2)]
-    given = patches.at[pl.ds(KEPT, 2)]
+    back_parts = (
+        pix.at[pl.ds(2, 2), pl.ds(0, TAIL)], pix.at[pl.ds(2, 2), pl.ds(TAIL, BLK - TAIL)]
+    )
+    given = (patches.at[pl.ds(KEPT, 2), pl.ds(0, TAIL)], patch_ends.at[pl.ds(KEPT, 2)])
 
     def local_half(half):
-        return pltpu.make_async_copy(
-            patches.at[pl.ds(2 * half, 2)], pix.at[pl.ds(2 * half, 2)], img_local.at[half]
+        pair = pl.ds(2 * half, 2)
+        return (
+            pltpu.make_async_copy(
+                patches.at[pair, pl.ds(0, TAIL)], pix.at[pair, pl.ds(0, TAIL)],
+                img_local.at[half],
+            ),
+            pltpu.make_async_copy(
+                patch_ends.at[pair], pix.at[pair, pl.ds(TAIL, BLK - TAIL)],
+                img_local.at[2 + half],
+            ),
         )
 
     def marks(pair):
@@ -438,7 +457,8 @@
             found = jnp.where(row == CLS - TAIL + 16 * index, value, found)
         return found
 
-    local_half(0).start()
+    for copy in local_half(0):
+        copy.start()
     for unit in range(2):
         for copy in weights_copies(unit):
             copy.start()
@@ -447,9 +467,14 @@
 
     @pl.when(jnp.logical_not(lower))
     def _():
-        push(given, back_half, img_send.at[0], img_recv.at[0], partner)
-        push(lab_given, lab.at[1], img_send.at[1], img_recv.at[1], partner)
-        local_half(1).start()
+        for index in range(2):
+            push(
+                given[index], back_parts[index], img_send.at[index], img_recv.at[index],
+                partner,
+            )
+        push(lab_given, lab.at[1], img_send.at[2], img_recv.at[2], partner)
+        for copy in local_half(1):
+            copy.start()
         lab[1] = marks(1)
 
     for unit in range(len(units)):
@@ -471,6 +496,9 @@
     head_bias[:, 0:NCLS] = head[D : D + 1, :]
     V[...] = jnp.zeros((VEC_ROWS, VEC_WIDE), F32)
     square_sum[...] = jnp.zeros((8, 128), F32)
+    if small_block > block // 2:
+        spare = small_block - block // 2
+        GS[:, :, :, block // 2 :, :] = jnp.zeros((2, n_y, 2, spare, D), BF)
     zeros = jnp.zeros((8, D), F32)
     patch_bias = glob[0:1, :]
 
@@ -519,16 +547,16 @@
             DXB[rows, :] = (normed * gain + shift).astype(BF)
         rows = pl.ds(aligned(base, 16), HALF)
         h1 = DXB[rows, :]
-        for tile in columns:
-            made = mm(h1, win[layer, :, tile * D : (tile + 1) * D])
-            if tile == 0:
-                made = made + vector(layer, 2 * D, D)
-            if tile == 2:
-                made = made + vector(layer, 3 * D, D)
-            if len(columns) == 3:
-                QKV[layer, rows, tile * D : (tile + 1) * D] = made.astype(BF)
-            else:
-                (DMB if tile == 1 else DA)[rows, :] = made.astype(BF)
+        if len(columns) == 3:
+            made = mm(h1, win[layer, :, 0 : 2 * D])
+            QKV[layer, rows, 0:D] = (made[:, 0:D] + vector(layer, 2 * D, D)).astype(BF)
+            QKV[layer, rows, D : 2 * D] = made[:, D:].astype(BF)
+            made = mm(h1, win[layer, :, 2 * D : 3 * D])
+            QKV[layer, rows, 2 * D :] = (made + vector(layer, 3 * D, D)).astype(BF)
+        else:
+            made = mm(h1, win[layer, :, D : 3 * D])
+            DMB[rows, :] = made[:, 0:D].astype(BF)
+            DA[rows, :] = (made[:, D:] + vector(layer, 3 * D, D)).astype(BF)
 
     ones = jnp.full((BLK, 128), 1.0, BF)
 
@@ -569,15 +597,19 @@
         at_place("mid", half, layer)
         at_place("b_up", half, layer)
         h2 = DXB[whole, :]
-        for tile in range(4):
-            columns = slice(tile * D, (tile + 1) * D)
-            made = mm(h2, win[layer, :, (4 + tile) * D : (5 + tile) * D])
-            bias = vector(layer, 7 * D + tile * D, D)
-            for at, size in pieces(HALF):
-                rows = pl.ds(aligned(base + at, 16), size)
-                active, slope = gelu_parts(made[at : at + size] + bias)
-                ACT[layer, rows, columns] = active.astype(BF)
-                SLOPE[layer, rows, columns] = slope.astype(BF)
+        for pair in range(2):
+            made = mm(h2, win[layer, :, (4 + 2 * pair) * D : (6 + 2 * pair) * D])
+            for tile in range(2):
+                start = (2 * pair + tile) * D
+                columns = slice(start, start + D)
+                bias = vector(layer, 7 * D + start, D)
+                for at, size in pieces(HALF):
+                    rows = pl.ds(aligned(base + at, 16), size)
+                    active, slope = gelu_parts(
+                        made[at : at + size, tile * D : (tile + 1) * D] + bias
+                    )
+                    ACT[layer, rows, columns] = active.astype(BF)
+                    SLOPE[layer, rows, columns] = slope.astype(BF)
         at_place("up", half, layer)
         at_place("b_down", half, layer)
         made = mm(ACT[layer, whole, :], wdn[layer])
@@ -592,15 +624,18 @@
     def forward_half(half, carry):
         @pl.when(half == 0)
         def _():
-            local_half(0).wait()
+            for copy in local_half(0):
+                copy.wait()
 
         @pl.when(jnp.logical_and(half == 1, lower))
         def _():
-            arrived(back_half, img_recv.at[0], img_send.at[0])
+            for index in range(2):
+                arrived(back_parts[index], img_recv.at[index], img_send.at[index])
 
         @pl.when(jnp.logical_and(half == 1, jnp.logical_not(lower)))
         def _():
-            local_half(1).wait()
+            for copy in local_half(1):
+                copy.wait()
 
         embed(half)
         at_place("embed", half)
@@ -695,15 +730,18 @@
                 G.at[k], RC.at[slot], RY.at[slot], RX.at[slot], RZ.at[slot], RES.at[k], block
             )
         k = k - CHUNKS
-        return GS.at[k], SC.at[0], SY.at[0], SX.at[0], SZ.at[0], SRES.at[k], block // 2
+        return GS.at[k], SC.at[0], SY.at[0], SX.at[0], SZ.at[0], SRES.at[k], small_block
 
     def splits(rows):
         by_x = cut(rows, n_x, 16)
         by_z = cut(rows // by_x, n_z, 16)
         return by_x, rows // by_x, by_z, rows // by_x // by_z
 
+    def step_of(rows, most=192):
+        return max(step for step in range(16, most + 1, 16) if rows % step == 0)
+
     def add_rows(rows, target, target_at, sources):
-        step = 48 if rows % 48 == 0 else 16
+        step = step_of(rows)
 
         def one(index, nothing):
             at = index * step
@@ -778,7 +816,7 @@
             rx[x] = mine[...]
             for o in range(1, n_x):
                 gone(rs, (k, r_x + o - 1))
-            step = 48 if rows % 48 == 0 else 16
+            step = step_of(rows)
 
             def one(index, nothing):
                 at = pl.ds(aligned(index * step, 16), step)
@@ -809,7 +847,7 @@
         own_slot = n_z - 1 if by_z > 1 else z
         rz[own_slot] = g[y, c, pl.ds(aligned(start, 16), rows_z), :]
         share = 1.0 / ((1 if by_x > 1 else n_x) * (1 if by_z > 1 else n_z))
-        step = 48 if rows_z % 48 == 0 else 16
+        step = step_of(rows_z, 96)
 
         def one(index, total):
             low = total_of(rz, n_z, index * step, step).astype(BF)
@@ -890,7 +928,7 @@
 
     @pl.when(lower)
     def _():
-        arrived(lab.at[1], img_recv.at[1], img_send.at[1])
+        arrived(lab.at[1], img_recv.at[2], img_send.at[2])
 
     marked = lab[...].reshape(CROWS, 128)[:, 0:1]
 
@@ -1052,16 +1090,19 @@
         base = half * HALF
         low = DXB[pl.ds(aligned(base, 16), HALF), :]
         ups = []
-        for tile in range(4):
-            columns = slice(tile * D, (tile + 1) * D)
-            made = mm_nt(low, wdn[layer, columns, :])
-            total = totals[tile]
-            for at, size in pieces(HALF):
-                rows = pl.ds(aligned(base + at, 16), size)
-                grad = (made[at : at + size] * SLOPE[layer, rows, columns].astype(F32)).astype(BF)
-                DH[rows, columns] = grad
-                total = total + fold(grad.astype(F32))
-            ups.append(total)
+        for pair in range(2):
+            made = mm_nt(low, wdn[layer, 2 * pair * D : 2 * (pair + 1) * D, :])
+            for tile in range(2):
+                start = (2 * pair + tile) * D
+                columns = slice(start, start + D)
+                total = totals[2 * pair + tile]
+                for at, size in pieces(HALF):
+                    rows = pl.ds(aligned(base + at, 16), size)
+                    part = made[at : at + size, tile * D : (tile + 1) * D]
+                    grad = (part * SLOPE[layer, rows, columns].astype(F32)).astype(BF)
+                    DH[rows, columns] = grad
+                    total = total + fold(grad.astype(F32))
+                ups.append(total)
         return tuple(ups)
 
     def mlp_back(layer, half, sums):
@@ -1132,11 +1173,12 @@
         gain, shift = vector(layer, at, D), vector(layer, at + D, D)
 
         def one(index, nothing):
-            rows = pl.ds(aligned(index * 64, 16), 64)
-            DXB[rows, :] = (ref[layer, rows, :].astype(F32) * gain + shift).astype(BF)
+            for at, size in pieces(BLK):
+                rows = pl.ds(aligned(index * BLK + at, 16), size)
+                DXB[rows, :] = (ref[layer, rows, :].astype(F32) * gain + shift).astype(BF)
             return nothing
 
-        lax.fori_loop(0, ROWS // 64, one, 0)
+        lax.fori_loop(0, KEPT, one, 0)
         return DXB[...].T
 
     def keep_in(k, tile, made):
@@ -1152,14 +1194,16 @@
         at_place("round", layer)
         turned = DXB[...].T
         per = min(rows_down, D)
-        for tile in range(4):
-            columns = slice(tile * D, (tile + 1) * D)
-            made = mm(turned, ACT[layer, :, columns]).astype(BF).T
-            for piece in range(D // per):
-                shard, at = divmod(tile * D + piece * per, rows_down)
-                G[kd, shard // 2, shard % 2, at : at + per, :] = made[
-                    piece * per : (piece + 1) * per
-                ]
+        for pair in range(2):
+            start = 2 * pair * D
+            wide = mm(turned, ACT[layer, :, start : start + 2 * D]).astype(BF)
+            for tile in range(2):
+                made = wide[:, tile * D : (tile + 1) * D].T
+                for piece in range(D // per):
+                    shard, at = divmod(start + tile * D + piece * per, rows_down)
+                    G[kd, shard // 2, shard % 2, at : at + per, :] = made[
+                        piece * per : (piece + 1) * per
+                    ]
         at_place("dn", layer)
 
         def one(half, totals):
@@ -1169,8 +1213,10 @@
 
         bias_up = lax.fori_loop(0, 2, one, (zeros,) * 4)
         turned = renew(N2, layer, 5 * D)
-        for tile in range(4):
-            keep_in(ku, tile, mm(turned, DH[:, tile * D : (tile + 1) * D]).astype(BF))
+        for pair in range(2):
+            made = mm(turned, DH[:, 2 * pair * D : 2 * (pair + 1) * D]).astype(BF)
+            keep_in(ku, 2 * pair, made[:, :D])
+            keep_in(ku, 2 * pair + 1, made[:, D:])
         at_place("ups", layer)
 
         def one_more(half, sums):
@@ -1194,10 +1240,10 @@
 
         lax.fori_loop(0, KEPT, two, 0)
         turned = renew(N1, layer, 0)
-        for tile in range(3):
-            keep_in(
-                kq, tile, mm(turned, DH[:, tile * D : (tile + 1) * D]).astype(BF)
-            )
+        made = mm(turned, DH[:, 0 : 2 * D]).astype(BF)
+        keep_in(kq, 0, made[:, :D])
+        keep_in(kq, 1, made[:, D:])
+        keep_in(kq, 2, mm(turned, DH[:, 2 * D : 3 * D]).astype(BF))
         at_place("qkv", layer)
         store_sums(
             layer,
@@ -1389,10 +1435,19 @@
         made = mm_tn(pix[:, :, tile * D : (tile + 1) * D].reshape(ROWS, D), low).astype(BF)
         for piece in range(D // rows_patch):
             shard = tile * (D // rows_patch) + piece
-            GS[1, shard // 2, shard % 2] = made[piece * rows_patch : (piece + 1) * rows_patch]
+            GS[1, shard // 2, shard % 2, 0:rows_patch, :] = made[piece * rows_patch : (piece + 1) * rows_patch]
 
     at_place("patch")
-    at_place("tail")
+    ending = SCHEDULE["tail",]
+    perform(ending[:-6])
+    early = [
+        key for key in sent
+        if key[0] in ("ag", "f") or (key[0] == "rs" and key[1][0] not in (4, 5, 7))
+    ]
+    for key in early:
+        source, send, recv, at = sent.pop(key)
+        left_here(source(), recv.at[at], send.at[at])
+    perform(ending[-6:])
     last_copies = [
         pltpu.make_async_copy(VF, vec_out, out_local.at[1 + CHUNKS + 2]),
         pltpu.make_async_copy(SQ.at[2], square_out, out_local.at[2 + CHUNKS + 2]),
@@ -1408,16 +1463,18 @@
 
     @pl.when(jnp.logical_not(lower))
     def _():
-        left_here(given, img_recv.at[0], img_send.at[0])
-        left_here(lab_given, img_recv.at[1], img_send.at[1])
+        for index in range(2):
+            left_here(given[index], img_recv.at[index], img_send.at[index])
+        left_here(lab_given, img_recv.at[2], img_send.at[2])
 
 
 def run_train(
-    n_rep, n_shard, patches, labels, counts, own_patch, own_in, own_down, vecs, glob, pos, head
+    n_rep, n_shard, patches, patch_ends, labels, counts, own_patch, own_in, own_down, vecs, glob, pos, head
 ):
     n_x = 2 ** ((n_rep.bit_length() - 2) // 2)
     n_z, n_y = n_rep // n_x, n_shard // 2
     block = 4 * (D // n_shard)
+    small_block = small_rows(block // 2, n_x, n_z)
     group = KEPT * n_shard
     keep = LAYERS - 1
     units = 1 + 3 * LAYERS
@@ -1455,12 +1512,12 @@
         functools.partial(train, n_rep, n_shard),
         out_shape=[
             jax.ShapeDtypeStruct((CHUNKS, block, D), BF),
-            jax.ShapeDtypeStruct((2, block // 2, D), BF),
+            jax.ShapeDtypeStruct((2, small_block, D), BF),
             jax.ShapeDtypeStruct((VEC_ROWS, VEC_WIDE), F32),
             jax.ShapeDtypeStruct((8, 128), F32),
             jax.ShapeDtypeStruct((2, n_x, n_z, group, WFAC), BF),
         ],
-        in_specs=[there] + [pl.BlockSpec(memory_space=pltpu.SMEM)] * 2 + [there] * 3 + [whole] * 4,
+        in_specs=[there] * 2 + [pl.BlockSpec(memory_space=pltpu.SMEM)] * 2 + [there] * 3 + [whole] * 4,
         out_specs=[there] * 5,
         scratch_shapes=[
             buf(ROWS, D, dtype=F32),
@@ -1485,7 +1542,7 @@
             buf(D, CPAD),
             buf(1, CPAD, dtype=F32),
             *reduction(CHUNKS, 3, block),
-            *reduction(2, 1, block // 2),
+            *reduction(2, 1, small_block),
             buf(2, group, WFAC),
             buf(group, WFAC),
             buf(n_y - 1, group, WFAC),
@@ -1511,8 +1568,8 @@
             sems(v_count),
             sems(q_count),
             sems(q_count),
-            sems(2),
-            sems(2),
+            sems(3),
+            sems(3),
             sems(4),
             sems(3 + chunks),
         ],
@@ -1523,7 +1580,7 @@
             flops=24_000_000_000, bytes_accessed=30_000_000, transcendentals=10_000_000
         ),
         name="train_step",
-    )(patches, labels, counts, own_patch, own_in, own_down, vecs, glob, pos, head)
+    )(patches, patch_ends, labels, counts, own_patch, own_in, own_down, vecs, glob, pos, head)
 
 
 def adam(weight, first, second, grad, factor, rate):
@@ -1780,9 +1837,9 @@
     m_patch, v_patch, m_in, v_in, m_down, v_down, m_vecs, v_vecs, m_glob, v_glob, m_pos, v_pos,
     m_head, v_head,
 ):
-    padded = jnp.pad(patches, ((0, 0), (0, BLK - PATCHES), (0, 0)))
+    ends = jnp.pad(patches[:, TAIL:], ((0, 0), (0, BLK - PATCHES), (0, 0)))
     res, small, vec, squares, factors = run_train(
-        n_rep, n_shard, padded, labels, counts, patch_w, layer_in, layer_down, layer_vecs,
+        n_rep, n_shard, patches, ends, labels, counts, patch_w, layer_in, layer_down, layer_vecs,
         glob_vecs, pos_embed, head,
     )
     arrays = [

time: 187 us -> 182 us (0.973)
  Pallas kernels: 183 us -> 178 us
    pallas_call x1, Pallas kernels: 161 us -> 157 us  [run_train(): pl.pallas_call(functools.partial(train, n_rep, n_shard), out_shape=[jax.S...]
    pad x1, local copies, waits for them, and re-layouts: 2.89 us -> 0.68 us  [shards(): ends = jnp.pad(patches[:, TAIL:], ((0, 0), (0, BLK - PATCHES), (0, 0)))]
where the time goes in v7:
time: 182 us; the launch traced here: 181 us
  Pallas kernels  178 us (98%)
    pallas_call x1, Pallas kernels, run_train(): pl.pallas_call(functools.partial(train, n_rep, n_shard), out_shape=[jax.S...  157 us
    pallas_call x1, Pallas kernels, run_update(): pl.pallas_call(functools.partial(update, n_rep, n_shard), out_shape=[one,...  21.3 us

profile of v7, /device:TPU:0, one launch (start us, length us, event | category | flops | bytes accessed | tf_op | source)
XLA Modules:
  0.0 181.2 jit_solution(8051361543173560488)
XLA Ops:
  1.3 0.9 slice.3
  2.2 0.7 pad.4.patch_ends
  2.9 156.8 %train_step.1 = (bf16[6,384,384]{2,1,0:T(8,128)(2,1)}, bf16[2,256,384]{2,1,0:T(8,128)(2,1)}, f32[256,384]{1,0:T(8,128)}, f32[8,128]{1,0:T(8,128)}, bf16[2,2,4,16,3456]{4,3,2,1,0:T(8,128)(2,1)}) custom-call(bf16[6,196,768]{2,1,0:T(8,128)(2,1)} %patches.1, bf16[6,16,768]{2,1,0:T(8,128)(2,1)} %pad.4.patch_ends, s32[6]{0:T(128)} %labels.1, s32[1]{0:T(128)S(6)} %copy.47.counts, ...), custom_call_target="tpu_custom_call" | custom-call | flops 24000000000 | bytes 30000000 | tf_op jit(solution)/shard_map/train_step/pallas_call | solution.py:1511
  159.7 21.3 %adamw.1 = (f32[1,1]{1,0:T(1,128)}, f32[1,1]{1,0:T(1,128)}, f32[192,384]{1,0:T(8,128)}, f32[192,384]{1,0:T(8,128)}, f32[192,384]{1,0:T(8,128)}, /*index=5*/f32[3...) custom-call(bf16[6,384,384]{2,1,0:T(8,128)(2,1)} %get-tuple-element., ...), custom_call_target="tpu_custom_call" | custom-call | flops 200000000 | bytes 50000000 | tf_op jit(solution)/shard_map/adamw/pallas_call | solution.py:1811

commit v8 on v7

--- a/solution.py
+++ b/solution.py
@@ -78,13 +78,11 @@
 
 
 def gelu_parts(hidden):
-    square = hidden * hidden
-    tangent = jnp.tanh(hidden * (GELU_SCALE + (GELU_SCALE * GELU_CUBIC) * square))
+    bent = hidden * (GELU_SCALE + (GELU_SCALE * GELU_CUBIC) * (hidden * hidden))
+    tangent = jnp.tanh(bent)
     share = 0.5 + 0.5 * tangent
-    active = hidden * share
-    inner = (2.0 * GELU_SCALE) + (6.0 * GELU_SCALE * GELU_CUBIC) * square
-    slope = share + active * (1.0 - share) * inner
-    return active, slope
+    slope = share + (1.0 - tangent * tangent) * (1.5 * bent - GELU_SCALE * hidden)
+    return hidden * share, slope
 
 
 def lane_mask(width, low, high):
@@ -92,7 +90,7 @@
     return jnp.where((lane >= low) & (lane < high), 1.0, 0.0).astype(BF)
 
 
-STEP = 32
+STEP = 16
 
 
 def pieces(total):
@@ -196,7 +194,7 @@
     X, N1, I1, QKV, ATT, N2, I2, ACT, SLOPE, DXB, DMB, DA, DH,
     pix, lab, lab_given, wp, win, wdn, low_head, head_bias,
     G, RC, RY, RX, RZ, RES, GS, SC, SY, SX, SZ, SRES,
-    FAC, FC, FY, FALL, V, VC, VY, VX, VZ, VF, SQ, SQZ, SQP, square_sum,
+    FAC, FC, FY, V, VC, VY, VX, VZ, VF, SQ, SQZ, SQP, square_sum,
     ag_send, ag_recv, ag_local, rs_send, rs_recv, f_send, f_recv, v_send, v_recv,
     q_send, q_recv,
     img_send, img_recv, img_local, out_local,
@@ -683,26 +681,30 @@
         for o in range(1, n_y):
             go(lambda: FAC.at[c], FY.at[o - 1], fac, f_y + o - 1, here.to(y=turn(y, o, n_y)))
 
+    def line_factors(z_at, x_at):
+        return all_factors.at[c, x_at, z_at]
+
     def factors_z():
         total = FAC[c]
         for o in range(1, n_y):
             arrived(FY.at[o - 1], f_recv.at[f_y + o - 1], f_send.at[f_y + o - 1])
             total = total + FY[o - 1]
-        FALL[z] = total
+        FC[...] = total
+        pltpu.make_async_copy(FC, line_factors(z, x), out_local.at[0]).start()
         for o in range(1, n_z):
             go(
-                lambda: FALL.at[z], FALL.at[z], fac, f_z + o - 1,
+                lambda: FC, line_factors(z, x), fac, f_z + o - 1,
                 here.to(z=turn(z, o, n_z)),
             )
 
     def factors_x():
         for o in range(1, n_z):
             index = f_z + o - 1
-            arrived(FALL.at[turn(z, n_z - o, n_z)], f_recv.at[index], f_send.at[index])
-        pltpu.make_async_copy(FALL, all_factors.at[c, x], out_local.at[0]).start()
+            arrived(line_factors(turn(z, n_z - o, n_z), x), f_recv.at[index], f_send.at[index])
+        pltpu.make_async_copy(FC, line_factors(z, x), out_local.at[0]).wait()
         for o in range(1, n_x):
             go(
-                lambda: FALL, all_factors.at[c, x], fac, f_x + o - 1,
+                lambda: all_factors.at[c, x], all_factors.at[c, x], fac, f_x + o - 1,
                 here.to(x=turn(x, o, n_x)),
             )
 
@@ -711,7 +713,6 @@
             index = f_x + o - 1
             came = all_factors.at[c, turn(x, n_x - o, n_x)]
             arrived(came, f_recv.at[index], f_send.at[index])
-        pltpu.make_async_copy(FALL, all_factors.at[c, x], out_local.at[0]).wait()
         go(lambda: all_factors.at[c], all_factors.at[c], fac, f_m, mate)
 
     def factors_done():
@@ -1546,7 +1547,6 @@
             buf(2, group, WFAC),
             buf(group, WFAC),
             buf(n_y - 1, group, WFAC),
-            buf(n_z, group, WFAC),
             buf(VEC_ROWS, VEC_WIDE, dtype=F32),
             buf(VEC_ROWS // 2, VEC_WIDE, dtype=F32),
             buf(n_y - 1, rows_y, VEC_WIDE, dtype=F32),
@@ -1584,15 +1584,15 @@
 
 
 def adam(weight, first, second, grad, factor, rate):
-    grad = grad * factor
-    first = BETA_FIRST * first + (1.0 - BETA_FIRST) * grad
-    second = BETA_SECOND * second + (1.0 - BETA_SECOND) * (grad * grad)
-    first_scale = 1.0 / (1.0 - BETA_FIRST**ADAM_STEP)
+    share = grad * factor
+    first = BETA_FIRST * first + share
+    square_scale = (1.0 - BETA_SECOND) / (1.0 - BETA_FIRST) ** 2
+    second = BETA_SECOND * second + square_scale * (share * share)
     root_scale = (1.0 / (1.0 - BETA_SECOND**ADAM_STEP)) ** 0.5
-    bottom = second * lax.rsqrt(second) * root_scale + ADAM_EPS
+    step_scale = rate / (1.0 - BETA_FIRST**ADAM_STEP) / root_scale
+    bottom = second * lax.rsqrt(second) + ADAM_EPS / root_scale
     step = first * lax.rsqrt(bottom * bottom)
-    weight = weight * (1.0 - rate * WEIGHT_DECAY) - step * (rate * first_scale)
-    return weight, first, second
+    return weight * (1.0 - rate * WEIGHT_DECAY) - step * step_scale, first, second
 
 
 def update(n_rep, n_shard, *refs):
@@ -1706,7 +1706,7 @@
     grad_norm = jnp.sqrt(sum_squares) * inv_count
     norm_out[...] = grad_norm
     loss_out[...] = vec[used : used + 1, 0:1] * inv_count
-    scale = jnp.minimum(1.0, CLIP_NORM / grad_norm) * inv_count
+    scale = jnp.minimum(1.0, CLIP_NORM / grad_norm) * inv_count * (1.0 - BETA_FIRST)
 
     def apply(array, where, grad, rate):
         refs = [buffers[3 * array + kind] for kind in range(3)]

time: 182 us -> 181 us (level)
  no operation moved by 1% of the time
where the time goes in v8:
time: 181 us
  Pallas kernels  178 us (98%)
    pallas_call x1, Pallas kernels, run_train(): pl.pallas_call(functools.partial(train, n_rep, n_shard), out_shape=[jax.S...  157 us
    pallas_call x1, Pallas kernels, run_update(): pl.pallas_call(functools.partial(update, n_rep, n_shard), out_shape=[one,...  21.2 us

profile of v8, /device:TPU:0, one launch (start us, length us, event | category | flops | bytes accessed | tf_op | source)
XLA Modules:
  0.0 181.0 jit_solution(12746883226068325854)
XLA Ops:
  1.3 0.9 slice.3
  2.2 0.7 pad.4.patch_ends
  2.9 156.7 %train_step.1 = (bf16[6,384,384]{2,1,0:T(8,128)(2,1)}, bf16[2,256,384]{2,1,0:T(8,128)(2,1)}, f32[256,384]{1,0:T(8,128)}, f32[8,128]{1,0:T(8,128)}, bf16[2,2,4,16,3456]{4,3,2,1,0:T(8,128)(2,1)}) custom-call(bf16[6,196,768]{2,1,0:T(8,128)(2,1)} %patches.1, bf16[6,16,768]{2,1,0:T(8,128)(2,1)} %pad.4.patch_ends, s32[6]{0:T(128)} %labels.1, s32[1]{0:T(128)S(6)} %copy.47.counts, ...), custom_call_target="tpu_custom_call" | custom-call | flops 24000000000 | bytes 30000000 | tf_op jit(solution)/shard_map/train_step/pallas_call | solution.py:1512
  159.6 21.2 %adamw.1 = (f32[1,1]{1,0:T(1,128)}, f32[1,1]{1,0:T(1,128)}, f32[192,384]{1,0:T(8,128)}, f32[192,384]{1,0:T(8,128)}, f32[192,384]{1,0:T(8,128)}, /*index=5*/f32[3...) custom-call(bf16[6,384,384]{2,1,0:T(8,128)(2,1)} %get-tuple-element., ...), custom_call_target="tpu_custom_call" | custom-call | flops 200000000 | bytes 50000000 | tf_op jit(solution)/shard_map/adamw/pallas_call | solution.py:1811

commit v9 on v8

--- a/solution.py
+++ b/solution.py
@@ -101,52 +101,50 @@
     ("cast", 0): ("ws0",),
     ("cast", 1): ("ws1",),
     ("cast", 2): ("ws2",),
-    ("b_start",): ("wf0", "ws3", "wf1", "wr0", "ws4", "we0",),
-    ("embed", 0): ("wf2", "ws5",),
-    ("b_norm", 0, 0): ("wr1", "wf3", "ws6", "we1",),
-    ("norm", 0, 0): ("wr2", "wf4", "ws7",),
-    ("att", 0, 0, 1): ("wr3",),
-    ("mid", 0, 0): ("wf5", "ws8",),
+    ("b_start",): ("wf0", "ws3", "wr0", "wf1", "ws4", "we0",),
+    ("b_norm", 0, 0): ("wf2", "ws5", "wr1", "we1",),
+    ("norm", 0, 0): ("wr2", "wf3", "ws6",),
+    ("mid", 0, 0): ("wf4", "ws7",),
     ("b_up", 0, 0): ("we2",),
-    ("up", 0, 0): ("wr4", "wf6", "ws9",),
-    ("b_down", 0, 0): ("we3",),
-    ("b_norm", 0, 1): ("wr5", "we4",),
-    ("norm", 0, 1): ("wf7",),
-    ("att", 0, 1, 0): ("wr6",),
-    ("att", 0, 1, 1): ("wf8",),
+    ("up", 0, 0): ("wr3",),
+    ("b_down", 0, 0): ("wf5", "ws8", "we3",),
+    ("b_norm", 0, 1): ("wr4", "wf6", "ws9", "we4",),
+    ("att", 0, 1, 0): ("wr5", "wf7",),
     ("b_up", 0, 1): ("we5",),
-    ("up", 0, 1): ("wr7", "wf9",),
+    ("up", 0, 1): ("wr6", "wf8",),
     ("b_down", 0, 1): ("we6",),
-    ("norm", 1, 0): ("wr8",),
-    ("att", 1, 0, 1): ("wr9",),
+    ("down", 0, 1): ("wr7",),
+    ("embed", 1): ("wf9",),
+    ("att", 1, 0, 0): ("wr8",),
+    ("up", 1, 0): ("wr9",),
     ("b_last",): ("we7", "we8", "we9",),
     ("class",): ("fc",),
     ("kv",): ("core6",),
-    ("lb", 1): ("fy",),
-    ("dn", 1): ("y6", "core0",),
-    ("act", 1, 1): ("fz",),
-    ("ups", 1): ("core1", "y0",),
+    ("lb", 0): ("fy",),
+    ("dn", 1): ("y6", "fz", "core0",),
+    ("ups", 1): ("y0", "core1",),
     ("mlpb", 1, 1): ("x6",),
+    ("out", 1): ("fx",),
     ("attb", 1, 0): ("y1",),
     ("attb", 1, 2): ("z6",),
-    ("attb", 1, 3): ("x0",),
-    ("qkv", 1): ("fx", "core2",),
-    ("fb", 1, 1): ("gz6",),
-    ("dn", 0): ("y2", "x1", "z0", "core3",),
+    ("qkv", 1): ("x0", "core2",),
+    ("fb", 1, 0): ("gz6",),
+    ("dn", 0): ("y2", "core3",),
     ("act", 0, 0): ("gx6",),
-    ("mlpb", 0, 0): ("gz0",),
-    ("attb", 0, 0): ("x2", "y3", "core4", "fm",),
-    ("attb", 0, 1): ("gx0",),
-    ("attb", 0, 2): ("z1",),
-    ("qkv", 0): ("gd6",),
-    ("fb", 0, 1): ("fd",),
-    ("emb",): ("z2", "x3", "y4", "core5", "gz1", "vc",),
-    ("patch",): ("core7",),
-    ("tail",): ("gd0", "gz2", "vy", "z3", "y7", "gx1", "x4", "y5", "vx", "gx2", "gd1", "gz3", "x7", "z4", "vz", "gx3", "gd2", "x5", "z7", "gz4", "vgz", "gd3", "gz7", "z5", "gx4", "vgx", "gx7", "gd4", "vgy", "gz5", "qz", "gd7", "vgc", "gx5", "qp", "vd", "gd5", "qd",),
+    ("act", 0, 1): ("z0",),
+    ("ups", 0): ("x1",),
+    ("mlpb", 0, 0): ("gd6",),
+    ("attb", 0, 0): ("gz0",),
+    ("attb", 0, 1): ("z1",),
+    ("attb", 0, 2): ("x2", "y3", "core4",),
+    ("qkv", 0): ("gx0",),
+    ("emb",): ("z2", "vc",),
+    ("patch",): ("gz1", "core7",),
+    ("tail",): ("vy", "gd0", "x3", "y4", "core5", "y7", "gz2", "vx", "z3", "gx1", "vz", "gx2", "x4", "y5", "gd1", "fv", "gz3", "vgz", "gd2", "x7", "z4", "gx3", "vgx", "z7", "x5", "gz4", "gd3", "vgy", "gz7", "z5", "gx4", "gx7", "gd4", "fm", "gz5", "qz", "gd7", "vgc", "fd", "vd", "gx5", "qp", "gd5", "qd",),
 }
 
 
-WFAC = FF + 5 * D
+WFAC = FF + 5 * D + 128
 VEC_ROWS = 256
 VEC_AT = BLK
 VEC_WIDE = D
@@ -669,7 +667,9 @@
     fac = ("f", f_send, f_recv)
     f_y, f_z = 1, n_y
     f_x = f_z + n_z - 1
-    f_m = f_x + n_x - 1
+    f_v = f_x + n_x - 1
+    f_m = f_v + n_y - 1
+    part_wide = WFAC // n_y
     group = KEPT * n_shard
 
     def factors_core():
@@ -679,21 +679,24 @@
         arrived(FC, f_recv.at[0], f_send.at[0])
         FAC[c] = FAC[c] + FC[...]
         for o in range(1, n_y):
-            go(lambda: FAC.at[c], FY.at[o - 1], fac, f_y + o - 1, here.to(y=turn(y, o, n_y)))
+            go(
+                lambda o=o: FAC.at[c, turn(y, o, n_y)], FY.at[o - 1], fac, f_y + o - 1,
+                here.to(y=turn(y, o, n_y)),
+            )
 
     def line_factors(z_at, x_at):
-        return all_factors.at[c, x_at, z_at]
+        return all_factors.at[c, y, x_at, z_at]
 
     def factors_z():
-        total = FAC[c]
+        total = FAC[c, y]
         for o in range(1, n_y):
             arrived(FY.at[o - 1], f_recv.at[f_y + o - 1], f_send.at[f_y + o - 1])
             total = total + FY[o - 1]
-        FC[...] = total
-        pltpu.make_async_copy(FC, line_factors(z, x), out_local.at[0]).start()
+        FC[0] = total
+        pltpu.make_async_copy(FC.at[0], line_factors(z, x), out_local.at[0]).start()
         for o in range(1, n_z):
             go(
-                lambda: FC, line_factors(z, x), fac, f_z + o - 1,
+                lambda: FC.at[0], line_factors(z, x), fac, f_z + o - 1,
                 here.to(z=turn(z, o, n_z)),
             )
 
@@ -701,17 +704,28 @@
         for o in range(1, n_z):
             index = f_z + o - 1
             arrived(line_factors(turn(z, n_z - o, n_z), x), f_recv.at[index], f_send.at[index])
-        pltpu.make_async_copy(FC, line_factors(z, x), out_local.at[0]).wait()
+        pltpu.make_async_copy(FC.at[0], line_factors(z, x), out_local.at[0]).wait()
         for o in range(1, n_x):
             go(
-                lambda: all_factors.at[c, x], all_factors.at[c, x], fac, f_x + o - 1,
+                lambda: all_factors.at[c, y, x], all_factors.at[c, y, x], fac, f_x + o - 1,
                 here.to(x=turn(x, o, n_x)),
             )
 
-    def factors_mate():
+    def factors_side():
         for o in range(1, n_x):
             index = f_x + o - 1
-            came = all_factors.at[c, turn(x, n_x - o, n_x)]
+            came = all_factors.at[c, y, turn(x, n_x - o, n_x)]
+            arrived(came, f_recv.at[index], f_send.at[index])
+        for o in range(1, n_y):
+            go(
+                lambda: all_factors.at[c, y], all_factors.at[c, y], fac, f_v + o - 1,
+                here.to(y=turn(y, o, n_y)),
+            )
+
+    def factors_mate():
+        for o in range(1, n_y):
+            index = f_v + o - 1
+            came = all_factors.at[c, turn(y, n_y - o, n_y)]
             arrived(came, f_recv.at[index], f_send.at[index])
         go(lambda: all_factors.at[c], all_factors.at[c], fac, f_m, mate)
 
@@ -916,8 +930,8 @@
         actions[f"gx{k}"] = functools.partial(gather_x, k)
         actions[f"gd{k}"] = functools.partial(gather_done, k)
     actions.update(
-        fc=factors_core, fy=factors_y, fz=factors_z, fx=factors_x, fm=factors_mate,
-        fd=factors_done,
+        fc=factors_core, fy=factors_y, fz=factors_z, fx=factors_x, fv=factors_side,
+        fm=factors_mate, fd=factors_done,
     )
 
     def tails(ref, layer=None):
@@ -1020,15 +1034,19 @@
     pick = jnp.where(
         ((pick_row - KEPT * here.shard) * 16 + (CLS - TAIL)) == pick_lane, 1.0, 0.0
     ).astype(BF)
-    at = 0
-    for piece in (active, h2, attended, h1, final, low_top):
-        FAC[0, :, at : at + piece.shape[-1]] = mm(pick, piece).astype(BF)
-        at += piece.shape[-1]
-    at = 0
-    for piece in (d_up, low_middle, d_query, d_logits):
-        FAC[1, :, at : at + piece.shape[-1]] = mm(pick, piece).astype(BF)
-        at += piece.shape[-1]
-    FAC[1, :, at:] = jnp.zeros((group, WFAC - at), BF)
+    def keep_factors(half, pieces_of):
+        at = 0
+        for piece in pieces_of:
+            made = None if piece is None else mm(pick, piece).astype(BF)
+            for lane in range(0, WFAC - at if made is None else made.shape[-1], 128):
+                part, column = divmod(at + lane, part_wide)
+                FAC[half, part, :, column : column + 128] = (
+                    jnp.zeros((group, 128), BF) if made is None else made[:, lane : lane + 128]
+                )
+            at += 0 if made is None else made.shape[-1]
+
+    keep_factors(0, (active, h2, attended, h1, final, low_top, None))
+    keep_factors(1, (d_up, low_middle, d_query, d_logits, None))
     at_place("class")
 
     turned = DXB[...].T
@@ -1443,7 +1461,7 @@
     perform(ending[:-6])
     early = [
         key for key in sent
-        if key[0] in ("ag", "f") or (key[0] == "rs" and key[1][0] not in (4, 5, 7))
+        if key[0] == "ag" or (key[0] == "rs" and key[1][0] not in (4, 5, 7))
     ]
     for key in early:
         source, send, recv, at = sent.pop(key)
@@ -1504,7 +1522,7 @@
     rows_z = rows_x // cut(rows_x, n_z, 8)
     ag_count = n_y + (n_y - 1) * (n_x - 1) * 2 + n_y - 1
     rs_count = 1 + (n_y - 1) + 2 * (n_x - 1) + 2 * (n_z - 1)
-    f_count = 1 + (n_y - 1) + (n_x - 1) + (n_z - 1) + 1
+    f_count = 1 + 2 * (n_y - 1) + (n_x - 1) + (n_z - 1) + 1
     v_count = 1 + 2 * (n_y - 1) + 2 * (n_x - 1) + 2 * (n_z - 1) + 1
     q_count = n_z - 1 + 2 * n_x * n_y - 1
     whole = pl.BlockSpec(memory_space=pltpu.VMEM)
@@ -1516,7 +1534,7 @@
             jax.ShapeDtypeStruct((2, small_block, D), BF),
             jax.ShapeDtypeStruct((VEC_ROWS, VEC_WIDE), F32),
             jax.ShapeDtypeStruct((8, 128), F32),
-            jax.ShapeDtypeStruct((2, n_x, n_z, group, WFAC), BF),
+            jax.ShapeDtypeStruct((2, n_y, n_x, n_z, group, WFAC // n_y), BF),
         ],
         in_specs=[there] * 2 + [pl.BlockSpec(memory_space=pltpu.SMEM)] * 2 + [there] * 3 + [whole] * 4,
         out_specs=[there] * 5,
@@ -1544,9 +1562,9 @@
             buf(1, CPAD, dtype=F32),
             *reduction(CHUNKS, 3, block),
             *reduction(2, 1, small_block),
-            buf(2, group, WFAC),
-            buf(group, WFAC),
-            buf(n_y - 1, group, WFAC),
+            buf(2, n_y, group, WFAC // n_y),
+            buf(n_y, group, WFAC // n_y),
+            buf(n_y - 1, group, WFAC // n_y),
             buf(VEC_ROWS, VEC_WIDE, dtype=F32),
             buf(VEC_ROWS // 2, VEC_WIDE, dtype=F32),
             buf(n_y - 1, rows_y, VEC_WIDE, dtype=F32),
@@ -1628,10 +1646,18 @@
         for move in moves(array, layer):
             move.start()
 
-    n_rows = factors.shape[1] * factors.shape[2] * factors.shape[3]
+    n_rows = factors.shape[2] * factors.shape[3] * factors.shape[4]
+    part_wide = factors.shape[5]
 
     def factor(half, at, size):
-        return factors[half, :, :, :, at : at + size].reshape(n_rows, size)
+        found = []
+        while size:
+            part, column = divmod(at, part_wide)
+            wide = min(size, part_wide - column)
+            piece = factors[half, part, :, :, :, column : column + wide]
+            found.append(piece.reshape(n_rows, wide))
+            at, size = at + wide, size - wide
+        return found[0] if len(found) == 1 else jnp.concatenate(found, axis=1)
 
     def squares(values):
         return fold(values * values)

time: 181 us -> 181 us (level)
  no operation moved by 1% of the time
where the time goes in v9:
time: 181 us
  Pallas kernels  178 us (98%)
    pallas_call x1, Pallas kernels, run_train(): pl.pallas_call(functools.partial(train, n_rep, n_shard), out_shape=[jax.S...  157 us
    pallas_call x1, Pallas kernels, run_update(): pl.pallas_call(functools.partial(update, n_rep, n_shard), out_shape=[one,...  21.2 us

profile of v9, /device:TPU:0, one launch (start us, length us, event | category | flops | bytes accessed | tf_op | source)
XLA Modules:
  0.0 181.1 jit_solution(12630964606571749083)
XLA Ops:
  1.3 0.9 slice.3
  2.2 0.7 pad.4.patch_ends
  2.9 156.8 %train_step.1 = (bf16[6,384,384]{2,1,0:T(8,128)(2,1)}, bf16[2,256,384]{2,1,0:T(8,128)(2,1)}, f32[256,384]{1,0:T(8,128)}, f32[8,128]{1,0:T(8,128)}, bf16[2,2,2,4,16,1792]{5,4,3,2,1,0:T(8,128)(2,1)}) custom-call(bf16[6,196,768]{2,1,0:T(8,128)(2,1)} %patches.1, bf16[6,16,768]{2,1,0:T(8,128)(2,1)} %pad.4.patch_ends, s32[6]{0:T(128)} %labels.1, ...), custom_call_target="tpu_custom_call" | custom-call | flops 24000000000 | bytes 30000000 | tf_op jit(solution)/shard_map/train_step/pallas_call | solution.py:1530
  159.7 21.2 %adamw.1 = (f32[1,1]{1,0:T(1,128)}, f32[1,1]{1,0:T(1,128)}, f32[192,384]{1,0:T(8,128)}, f32[192,384]{1,0:T(8,128)}, f32[192,384]{1,0:T(8,128)}, /*index=5*/f32[3...) custom-call(bf16[6,384,384]{2,1,0:T(8,128)(2,1)} %get-tuple-element., ...), custom_call_target="tpu_custom_call" | custom-call | flops 200000000 | bytes 50000000 | tf_op jit(solution)/shard_map/adamw/pallas_call | solution.py:1837

commit v10 on v9

--- a/solution.py
+++ b/solution.py
@@ -101,46 +101,52 @@
     ("cast", 0): ("ws0",),
     ("cast", 1): ("ws1",),
     ("cast", 2): ("ws2",),
-    ("b_start",): ("wf0", "ws3", "wr0", "wf1", "ws4", "we0",),
-    ("b_norm", 0, 0): ("wf2", "ws5", "wr1", "we1",),
-    ("norm", 0, 0): ("wr2", "wf3", "ws6",),
-    ("mid", 0, 0): ("wf4", "ws7",),
+    ("cast", 8): ("wf0", "ws3",),
+    ("b_start",): ("wr0", "wf1", "ws4", "we0",),
+    ("b_norm", 0, 0): ("wf2", "ws5", "wr1", "wf3", "ws6", "we1",),
+    ("norm", 0, 0): ("wr2",),
+    ("att", 0, 0, 0): ("wf4", "ws7",),
+    ("att", 0, 0, 1): ("wr3",),
     ("b_up", 0, 0): ("we2",),
-    ("up", 0, 0): ("wr3",),
-    ("b_down", 0, 0): ("wf5", "ws8", "we3",),
-    ("b_norm", 0, 1): ("wr4", "wf6", "ws9", "we4",),
-    ("att", 0, 1, 0): ("wr5", "wf7",),
+    ("up", 0, 0): ("wr4", "wf5", "ws8",),
+    ("b_down", 0, 0): ("we3",),
+    ("down", 0, 0): ("wf6", "ws9",),
+    ("b_norm", 0, 1): ("we4",),
+    ("norm", 0, 1): ("wf7", "wr5",),
+    ("mid", 0, 1): ("wr6", "wf8",),
     ("b_up", 0, 1): ("we5",),
-    ("up", 0, 1): ("wr6", "wf8",),
+    ("up", 0, 1): ("wf9",),
     ("b_down", 0, 1): ("we6",),
     ("down", 0, 1): ("wr7",),
-    ("embed", 1): ("wf9",),
-    ("att", 1, 0, 0): ("wr8",),
-    ("up", 1, 0): ("wr9",),
+    ("norm", 1, 0): ("wr8",),
+    ("att", 1, 0, 1): ("wr9",),
     ("b_last",): ("we7", "we8", "we9",),
     ("class",): ("fc",),
     ("kv",): ("core6",),
     ("lb", 0): ("fy",),
-    ("dn", 1): ("y6", "fz", "core0",),
-    ("ups", 1): ("y0", "core1",),
-    ("mlpb", 1, 1): ("x6",),
-    ("out", 1): ("fx",),
-    ("attb", 1, 0): ("y1",),
-    ("attb", 1, 2): ("z6",),
-    ("qkv", 1): ("x0", "core2",),
-    ("fb", 1, 0): ("gz6",),
-    ("dn", 0): ("y2", "core3",),
-    ("act", 0, 0): ("gx6",),
-    ("act", 0, 1): ("z0",),
-    ("ups", 0): ("x1",),
-    ("mlpb", 0, 0): ("gd6",),
-    ("attb", 0, 0): ("gz0",),
-    ("attb", 0, 1): ("z1",),
-    ("attb", 0, 2): ("x2", "y3", "core4",),
-    ("qkv", 0): ("gx0",),
-    ("emb",): ("z2", "vc",),
-    ("patch",): ("gz1", "core7",),
-    ("tail",): ("vy", "gd0", "x3", "y4", "core5", "y7", "gz2", "vx", "z3", "gx1", "vz", "gx2", "x4", "y5", "gd1", "fv", "gz3", "vgz", "gd2", "x7", "z4", "gx3", "vgx", "z7", "x5", "gz4", "gd3", "vgy", "gz7", "z5", "gx4", "gx7", "gd4", "fm", "gz5", "qz", "gd7", "vgc", "fd", "vd", "gx5", "qp", "gd5", "qd",),
+    ("round", 1): ("y6",),
+    ("dn", 1): ("fz", "core0",),
+    ("ups", 1): ("y0", "x6", "core1",),
+    ("mlpb", 1, 0): ("fx",),
+    ("out", 1): ("y1", "z6",),
+    ("attb", 1, 2): ("x0", "gz6",),
+    ("qkv", 1): ("core2",),
+    ("fb", 1, 0): ("gx6",),
+    ("fb", 1, 1): ("x1", "z0",),
+    ("round", 0): ("y2",),
+    ("dn", 0): ("gd6", "core3",),
+    ("act", 0, 1): ("z1", "gz0",),
+    ("mlpb", 0, 0): ("x2", "y3", "core4",),
+    ("mlpb", 0, 1): ("gz1",),
+    ("attb", 0, 0): ("gx0",),
+    ("attb", 0, 1): ("z2",),
+    ("attb", 0, 2): ("gx1",),
+    ("attb", 0, 3): ("x3", "y4", "gd0",),
+    ("qkv", 0): ("gz2", "core5",),
+    ("fb", 0, 0): ("gd1",),
+    ("emb",): ("vc",),
+    ("patch",): ("z3", "gx2", "core7",),
+    ("tail",): ("vy", "x4", "y5", "y7", "fv", "vx", "gz3", "gd2", "z4", "vz", "gx3", "x5", "gz4", "vgz", "gd3", "x7", "z5", "gx4", "vgx", "z7", "gz5", "gd4", "vgy", "gz7", "qz", "fm", "gx5", "vgc", "gx7", "qp", "fd", "vd", "gd5", "gd7", "qd",),
 }
 
 

time: 181 us -> 178 us (0.983)
  Pallas kernels: 178 us -> 174 us
    pallas_call x1, Pallas kernels: 157 us -> 153 us  [run_train(): pl.pallas_call(functools.partial(train, n_rep, n_shard), out_shape=[jax.S...]
where the time goes in v10:
time: 178 us
  Pallas kernels  174 us (98%)
    pallas_call x1, Pallas kernels, run_train(): pl.pallas_call(functools.partial(train, n_rep, n_shard), out_shape=[jax.S...  153 us
    pallas_call x1, Pallas kernels, run_update(): pl.pallas_call(functools.partial(update, n_rep, n_shard), out_shape=[one,...  21.2 us

profile of v10, /device:TPU:0, one launch (start us, length us, event | category | flops | bytes accessed | tf_op | source)
XLA Modules:
  0.0 177.5 jit_solution(4908504104871898699)
XLA Ops:
  1.3 0.9 slice.3
  2.2 0.7 pad.4.patch_ends
  2.9 153.2 %train_step.1 = (bf16[6,384,384]{2,1,0:T(8,128)(2,1)}, bf16[2,256,384]{2,1,0:T(8,128)(2,1)}, f32[256,384]{1,0:T(8,128)}, f32[8,128]{1,0:T(8,128)}, bf16[2,2,2,4,16,1792]{5,4,3,2,1,0:T(8,128)(2,1)}) custom-call(bf16[6,196,768]{2,1,0:T(8,128)(2,1)} %patches.1, bf16[6,16,768]{2,1,0:T(8,128)(2,1)} %pad.4.patch_ends, s32[6]{0:T(128)} %labels.1, ...), custom_call_target="tpu_custom_call" | custom-call | flops 24000000000 | bytes 30000000 | tf_op jit(solution)/shard_map/train_step/pallas_call | solution.py:1536
  156.1 21.2 %adamw.1 = (f32[1,1]{1,0:T(1,128)}, f32[1,1]{1,0:T(1,128)}, f32[192,384]{1,0:T(8,128)}, f32[192,384]{1,0:T(8,128)}, f32[192,384]{1,0:T(8,128)}, /*index=5*/f32[3...) custom-call(bf16[6,384,384]{2,1,0:T(8,128)(2,1)} %get-tuple-element., ...), custom_call_target="tpu_custom_call" | custom-call | flops 200000000 | bytes 50000000 | tf_op jit(solution)/shard_map/adamw/pallas_call | solution.py:1843

commit v11 on v10

--- a/solution.py
+++ b/solution.py
@@ -112,14 +112,13 @@
     ("b_down", 0, 0): ("we3",),
     ("down", 0, 0): ("wf6", "ws9",),
     ("b_norm", 0, 1): ("we4",),
-    ("norm", 0, 1): ("wf7", "wr5",),
+    ("att", 0, 1, 0): ("wr5", "wf7",),
     ("mid", 0, 1): ("wr6", "wf8",),
     ("b_up", 0, 1): ("we5",),
-    ("up", 0, 1): ("wf9",),
     ("b_down", 0, 1): ("we6",),
-    ("down", 0, 1): ("wr7",),
+    ("down", 0, 1): ("wr7", "wf9",),
     ("norm", 1, 0): ("wr8",),
-    ("att", 1, 0, 1): ("wr9",),
+    ("mid", 1, 0): ("wr9",),
     ("b_last",): ("we7", "we8", "we9",),
     ("class",): ("fc",),
     ("kv",): ("core6",),
@@ -132,7 +131,7 @@
     ("attb", 1, 2): ("x0", "gz6",),
     ("qkv", 1): ("core2",),
     ("fb", 1, 0): ("gx6",),
-    ("fb", 1, 1): ("x1", "z0",),
+    ("fb", 1, 1): ("z0", "x1",),
     ("round", 0): ("y2",),
     ("dn", 0): ("gd6", "core3",),
     ("act", 0, 1): ("z1", "gz0",),
@@ -140,13 +139,12 @@
     ("mlpb", 0, 1): ("gz1",),
     ("attb", 0, 0): ("gx0",),
     ("attb", 0, 1): ("z2",),
-    ("attb", 0, 2): ("gx1",),
-    ("attb", 0, 3): ("x3", "y4", "gd0",),
+    ("attb", 0, 3): ("x3", "y4", "gx1", "gd0",),
     ("qkv", 0): ("gz2", "core5",),
-    ("fb", 0, 0): ("gd1",),
+    ("fb", 0, 1): ("z3",),
     ("emb",): ("vc",),
-    ("patch",): ("z3", "gx2", "core7",),
-    ("tail",): ("vy", "x4", "y5", "y7", "fv", "vx", "gz3", "gd2", "z4", "vz", "gx3", "x5", "gz4", "vgz", "gd3", "x7", "z5", "gx4", "vgx", "z7", "gz5", "gd4", "vgy", "gz7", "qz", "fm", "gx5", "vgc", "gx7", "qp", "fd", "vd", "gd5", "gd7", "qd",),
+    ("patch",): ("gx2", "core7",),
+    ("tail",): ("vy", "gd1", "x4", "y5", "y7", "fv", "gz3", "vx", "gd2", "z4", "gx3", "vz", "x5", "gz4", "gd3", "vgz", "x7", "z5", "gx4", "vgx", "z7", "gz5", "gd4", "vgy", "gz7", "qz", "fm", "gx5", "vgc", "gx7", "qp", "fd", "vd", "gd5", "gd7", "qd",),
 }
 
 
@@ -560,7 +558,14 @@
             DMB[rows, :] = made[:, 0:D].astype(BF)
             DA[rows, :] = (made[:, D:] + vector(layer, 3 * D, D)).astype(BF)
 
-    ones = jnp.full((BLK, 128), 1.0, BF)
+    lanes = 256
+    fill = jnp.zeros((lanes - BLK, 128), BF)
+    ones = jnp.full((lanes, 128), 1.0, BF)
+    wide_lane = lax.broadcasted_iota(jnp.int32, (1, lanes), 1)
+    wide_key_row = jnp.where((wide_lane < PATCHES) | (wide_lane == CLS), 0.0, -1e30)
+
+    def fill_up(values):
+        return jnp.concatenate([jnp.concatenate([values, fill], axis=0), ones], axis=1)
 
     def attend(layer, image):
         rows = pl.ds(aligned(image * BLK, 16), BLK)
@@ -570,14 +575,14 @@
             keys = QKV[layer, rows, D + at : D + at + 128]
             values = QKV[layer, rows, 2 * D + at : 2 * D + at + 128]
             both = jnp.concatenate([query * even, query * odd], axis=0)
-            scores = mm_nt(both, keys)
+            scores = mm_nt(both, jnp.concatenate([keys, fill], axis=0))
             probs = []
             for row, size in pieces(HALF):
-                part = scores[row : row + size] + key_row
+                part = scores[row : row + size] + wide_key_row
                 probs.append(jnp.exp(part - jnp.max(part, axis=-1, keepdims=True)).astype(BF))
             probs = jnp.concatenate(probs, axis=0)
-            first = mm(probs[:BLK], jnp.concatenate([values * even, ones], axis=1))
-            second = mm(probs[BLK:], jnp.concatenate([values * odd, ones], axis=1))
+            first = mm(probs[:BLK], fill_up(values * even))
+            second = mm(probs[BLK:], fill_up(values * odd))
             made = first[:, :128] * (1.0 / first[:, 128:])
             made = made + second[:, :128] * (1.0 / second[:, 128:])
             ATT[layer, rows, at : at + 128] = made.astype(BF)
@@ -1160,12 +1165,14 @@
             ups = DA[rows, at : at + 128]
             keys_both = jnp.concatenate([keys * even, keys * odd], axis=0)
             values_both = jnp.concatenate([values * even, values * odd], axis=0)
+            query = jnp.concatenate([query, fill], axis=0)
+            ups = jnp.concatenate([ups, fill], axis=0)
             scores = mm_nt(keys_both, query)
             d_probs = mm_nt(values_both, ups)
             probs, d_scores = [], []
             for base in (0, BLK):
                 low_probs, low_grads = [], []
-                for first, end in ((0, 128), (128, BLK)):
+                for first, end in ((0, 128), (128, lanes)):
                     part = jnp.concatenate(
                         [
                             scores[base : base + TAIL, first:end],
@@ -1185,7 +1192,7 @@
             d_scores = jnp.concatenate(d_scores, axis=0)
             d_values = mm(probs, ups)
             d_keys = mm(d_scores, query)
-            d_query = mm_tn(d_scores, keys_both) * 0.125
+            d_query = mm_tn(d_scores, keys_both)[:BLK] * 0.125
             DH[rows, at : at + 128] = d_query.astype(BF)
             DH[rows, D + at : D + at + 128] = jnp.where(
                 low_lane, d_keys[:BLK], d_keys[BLK:]
@@ -1620,13 +1627,13 @@
 
 
 def update(n_rep, n_shard, *refs):
-    res, small, vec, exchanged, factors = refs[0:5]
+    res_there, small_there, vec, exchanged, factors = refs[0:5]
     sources = refs[5:26]
     loss_out, norm_out = refs[26:28]
     targets = refs[28:49]
     buffers = refs[49:70]
     results = refs[70:91]
-    last_in, last_down, passing, grad_head, in_sems, out_sems = refs[91:]
+    last_in, last_down, passing, grad_head, res, small, in_sems, out_sems, grad_sems = refs[91:]
     shard = lax.axis_index("shard")
     rows_in = D // n_shard
     rows_down = FF // n_shard
@@ -1647,10 +1654,15 @@
         return found
 
     layered = [(1, layer) for layer in range(LAYERS)] + [(2, layer) for layer in range(LAYERS)]
-    order = layered + [(0, None), (6, None), (5, None), (3, None), (4, None)]
+    order = [(4, None), (3, None), (5, None), (6, None)] + layered + [(0, None)]
+    res_copy = pltpu.make_async_copy(res_there, res, grad_sems.at[0])
+    small_copy = pltpu.make_async_copy(small_there, small, grad_sems.at[1])
+    small_copy.start()
     for array, layer in order:
         for move in moves(array, layer):
             move.start()
+        if array == 6:
+            res_copy.start()
 
     n_rows = factors.shape[2] * factors.shape[3] * factors.shape[4]
     part_wide = factors.shape[5]
@@ -1681,6 +1693,7 @@
         made = mm_tn(h2, factor(1, tile * D, D))
         keep_in(4 + tile, made)
         total = total + squares(made)
+    small_copy.wait()
     for tile in range(2):
         last_in[:, (1 + tile) * D : (2 + tile) * D] = small[
             0, tile * rows_in : (tile + 1) * rows_in, :
@@ -1761,6 +1774,36 @@
 
         lax.fori_loop(0, count, one, 0)
 
+    begin(4)
+    rows = [patch_bias, class_row, vec[used - 2 : used - 1, 0:D], vec[used - 1 : used, 0:D]]
+    for index, row in enumerate(rows):
+        apply(4, (slice(index, index + 1), slice(0, D)), row, VECTOR_RATE)
+    finish(4)
+    begin(3)
+    for layer in range(LAYERS):
+        for piece in range(12):
+            row = VEC_AT + 12 * layer + piece
+            where = (slice(layer, layer + 1), slice(piece * D, (piece + 1) * D))
+            apply(3, where, vec[row : row + 1, 0:D], VECTOR_RATE)
+    finish(3)
+    begin(5)
+    apply(5, (slice(0, 1), slice(0, D)), class_row, VECTOR_RATE)
+    for at in range(0, PATCHES, 28):
+        apply(
+            5, (slice(1 + at, 29 + at), slice(0, D)), vec[at : at + 28, 0:D], VECTOR_RATE
+        )
+    finish(5)
+    begin(6)
+
+    def head_rows(index):
+        for part in range(3):
+            rows = pl.ds(pl.multiple_of(index * 48 + part * 16, 16), 16)
+            apply(6, (rows, slice(0, NCLS)), grad_head[rows, 0:NCLS], LEARNING_RATE)
+
+    loop(D // 48, head_rows)
+    apply(6, (slice(D, D + 1), slice(0, NCLS)), grad_head[D : D + 1, 0:NCLS], LEARNING_RATE)
+    finish(6)
+    res_copy.wait()
     step = 32 if rows_in % 32 == 0 else 16
     for layer in range(LAYERS):
         begin(1, layer)
@@ -1802,35 +1845,6 @@
 
     loop(PATCH_DIM // n_shard // 96, patch_rows)
     finish(0)
-    begin(6)
-
-    def head_rows(index):
-        for part in range(3):
-            rows = pl.ds(pl.multiple_of(index * 48 + part * 16, 16), 16)
-            apply(6, (rows, slice(0, NCLS)), grad_head[rows, 0:NCLS], LEARNING_RATE)
-
-    loop(D // 48, head_rows)
-    apply(6, (slice(D, D + 1), slice(0, NCLS)), grad_head[D : D + 1, 0:NCLS], LEARNING_RATE)
-    finish(6)
-    begin(5)
-    apply(5, (slice(0, 1), slice(0, D)), class_row, VECTOR_RATE)
-    for at in range(0, PATCHES, 28):
-        apply(
-            5, (slice(1 + at, 29 + at), slice(0, D)), vec[at : at + 28, 0:D], VECTOR_RATE
-        )
-    finish(5)
-    begin(3)
-    for layer in range(LAYERS):
-        for piece in range(12):
-            row = VEC_AT + 12 * layer + piece
-            where = (slice(layer, layer + 1), slice(piece * D, (piece + 1) * D))
-            apply(3, where, vec[row : row + 1, 0:D], VECTOR_RATE)
-    finish(3)
-    begin(4)
-    rows = [patch_bias, class_row, vec[used - 2 : used - 1, 0:D], vec[used - 1 : used, 0:D]]
-    for index, row in enumerate(rows):
-        apply(4, (slice(index, index + 1), slice(0, D)), row, VECTOR_RATE)
-    finish(4)
     for array, layer in order:
         for move in moves(array, layer, out=True):
             move.wait()
@@ -1843,7 +1857,7 @@
     made = pl.pallas_call(
         functools.partial(update, n_rep, n_shard),
         out_shape=[one, one] + [jax.ShapeDtypeStruct(a.shape, F32) for a in arrays],
-        in_specs=[whole] * 5 + [there] * 21,
+        in_specs=[there] * 2 + [whole] * 3 + [there] * 21,
         out_specs=[whole] * 2 + [there] * 21,
         scratch_shapes=[pltpu.VMEM(a.shape, F32) for a in (*arrays, *arrays)]
         + [
@@ -1851,8 +1865,11 @@
             pltpu.VMEM((FF // n_shard, D), F32),
             pltpu.VMEM((2, D, D), F32),
             pltpu.VMEM((D + 8, CPAD), F32),
+            pltpu.VMEM(res.shape, BF),
+            pltpu.VMEM(small.shape, BF),
             pltpu.SemaphoreType.DMA((21, LAYERS)),
             pltpu.SemaphoreType.DMA((21, LAYERS)),
+            pltpu.SemaphoreType.DMA((2,)),
         ],
         compiler_params=pltpu.CompilerParams(vmem_limit_bytes=62 * 1024 * 1024),
         cost_estimate=pl.CostEstimate(

time: 178 us -> 176 us (0.989)
    pallas_call x1, Pallas kernels: 153 us -> 151 us  [run_train(): pl.pallas_call(functools.partial(train, n_rep, n_shard), out_shape=[jax.S...]
where the time goes in v11:
time: 176 us
  Pallas kernels  173 us (98%)
    pallas_call x1, Pallas kernels, run_train(): pl.pallas_call(functools.partial(train, n_rep, n_shard), out_shape=[jax.S...  151 us
    pallas_call x1, Pallas kernels, run_update(): pl.pallas_call(functools.partial(update, n_rep, n_shard), out_shape=[one,...  21.7 us

profile of v11, /device:TPU:0, one launch (start us, length us, event | category | flops | bytes accessed | tf_op | source)
XLA Modules:
  0.0 176.1 jit_solution(928662281408228974)
XLA Ops:
  1.3 0.9 slice.3
  2.2 0.7 pad.4.patch_ends
  2.9 151.3 %train_step.1 = (bf16[6,384,384]{2,1,0:T(8,128)(2,1)}, bf16[2,256,384]{2,1,0:T(8,128)(2,1)}, f32[256,384]{1,0:T(8,128)}, f32[8,128]{1,0:T(8,128)}, bf16[2,2,2,4,16,1792]{5,4,3,2,1,0:T(8,128)(2,1)}) custom-call(bf16[6,196,768]{2,1,0:T(8,128)(2,1)} %patches.1, bf16[6,16,768]{2,1,0:T(8,128)(2,1)} %pad.4.patch_ends, s32[6]{0:T(128)} %labels.1, ...), custom_call_target="tpu_custom_call" | custom-call | flops 24000000000 | bytes 30000000 | tf_op jit(solution)/shard_map/train_step/pallas_call | solution.py:1543
  154.2 21.7 %adamw.1 = (f32[1,1]{1,0:T(1,128)}, f32[1,1]{1,0:T(1,128)}, f32[192,384]{1,0:T(8,128)}, f32[192,384]{1,0:T(8,128)}, f32[192,384]{1,0:T(8,128)}, /*index=5*/f32[3...) custom-call(bf16[6,384,384]{2,1,0:T(8,128)(2,1)} %get-tuple-element., ...), custom_call_target="tpu_custom_call" | custom-call | flops 200000000 | bytes 50000000 | tf_op jit(solution)/shard_map/adamw/pallas_call | solution.py:1857

commit v12 on v11

--- a/solution.py
+++ b/solution.py
@@ -1653,16 +1653,15 @@
             found.append(pltpu.make_async_copy(src, dst, sem.at[index, slot]))
         return found
 
-    layered = [(1, layer) for layer in range(LAYERS)] + [(2, layer) for layer in range(LAYERS)]
-    order = [(4, None), (3, None), (5, None), (6, None)] + layered + [(0, None)]
+    order = [(array, layer) for layer in range(keep) for array in (1, 2)]
+    order += [(array, None) for array in (0, 4, 3, 5, 6)] + [(1, keep), (2, keep)]
     res_copy = pltpu.make_async_copy(res_there, res, grad_sems.at[0])
     small_copy = pltpu.make_async_copy(small_there, small, grad_sems.at[1])
+    res_copy.start()
     small_copy.start()
     for array, layer in order:
         for move in moves(array, layer):
             move.start()
-        if array == 6:
-            res_copy.start()
 
     n_rows = factors.shape[2] * factors.shape[3] * factors.shape[4]
     part_wide = factors.shape[5]
@@ -1677,60 +1676,25 @@
             at, size = at + wide, size - wide
         return found[0] if len(found) == 1 else jnp.concatenate(found, axis=1)
 
-    def squares(values):
-        return fold(values * values)
-
-    total = jnp.zeros((8, D), F32)
-    own_rows = pl.multiple_of(shard * rows_in, 8)
-
-    def keep_in(column, made):
-        slot = column % 2
-        passing[slot] = made
-        last_in[:, column * D : (column + 1) * D] = passing[slot, pl.ds(own_rows, rows_in), :]
-
-    h2 = factor(0, FF, D)
-    for tile in range(4):
-        made = mm_tn(h2, factor(1, tile * D, D))
-        keep_in(4 + tile, made)
-        total = total + squares(made)
-    small_copy.wait()
-    for tile in range(2):
-        last_in[:, (1 + tile) * D : (2 + tile) * D] = small[
-            0, tile * rows_in : (tile + 1) * rows_in, :
-        ].astype(F32)
-    made = mm_tn(factor(0, FF + 2 * D, D), factor(1, FF + D, D))
-    keep_in(0, made)
-    total = total + squares(made)
-    made = mm_tn(factor(0, FF + D, D), factor(1, FF, D))
-    keep_in(3, made)
-    total = total + squares(made)
-    d_top = factor(0, FF + 4 * D, D)
-    per = min(rows_down, D)
-    for tile in range(4):
-        made = mm_tn(factor(0, tile * D, D), d_top)
-        total = total + squares(made)
-        for piece in range(D // per):
-            owner, at = divmod(tile * D + piece * per, rows_down)
-
-            def keep_down(made=made, piece=piece, at=at):
-                last_down[at : at + per, :] = made[piece * per : (piece + 1) * per]
-
-            pl.when(shard == owner)(keep_down)
-    final = factor(0, FF + 3 * D, D)
-    wide = jnp.zeros((8, 128), F32)
-    for at in range(0, CPAD, 512):
-        d_logits = factor(1, FF + 2 * D + at, 512)
-        made = mm_tn(final, d_logits)
-        grad_head[0:D, at : at + 512] = made
-        bias = down_sum(d_logits.astype(F32))
-        grad_head[D : D + 1, at : at + 512] = bias
-        sums = squares(made)
-        for lane in range(0, 512, 128):
-            wide = wide + sums[:, lane : lane + 128]
-            row = bias[:, lane : lane + 128]
-            wide = wide + (row * row) * 0.125
-    for lane in range(0, D, 128):
-        wide = wide + total[:, lane : lane + 128]
+    def gram_squares(left, right):
+        total = jnp.zeros((8, 128), F32)
+        for row in range(0, n_rows, 128):
+            both = mm_nt(left[row : row + 128], left) * mm_nt(right[row : row + 128], right)
+            both = fold(both)
+            for lane in range(0, n_rows, 128):
+                total = total + both[:, lane : lane + 128]
+        return total
+
+    d_logits = factor(1, FF + 2 * D, CPAD)
+    head_bias = down_sum(d_logits.astype(F32))
+    wide = gram_squares(factor(0, 0, FF), factor(0, FF + 4 * D, D))
+    wide = wide + gram_squares(factor(0, FF, D), factor(1, 0, FF))
+    wide = wide + gram_squares(factor(0, FF + D, D), factor(1, FF, D))
+    wide = wide + gram_squares(factor(0, FF + 2 * D, D), factor(1, FF + D, D))
+    wide = wide + gram_squares(factor(0, FF + 3 * D, D), d_logits)
+    for lane in range(0, CPAD, 128):
+        row = head_bias[:, lane : lane + 128]
+        wide = wide + (row * row) * 0.125
     used = VEC_AT + 12 * LAYERS + 2
     parts = jnp.zeros((8, D), F32)
     kept_rows = lax.broadcasted_iota(jnp.int32, (8, 1), 0)
@@ -1774,6 +1738,55 @@
 
         lax.fori_loop(0, count, one, 0)
 
+    step = 32 if rows_in % 32 == 0 else 16
+
+    def update_in(layer):
+        begin(1, layer)
+
+        def column_of(column):
+            lanes = pl.ds(pl.multiple_of(column * D, 128), D)
+            for at in range(0, rows_in, step):
+                if layer < keep:
+                    k = 3 * (keep - 1 - layer) + jnp.where(column < 4, 2, 1)
+                    row = pl.multiple_of(lax.rem(column, 4) * rows_in + at, 16)
+                    grad = res[k, pl.ds(row, step), :].astype(F32)
+                else:
+                    grad = last_in[at : at + step, lanes]
+                apply(1, (layer, slice(at, at + step), lanes), grad, LEARNING_RATE)
+
+        loop(8, column_of)
+        finish(1, layer)
+
+    def update_down(layer):
+        begin(2, layer)
+
+        def rows_of(index):
+            for part in range(3):
+                at = pl.multiple_of(index * 96 + part * 32, 16)
+                if layer < keep:
+                    grad = res[3 * (keep - 1 - layer), pl.ds(at, 32), :].astype(F32)
+                else:
+                    grad = last_down[pl.ds(at, 32), :]
+                apply(2, (layer, pl.ds(at, 32), slice(0, D)), grad, LEARNING_RATE)
+
+        loop(rows_down // 96, rows_of)
+        finish(2, layer)
+
+    res_copy.wait()
+    for layer in range(keep):
+        update_in(layer)
+        update_down(layer)
+    small_copy.wait()
+    begin(0)
+
+    def patch_rows(index):
+        for part in range(3):
+            at = pl.multiple_of(index * 96 + part * 32, 16)
+            grad = small[1, pl.ds(at, 32), :].astype(F32)
+            apply(0, (pl.ds(at, 32), slice(0, D)), grad, LEARNING_RATE)
+
+    loop(PATCH_DIM // n_shard // 96, patch_rows)
+    finish(0)
     begin(4)
     rows = [patch_bias, class_row, vec[used - 2 : used - 1, 0:D], vec[used - 1 : used, 0:D]]
     for index, row in enumerate(rows):
@@ -1793,6 +1806,10 @@
             5, (slice(1 + at, 29 + at), slice(0, D)), vec[at : at + 28, 0:D], VECTOR_RATE
         )
     finish(5)
+    final = factor(0, FF + 3 * D, D)
+    for at in range(0, CPAD, 512):
+        grad_head[0:D, at : at + 512] = mm_tn(final, d_logits[:, at : at + 512])
+    grad_head[D : D + 1, :] = head_bias
     begin(6)
 
     def head_rows(index):
@@ -1803,48 +1820,38 @@
     loop(D // 48, head_rows)
     apply(6, (slice(D, D + 1), slice(0, NCLS)), grad_head[D : D + 1, 0:NCLS], LEARNING_RATE)
     finish(6)
-    res_copy.wait()
-    step = 32 if rows_in % 32 == 0 else 16
-    for layer in range(LAYERS):
-        begin(1, layer)
-
-        def column_of(column):
-            lanes = pl.ds(pl.multiple_of(column * D, 128), D)
-            for at in range(0, rows_in, step):
-                if layer < keep:
-                    k = 3 * (keep - 1 - layer) + jnp.where(column < 4, 2, 1)
-                    row = pl.multiple_of(lax.rem(column, 4) * rows_in + at, 16)
-                    grad = res[k, pl.ds(row, step), :].astype(F32)
-                else:
-                    grad = last_in[at : at + step, lanes]
-                apply(1, (layer, slice(at, at + step), lanes), grad, LEARNING_RATE)
-
-        loop(8, column_of)
-        finish(1, layer)
-    for layer in range(LAYERS):
-        begin(2, layer)
-
-        def rows_of(index):
-            for part in range(3):
-                at = pl.multiple_of(index * 96 + part * 32, 16)
-                if layer < keep:
-                    grad = res[3 * (keep - 1 - layer), pl.ds(at, 32), :].astype(F32)
-                else:
-                    grad = last_down[pl.ds(at, 32), :]
-                apply(2, (layer, pl.ds(at, 32), slice(0, D)), grad, LEARNING_RATE)
-
-        loop(rows_down // 96, rows_of)
-        finish(2, layer)
-    begin(0)
-
-    def patch_rows(index):
-        for part in range(3):
-            at = pl.multiple_of(index * 96 + part * 32, 16)
-            grad = small[1, pl.ds(at, 32), :].astype(F32)
-            apply(0, (pl.ds(at, 32), slice(0, D)), grad, LEARNING_RATE)
-
-    loop(PATCH_DIM // n_shard // 96, patch_rows)
-    finish(0)
+    own_rows = pl.multiple_of(shard * rows_in, 8)
+
+    def keep_in(column, made):
+        slot = column % 2
+        passing[slot] = made
+        last_in[:, column * D : (column + 1) * D] = passing[slot, pl.ds(own_rows, rows_in), :]
+
+    h2 = factor(0, FF, D)
+    for tile in range(4):
+        made = mm_tn(h2, factor(1, tile * D, D))
+        keep_in(4 + tile, made)
+    for tile in range(2):
+        last_in[:, (1 + tile) * D : (2 + tile) * D] = small[
+            0, tile * rows_in : (tile + 1) * rows_in, :
+        ].astype(F32)
+    made = mm_tn(factor(0, FF + 2 * D, D), factor(1, FF + D, D))
+    keep_in(0, made)
+    made = mm_tn(factor(0, FF + D, D), factor(1, FF, D))
+    keep_in(3, made)
+    d_top = factor(0, FF + 4 * D, D)
+    per = min(rows_down, D)
+    for tile in range(4):
+        made = mm_tn(factor(0, tile * D, D), d_top)
+        for piece in range(D // per):
+            owner, at = divmod(tile * D + piece * per, rows_down)
+
+            def keep_down(made=made, piece=piece, at=at):
+                last_down[at : at + per, :] = made[piece * per : (piece + 1) * per]
+
+            pl.when(shard == owner)(keep_down)
+    update_in(keep)
+    update_down(keep)
     for array, layer in order:
         for move in moves(array, layer, out=True):
             move.wait()

time: 176 us -> 177 us (level)
  no operation moved by 1% of the time
where the time goes in v12:
time: 177 us; the launch traced here: 176 us
  Pallas kernels  173 us (98%)
    pallas_call x1, Pallas kernels, run_train(): pl.pallas_call(functools.partial(train, n_rep, n_shard), out_shape=[jax.S...  151 us
    pallas_call x1, Pallas kernels, run_update(): pl.pallas_call(functools.partial(update, n_rep, n_shard), out_shape=[one,...  21.9 us

profile of v12, /device:TPU:0, one launch (start us, length us, event | category | flops | bytes accessed | tf_op | source)
XLA Modules:
  0.0 176.2 jit_solution(14712782997017566037)
XLA Ops:
  1.3 0.9 slice.3
  2.2 0.7 pad.4.patch_ends
  2.9 151.2 %train_step.1 = (bf16[6,384,384]{2,1,0:T(8,128)(2,1)}, bf16[2,256,384]{2,1,0:T(8,128)(2,1)}, f32[256,384]{1,0:T(8,128)}, f32[8,128]{1,0:T(8,128)}, bf16[2,2,2,4,16,1792]{5,4,3,2,1,0:T(8,128)(2,1)}) custom-call(bf16[6,196,768]{2,1,0:T(8,128)(2,1)} %patches.1, bf16[6,16,768]{2,1,0:T(8,128)(2,1)} %pad.4.patch_ends, s32[6]{0:T(128)} %labels.1, ...), custom_call_target="tpu_custom_call" | custom-call | flops 24000000000 | bytes 30000000 | tf_op jit(solution)/shard_map/train_step/pallas_call | solution.py:1543
  154.1 21.9 %adamw.1 = (f32[1,1]{1,0:T(1,128)}, f32[1,1]{1,0:T(1,128)}, f32[192,384]{1,0:T(8,128)}, f32[192,384]{1,0:T(8,128)}, f32[192,384]{1,0:T(8,128)}, /*index=5*/f32[3...) custom-call(bf16[6,384,384]{2,1,0:T(8,128)(2,1)} %get-tuple-element., ...), custom_call_target="tpu_custom_call" | custom-call | flops 200000000 | bytes 50000000 | tf_op jit(solution)/shard_map/adamw/pallas_call | solution.py:1864

commit v13 on v12

--- a/solution.py
+++ b/solution.py
@@ -191,15 +191,15 @@
 
 def train(
     n_rep, n_shard,
-    patches, patch_ends, labels, counts, own_patch, own_in, own_down, vecs, glob, pos, head,
+    patches, patch_ends, labels, counts, own_patch, own_in, own_down, vecs, glob, pos_there, head_there,
     res_out, small_out, vec_out, square_out, all_factors,
     X, N1, I1, QKV, ATT, N2, I2, ACT, SLOPE, DXB, DMB, DA, DH,
-    pix, lab, lab_given, wp, win, wdn, low_head, head_bias,
+    pos, head, pix, lab, lab_given, wp, win, wdn, low_head, head_bias,
     G, RC, RY, RX, RZ, RES, GS, SC, SY, SX, SZ, SRES,
     FAC, FC, FY, V, VC, VY, VX, VZ, VF, SQ, SQZ, SQP, square_sum,
     ag_send, ag_recv, ag_local, rs_send, rs_recv, f_send, f_recv, v_send, v_recv,
     q_send, q_recv,
-    img_send, img_recv, img_local, out_local,
+    img_send, img_recv, img_local, own_local, out_local,
 ):
     here = Place(n_rep, n_shard)
     n_x, n_y, n_z = here.n_x, here.n_y, here.n_z
@@ -254,7 +254,6 @@
     others += [here.to(z=turn(z, o, n_z)) for o in range(1, n_z)]
     for other in others:
         pl.semaphore_signal(barrier, inc=1, device_id=other, device_id_type=MESH)
-    pl.semaphore_wait(barrier, len(others))
 
     def weight(kind, layer, shard, part=None):
         if kind == "patch":
@@ -457,13 +456,20 @@
             found = jnp.where(row == CLS - TAIL + 16 * index, value, found)
         return found
 
-    for copy in local_half(0):
-        copy.start()
     for unit in range(2):
         for copy in weights_copies(unit):
             copy.start()
+    for copy in local_half(0):
+        copy.start()
+    pos_copy = pltpu.make_async_copy(pos_there, pos, own_local.at[0])
+    head_copy = pltpu.make_async_copy(head_there, head, own_local.at[1])
+    pos_copy.start()
+    head_copy.start()
     lab[0] = marks(0)
     lab_given[...] = marks(2)
+    weights_cast(0)
+    pl.semaphore_wait(barrier, len(others))
+    at_place("cast", 0)
 
     @pl.when(jnp.logical_not(lower))
     def _():
@@ -477,7 +483,7 @@
             copy.start()
         lab[1] = marks(1)
 
-    for unit in range(len(units)):
+    for unit in range(1, len(units)):
         weights_cast(unit)
         at_place("cast", unit)
 
@@ -489,6 +495,8 @@
     key_sub = lax.broadcasted_iota(jnp.int32, (BLK, 1), 0)
     key_column = jnp.where((key_sub < PATCHES) | (key_sub == CLS), 0.0, -1e30)
     whole_lanes = NCLS // 128 * 128
+    head_copy.wait()
+    pos_copy.wait()
     low_head[:, 0:whole_lanes] = head[0:D, 0:whole_lanes].astype(BF)
     low_head[:, whole_lanes:] = jnp.zeros((D, CPAD - whole_lanes), BF)
     low_head[:, whole_lanes:NCLS] = head[0:D, whole_lanes:NCLS].astype(BF)
@@ -1549,7 +1557,7 @@
             jax.ShapeDtypeStruct((8, 128), F32),
             jax.ShapeDtypeStruct((2, n_y, n_x, n_z, group, WFAC // n_y), BF),
         ],
-        in_specs=[there] * 2 + [pl.BlockSpec(memory_space=pltpu.SMEM)] * 2 + [there] * 3 + [whole] * 4,
+        in_specs=[there] * 2 + [pl.BlockSpec(memory_space=pltpu.SMEM)] * 2 + [there] * 3 + [whole] * 2 + [there] * 2,
         out_specs=[there] * 5,
         scratch_shapes=[
             buf(ROWS, D, dtype=F32),
@@ -1565,6 +1573,8 @@
             buf(ROWS, D),
             buf(ROWS, D),
             buf(ROWS, FF),
+            pltpu.VMEM(pos.shape, F32),
+            pltpu.VMEM(head.shape, F32),
             buf(KEPT, BLK, PATCH_DIM),
             buf(2, 32, 128, dtype=F32),
             buf(32, 128, dtype=F32),
@@ -1602,6 +1612,7 @@
             sems(3),
             sems(3),
             sems(4),
+            sems(2),
             sems(3 + chunks),
         ],
         compiler_params=pltpu.CompilerParams(
@@ -1893,7 +1904,7 @@
     m_patch, v_patch, m_in, v_in, m_down, v_down, m_vecs, v_vecs, m_glob, v_glob, m_pos, v_pos,
     m_head, v_head,
 ):
-    ends = jnp.pad(patches[:, TAIL:], ((0, 0), (0, BLK - PATCHES), (0, 0)))
+    ends = lax.pad(patches, BF(0), ((0, 0, 0), (-TAIL, BLK - PATCHES, 0), (0, 0, 0)))
     res, small, vec, squares, factors = run_train(
         n_rep, n_shard, patches, ends, labels, counts, patch_w, layer_in, layer_down, layer_vecs,
         glob_vecs, pos_embed, head,

time: 177 us -> 176 us (level)
  no operation moved by 1% of the time
where the time goes in v13:
time: 176 us; the launch traced here: 175 us
  Pallas kernels  172 us (98%)
    pallas_call x1, Pallas kernels, run_train(): pl.pallas_call(functools.partial(train, n_rep, n_shard), out_shape=[jax.S...  150 us
    pallas_call x1, Pallas kernels, run_update(): pl.pallas_call(functools.partial(update, n_rep, n_shard), out_shape=[one,...  21.9 us

profile of v13, /device:TPU:0, one launch (start us, length us, event | category | flops | bytes accessed | tf_op | source)
XLA Modules:
  0.0 175.2 jit_solution(4419708501536687645)
XLA Ops:
  1.3 1.6 pad_slice_fusion.patch_ends
  2.9 150.2 %train_step.1 = (bf16[6,384,384]{2,1,0:T(8,128)(2,1)}, bf16[2,256,384]{2,1,0:T(8,128)(2,1)}, f32[256,384]{1,0:T(8,128)}, f32[8,128]{1,0:T(8,128)}, bf16[2,2,2,4,16,1792]{5,4,3,2,1,0:T(8,128)(2,1)}) custom-call(bf16[6,196,768]{2,1,0:T(8,128)(2,1)} %patches.1, bf16[6,16,768]{2,1,0:T(8,128)(2,1)} %pad_slice_fusion.patch_ends, s32[6]{0:T(128)} %labels.1, ...), custom_call_target="tpu_custom_call" | custom-call | flops 24000000000 | bytes 30000000 | tf_op jit(solution)/shard_map/train_step/pallas_call | solution.py:1551
  153.1 21.9 %adamw.1 = (f32[1,1]{1,0:T(1,128)}, f32[1,1]{1,0:T(1,128)}, f32[192,384]{1,0:T(8,128)}, f32[192,384]{1,0:T(8,128)}, f32[192,384]{1,0:T(8,128)}, /*index=5*/f32[3...) custom-call(bf16[6,384,384]{2,1,0:T(8,128)(2,1)} %get-tuple-element., ...), custom_call_target="tpu_custom_call" | custom-call | flops 200000000 | bytes 50000000 | tf_op jit(solution)/shard_map/adamw/pallas_call | solution.py:1875

commit v14 on v13

--- a/solution.py
+++ b/solution.py
@@ -660,12 +660,10 @@
             first_norm(layer, half, (0, 1, 2))
             at_place("norm", half, layer)
 
-            def attend_one(index, nothing):
+            for index in range(2):
                 attend(layer, 2 * half + index)
+            for index in range(2):
                 at_place("att", half, layer, index)
-                return nothing
-
-            lax.fori_loop(0, 2, attend_one, 0)
             mlp(layer, half)
             return inner
 

time: 176 us -> 173 us (0.983)
  Pallas kernels: 172 us -> 170 us
    pallas_call x1, Pallas kernels: 150 us -> 148 us  [run_train(): pl.pallas_call(functools.partial(train, n_rep, n_shard), out_shape=[jax.S...]
where the time goes in v14:
time: 173 us
  Pallas kernels  170 us (98%)
    pallas_call x1, Pallas kernels, run_train(): pl.pallas_call(functools.partial(train, n_rep, n_shard), out_shape=[jax.S...  148 us
    pallas_call x1, Pallas kernels, run_update(): pl.pallas_call(functools.partial(update, n_rep, n_shard), out_shape=[one,...  21.9 us

profile of v14, /device:TPU:0, one launch (start us, length us, event | category | flops | bytes accessed | tf_op | source)
XLA Modules:
  0.0 172.8 jit_solution(6032634262332809970)
XLA Ops:
  1.3 1.6 pad_slice_fusion.patch_ends
  2.9 147.8 %train_step.1 = (bf16[6,384,384]{2,1,0:T(8,128)(2,1)}, bf16[2,256,384]{2,1,0:T(8,128)(2,1)}, f32[256,384]{1,0:T(8,128)}, f32[8,128]{1,0:T(8,128)}, bf16[2,2,2,4,16,1792]{5,4,3,2,1,0:T(8,128)(2,1)}) custom-call(bf16[6,196,768]{2,1,0:T(8,128)(2,1)} %patches.1, bf16[6,16,768]{2,1,0:T(8,128)(2,1)} %pad_slice_fusion.patch_ends, s32[6]{0:T(128)} %labels.1, ...), custom_call_target="tpu_custom_call" | custom-call | flops 24000000000 | bytes 30000000 | tf_op jit(solution)/shard_map/train_step/pallas_call | solution.py:1549
  150.7 21.9 %adamw.1 = (f32[1,1]{1,0:T(1,128)}, f32[1,1]{1,0:T(1,128)}, f32[192,384]{1,0:T(8,128)}, f32[192,384]{1,0:T(8,128)}, f32[192,384]{1,0:T(8,128)}, /*index=5*/f32[3...) custom-call(bf16[6,384,384]{2,1,0:T(8,128)(2,1)} %get-tuple-element., ...), custom_call_target="tpu_custom_call" | custom-call | flops 200000000 | bytes 50000000 | tf_op jit(solution)/shard_map/adamw/pallas_call | solution.py:1873
